TPU v7x, 32 devices: a whole 2x2x4 slice. The times are simulated.
32 devices in a mesh: seq: 8 (over z, y), batch: 4 (over x, core).
Axes of the slice: x: 2, y: 2, z: 4, core: 2. Of those that a mesh axis runs over, the one named last changes fastest.
Arguments:
- tokens: bfloat16 [4, 2048, 1024], P('batch', 'seq'), may hold values from -6 to 6
- w_query: float32 [1024, 1024], P('batch', 'seq'), may hold values from -0.1875 to 0.1875
- w_key: float32 [1024, 1024], P('batch', 'seq'), may hold values from -0.1875 to 0.1875
- w_value: float32 [1024, 1024], P('batch', 'seq'), may hold values from -0.1875 to 0.1875
- w_out: float32 [1024, 1024], P('batch', 'seq'), may hold values from -0.75 to 0.75
- w_ada: float32 [1024, 6144], P('batch', 'seq'), may hold values from -0.375 to 0.375
- w_up: float32 [1024, 2048], P('batch', 'seq'), may hold values from -0.1875 to 0.1875
- w_down: float32 [2048, 1024], P('batch', 'seq'), may hold values from -0.125 to 0.125
- segments: int32 [4, 2048], P('batch', 'seq'), may hold values from 0 to 15, as said below
- validity: int32 [4, 2048], P('batch', 'seq'), may hold values from 0 to 1, as said below
- timesteps: int32 [4, 16], P('batch'), may hold values from 0 to 999
- cotangent: bfloat16 [4, 2048, 1024], P('batch', 'seq'), may hold values from -6 to 6
Outputs:
- output: bfloat16 [4, 2048, 1024], P('batch', 'seq')
- grad_tokens: bfloat16 [4, 2048, 1024], P('batch', 'seq')
- grad_query: float32 [1024, 1024], P('batch', 'seq')
- grad_key: float32 [1024, 1024], P('batch', 'seq')
- grad_value: float32 [1024, 1024], P('batch', 'seq')
- grad_out: float32 [1024, 1024], P('batch', 'seq')
- grad_ada: float32 [1024, 6144], P('batch', 'seq')
- grad_up: float32 [1024, 2048], P('batch', 'seq')
- grad_down: float32 [2048, 1024], P('batch', 'seq')
Inputs may be any that keep to these rules, and one draw needn't show every extreme that they name: `segments`: in each replica one clip, drawn from the seed, holds the first rows of every device's 256 frames; the other clips' frames follow in order of clip id; every clip that has frames has frames with validity 1. `validity`: frames with 0 belong to the clip that spans every device.
All inputs are finite; a program needn't handle non-finite values.
Results may differ from a plain program's by a relative error of at most 0.018.
The roundings to bfloat16 on the way count: a program that leaves them out, or rounds other values in their place, can miss the bound.
Values may be sent and summed in bfloat16 or wider, within the bound.
No kernel may reach another device: no remote copies, remote signals or barrier semaphores. Data moves between devices by JAX's collectives and lax.ppermute only.
A program may use at most 320 MiB of HBM per device.

v0:
```python
from functools import partial
import math

import jax
import jax.numpy as jnp
from jax import lax
from jax.experimental import pallas as pl
from jax.experimental.pallas import tpu as pltpu
from jax.sharding import PartitionSpec as P

D = 1024
HEADS = 16
HEAD = 64
CLIPS = 16


def carried_in(part, axis, combine, identity):
    place = lax.axis_index(axis)
    gathered = lax.all_gather(part, axis)
    state = jnp.zeros_like(part) + jnp.asarray(identity, part.dtype)

    def one(step, state):
        return combine(state, lax.dynamic_index_in_dim(gathered, step, 0, False))

    return lax.fori_loop(0, place, one, state)


def matmul(left, right):
    return jnp.dot(left, right, preferred_element_type=jnp.float32)


def time_embedding(timestep_row):
    half_width = D // 2
    frequency = jnp.exp(-math.log(10000.0) * jnp.arange(half_width, dtype=jnp.float32) / half_width)
    angle = timestep_row.astype(jnp.float32)[:, None] * frequency[None, :]
    return jnp.concatenate([jnp.sin(angle), jnp.cos(angle)], axis=1)


def rotate_pairs(vectors, position, direction):
    half_size = vectors.shape[-1] // 2
    frequency = jnp.exp(-math.log(10000.0) * jnp.arange(half_size, dtype=jnp.float32) / half_size)
    angle = position[:, None] * frequency[None, :]
    cosine = jnp.cos(angle)[:, None, :]
    sine = jnp.sin(angle)[:, None, :] * direction
    first_half = vectors[..., :half_size]
    second_half = vectors[..., half_size:]
    return jnp.concatenate(
        [first_half * cosine - second_half * sine, second_half * cosine + first_half * sine],
        axis=-1,
    )


def normalize(inputs):
    centered = inputs - jnp.mean(inputs, axis=-1, keepdims=True)
    inverse = lax.rsqrt(jnp.mean(centered * centered, axis=-1, keepdims=True) + 1e-06)
    return (centered * inverse, inverse)


def norm_backward(grad_normed, normed, inverse):
    mean_grad = jnp.mean(grad_normed, axis=-1, keepdims=True)
    mean_mixed = jnp.mean(grad_normed * normed, axis=-1, keepdims=True)
    return inverse * (grad_normed - mean_grad - normed * mean_mixed)


def add_counts(earlier, later):
    return earlier + later


def block_rows_for(row_count):
    chosen = 1
    for candidate in range(1, 513):
        if row_count % candidate == 0:
            chosen = candidate
    return chosen


def stack_blocks(shard_piece):
    row_count = shard_piece[0].shape[0]
    block_rows = block_rows_for(row_count)
    block_count = row_count // block_rows
    return (
        shard_piece[0].reshape(block_count, block_rows, HEADS, HEAD),
        shard_piece[1].reshape(block_count, block_rows, HEADS, HEAD),
        shard_piece[2].reshape(block_count, block_rows),
    )


def forward_block(carried, key_block, queries, query_codes):
    running_max, running_sum, accumulated = carried
    key_rows, values, key_codes = key_block
    scores = (
        jnp.einsum("qhe,khe->hqk", queries, key_rows, preferred_element_type=jnp.float32) * 0.125
    )
    allowed = (query_codes[:, None] == key_codes.astype(jnp.float32)[None, :])[None]
    masked = jnp.where(allowed, scores, -1e30)
    new_max = jnp.maximum(running_max, jnp.max(masked, axis=2))
    rescale = jnp.exp(running_max - new_max)
    weights = jnp.where(allowed, jnp.exp(masked - new_max[:, :, None]), 0.0)
    running_sum = running_sum * rescale + jnp.sum(weights, axis=2)
    product = jnp.einsum(
        "hqk,khe->qhe", weights, values.astype(jnp.float32), precision=lax.Precision.HIGHEST
    )
    accumulated = accumulated * rescale.T[:, :, None] + product
    return (new_max, running_sum, accumulated)


def block_grads(key_block, queries, query_codes, grad_attn, log_total, delta_rows):
    key_rows, values, key_codes = key_block
    scores = (
        jnp.einsum("qhe,khe->hqk", queries, key_rows, preferred_element_type=jnp.float32) * 0.125
    )
    allowed = (query_codes[:, None] == key_codes.astype(jnp.float32)[None, :])[None]
    probabilities = jnp.exp(jnp.where(allowed, scores, -1e30) - log_total[:, :, None])
    grad_probs = jnp.einsum("qhe,khe->hqk", grad_attn, values, preferred_element_type=jnp.float32)
    grad_scores = (probabilities * (grad_probs - delta_rows[:, :, None])).astype(jnp.bfloat16)
    return (probabilities, grad_scores)


def body(
    tokens,
    w_query,
    w_key,
    w_value,
    w_out,
    w_ada,
    w_up,
    w_down,
    segments,
    validity,
    timesteps,
    cotangent,
):
    inputs = tokens[0].astype(jnp.float32)
    segment = segments[0]
    valid_row = validity[0]
    timestep_row = timesteps[0]
    grad_output = cotangent[0].astype(jnp.float32)
    frame_count = inputs.shape[0]
    highest = lax.Precision.HIGHEST
    cols_q, cols_k, cols_v, cols_o, cols_a, cols_u, cols_d = (
        lax.all_gather(w_query.astype(jnp.bfloat16), "seq", axis=1, tiled=True),
        lax.all_gather(w_key.astype(jnp.bfloat16), "seq", axis=1, tiled=True),
        lax.all_gather(w_value.astype(jnp.bfloat16), "seq", axis=1, tiled=True),
        lax.all_gather(w_out.astype(jnp.bfloat16), "seq", axis=1, tiled=True),
        lax.all_gather(w_ada.astype(jnp.bfloat16), "seq", axis=1, tiled=True),
        lax.all_gather(w_up.astype(jnp.bfloat16), "seq", axis=1, tiled=True),
        lax.all_gather(w_down.astype(jnp.bfloat16), "seq", axis=1, tiled=True),
    )
    full_q, full_k, full_v, full_o, full_a, full_u, full_d = (
        lax.all_gather(cols_q, "batch", axis=0, tiled=True),
        lax.all_gather(cols_k, "batch", axis=0, tiled=True),
        lax.all_gather(cols_v, "batch", axis=0, tiled=True),
        lax.all_gather(cols_o, "batch", axis=0, tiled=True),
        lax.all_gather(cols_a, "batch", axis=0, tiled=True),
        lax.all_gather(cols_u, "batch", axis=0, tiled=True),
        lax.all_gather(cols_d, "batch", axis=0, tiled=True),
    )
    silu_time = jax.nn.silu(time_embedding(timestep_row)).astype(jnp.bfloat16)
    emb_rows = matmul(silu_time, full_a)
    member = segment[:, None] == jnp.arange(CLIPS, dtype=jnp.int32)[None, :]
    one_hot = member.astype(jnp.float32)
    counted = member.astype(jnp.int32)
    modulation = jnp.dot(one_hot, emb_rows, precision=highest)
    shift_attn, scale_attn, gate_attn, shift_ffn, scale_ffn, gate_ffn = jnp.split(
        modulation, 6, axis=1
    )
    offsets = carried_in(
        jnp.sum(counted, axis=0), "seq", add_counts, jnp.zeros((CLIPS,), jnp.int32)
    )
    before = jnp.cumsum(counted, axis=0) - counted + offsets[None, :]
    position = jnp.sum(before * counted, axis=1).astype(jnp.float32)
    normed, inverse = normalize(inputs)
    attn_input = (normed * (1.0 + scale_attn) + shift_attn).astype(jnp.bfloat16)
    queries = rotate_pairs(
        matmul(attn_input, full_q).reshape(frame_count, HEADS, HEAD), position, 1.0
    ).astype(jnp.bfloat16)
    key_flat = (
        rotate_pairs(matmul(attn_input, full_k).reshape(frame_count, HEADS, HEAD), position, 1.0)
        .astype(jnp.bfloat16)
        .reshape(frame_count, D)
    )
    value_flat = matmul(attn_input, full_v).astype(jnp.bfloat16)
    key_codes = jnp.where(valid_row == 1, segment, -1).astype(jnp.bfloat16)
    query_codes = segment.astype(jnp.float32)
    start_state = (
        jnp.full((HEADS, frame_count), -1e30, jnp.float32),
        jnp.zeros((HEADS, frame_count), jnp.float32),
        jnp.zeros((frame_count, HEADS, HEAD), jnp.float32),
    )

    def step(state, key_block):
        return (forward_block(state, key_block, queries, query_codes), None)

    running_max, running_sum, accumulated = lax.scan(
        step,
        start_state,
        stack_blocks(
            (
                lax.all_gather(key_flat, "seq", axis=0, tiled=True),
                lax.all_gather(value_flat, "seq", axis=0, tiled=True),
                lax.all_gather(key_codes, "seq", axis=0, tiled=True),
            )
        ),
    )[0]
    attended = accumulated / running_sum.T[:, :, None]
    log_total = running_max + jnp.log(running_sum)
    attended_low = attended.reshape(frame_count, D).astype(jnp.bfloat16)
    attn_branch = matmul(attended_low, full_o)
    middle = inputs + gate_attn * attn_branch
    normed_mid, inverse_mid = normalize(middle)
    ffn_input = (normed_mid * (1.0 + scale_ffn) + shift_ffn).astype(jnp.bfloat16)
    hidden = matmul(ffn_input, full_u)
    activated, gelu_pull = jax.vjp(partial(jax.nn.gelu, approximate=True), hidden)
    activated_low = activated.astype(jnp.bfloat16)
    ffn_branch = matmul(activated_low, full_d)
    result = middle + gate_ffn * ffn_branch
    back_q, back_k, back_v, back_o, back_u, back_d = (
        full_q,
        full_k,
        full_v,
        full_o,
        full_u,
        full_d,
    )
    grad_gate_ffn = grad_output * ffn_branch
    g_ffn = (grad_output * gate_ffn).astype(jnp.bfloat16)
    grad_down_local = matmul(activated_low.T, g_ffn)
    grad_activated = matmul(g_ffn, back_d.T)
    g_hidden = gelu_pull(grad_activated)[0].astype(jnp.bfloat16)
    grad_up_local = matmul(ffn_input.T, g_hidden)
    grad_ffn_input = matmul(g_hidden, back_u.T)
    grad_middle = grad_output + norm_backward(
        grad_ffn_input * (1.0 + scale_ffn), normed_mid, inverse_mid
    )
    grad_scale_ffn = grad_ffn_input * normed_mid
    grad_gate_attn = grad_middle * attn_branch
    g_attn = (grad_middle * gate_attn).astype(jnp.bfloat16)
    grad_out_local = matmul(attended_low.T, g_attn)
    grad_attn = matmul(g_attn, back_o.T).astype(jnp.bfloat16).reshape(frame_count, HEADS, HEAD)
    delta_rows = jnp.einsum("qhe,qhe->hq", grad_attn.astype(jnp.float32), attended)
    zero_query = jnp.zeros((frame_count, HEADS, HEAD), jnp.float32)
    gathered = (
        lax.all_gather(key_flat, "seq", axis=0, tiled=True),
        lax.all_gather(value_flat, "seq", axis=0, tiled=True),
        lax.all_gather(key_codes, "seq", axis=0, tiled=True),
    )
    pack_rows = gathered[0].shape[0]
    grad_attn_wide = grad_attn.astype(jnp.float32)

    def joint_step(total_grad, key_block):
        probabilities, grad_scores = block_grads(
            key_block, queries, query_codes, grad_attn, log_total, delta_rows
        )
        total_grad = total_grad + 0.125 * jnp.einsum(
            "hqk,khe->qhe", grad_scores, key_block[0], preferred_element_type=jnp.float32
        )
        grad_keys = 0.125 * jnp.einsum(
            "hqk,qhe->khe", grad_scores, queries, preferred_element_type=jnp.float32
        )
        grad_values = jnp.einsum("hqk,qhe->khe", probabilities, grad_attn_wide, precision=highest)
        return (total_grad, (grad_keys, grad_values))

    grad_queries_rot, both_grads = lax.scan(joint_step, zero_query, stack_blocks(gathered))
    key_value_terms = jnp.concatenate(
        [both_grads[0].reshape(pack_rows, D), both_grads[1].reshape(pack_rows, D)], axis=1
    )
    key_value_grad = lax.psum_scatter(key_value_terms, "seq", scatter_dimension=0, tiled=True)
    g_query = (
        rotate_pairs(grad_queries_rot, position, -1.0).reshape(frame_count, D).astype(jnp.bfloat16)
    )
    g_key = (
        rotate_pairs(key_value_grad[:, :D].reshape(frame_count, HEADS, HEAD), position, -1.0)
        .reshape(frame_count, D)
        .astype(jnp.bfloat16)
    )
    g_value = key_value_grad[:, D:].astype(jnp.bfloat16)
    grad_query_local = matmul(attn_input.T, g_query)
    grad_key_local = matmul(attn_input.T, g_key)
    grad_value_local = matmul(attn_input.T, g_value)
    grad_attn_input = (
        matmul(g_query, back_q.T) + matmul(g_key, back_k.T) + matmul(g_value, back_v.T)
    )
    grad_inputs = grad_middle + norm_backward(grad_attn_input * (1.0 + scale_attn), normed, inverse)
    grad_modulation = jnp.concatenate(
        [
            grad_attn_input,
            grad_attn_input * normed,
            grad_gate_attn,
            grad_ffn_input,
            grad_scale_ffn,
            grad_gate_ffn,
        ],
        axis=1,
    )
    grad_emb = jnp.dot(one_hot.T, grad_modulation, precision=highest)
    grad_ada_local = jnp.dot(silu_time.astype(jnp.float32).T, grad_emb, precision=highest)
    part_q, part_k, part_v, part_o, part_a, part_u, part_d = (
        lax.psum_scatter(grad_query_local, "seq", scatter_dimension=1, tiled=True),
        lax.psum_scatter(grad_key_local, "seq", scatter_dimension=1, tiled=True),
        lax.psum_scatter(grad_value_local, "seq", scatter_dimension=1, tiled=True),
        lax.psum_scatter(grad_out_local, "seq", scatter_dimension=1, tiled=True),
        lax.psum_scatter(grad_ada_local, "seq", scatter_dimension=1, tiled=True),
        lax.psum_scatter(grad_up_local, "seq", scatter_dimension=1, tiled=True),
        lax.psum_scatter(grad_down_local, "seq", scatter_dimension=1, tiled=True),
    )
    final_q, final_k, final_v, final_o, final_a, final_u, final_d = (
        lax.psum_scatter(
            part_q.astype(jnp.bfloat16), "batch", scatter_dimension=0, tiled=True
        ).astype(jnp.float32),
        lax.psum_scatter(
            part_k.astype(jnp.bfloat16), "batch", scatter_dimension=0, tiled=True
        ).astype(jnp.float32),
        lax.psum_scatter(
            part_v.astype(jnp.bfloat16), "batch", scatter_dimension=0, tiled=True
        ).astype(jnp.float32),
        lax.psum_scatter(
            part_o.astype(jnp.bfloat16), "batch", scatter_dimension=0, tiled=True
        ).astype(jnp.float32),
        lax.psum_scatter(
            part_a.astype(jnp.bfloat16), "batch", scatter_dimension=0, tiled=True
        ).astype(jnp.float32),
        lax.psum_scatter(
            part_u.astype(jnp.bfloat16), "batch", scatter_dimension=0, tiled=True
        ).astype(jnp.float32),
        lax.psum_scatter(
            part_d.astype(jnp.bfloat16), "batch", scatter_dimension=0, tiled=True
        ).astype(jnp.float32),
    )
    return (
        result.astype(jnp.bfloat16)[None],
        grad_inputs.astype(jnp.bfloat16)[None],
        final_q,
        final_k,
        final_v,
        final_o,
        final_a,
        final_u,
        final_d,
    )


TWO = 2 * HEAD
ROWS = 256
BIG = 1e30
SEQ = 8
REPLICAS = 4
VMEM_MIB = 60
BLOCK = 256


def swap(part, axis, distance):
    size = SEQ if axis == "seq" else REPLICAS
    return lax.ppermute(part, axis, [(i, i ^ distance) for i in range(size)])


def exchange(blocks):
    return lax.all_to_all(blocks, "seq", 0, 0, tiled=True)


def turn(vectors, cosine, sine):
    lane = lax.broadcasted_iota(jnp.int32, vectors.shape, 1)
    first = (lane % HEAD) < HEAD // 2
    partner = jnp.where(
        first,
        pltpu.roll(vectors, TWO - HEAD // 2, 1),
        pltpu.roll(vectors, HEAD // 2, 1),
    )
    return vectors * cosine + partner * jnp.where(first, -sine, sine)


def of_head(vectors, head):
    lane = lax.broadcasted_iota(jnp.int32, vectors.shape, 1)
    return jnp.where(lane // HEAD == head, vectors, jnp.zeros_like(vectors))


def dot_t(left, right):
    return lax.dot_general(
        left, right, (((1,), (1,)), ((), ())), preferred_element_type=jnp.float32
    )


def project_kernel(place_ref, a_ref, b_ref, c_ref, d_ref, member_ref, bar_ref, cos_ref, sin_ref,
                   emb_ref, w_ref, *refs):
    x_ref, input_ref, q_ref, k_ref, kt_ref, v_ref, vt_ref, chunk_ref = refs[-8:]
    for step, ref in enumerate((a_ref, b_ref, c_ref, d_ref)):

        @pl.when(pl.program_id(0) == step)
        def _():
            chunk_ref[...] = ref[...]

    chunk = chunk_ref[...]
    x_ref[...] = chunk
    normed, _ = standardize(chunk.astype(jnp.float32))
    modulation = matmul(member_ref[...], emb_ref[...])
    low = (normed * (1.0 + modulation[:, D:]) + modulation[:, :D]).astype(jnp.bfloat16)
    input_ref[...] = low
    weight = jnp.concatenate([w_ref[b ^ place_ref[1]] for b in range(REPLICAS)], axis=0)
    product = matmul(low, weight)
    cosine, sine = cos_ref[...], sin_ref[...]
    keys = turn(product[:, TWO:2 * TWO], cosine, sine)
    values = product[:, 2 * TWO:]
    q_ref[...] = turn(product[:, :TWO], cosine, sine).astype(jnp.bfloat16)
    k_ref[:, :TWO] = keys.astype(jnp.bfloat16)
    k_ref[:, TWO:] = bar_ref[...]
    kt_ref[...] = keys.T.astype(jnp.bfloat16)
    v_ref[...] = values.astype(jnp.bfloat16)
    vt_ref[...] = values.T.astype(jnp.bfloat16)


def rows_spec(width):
    return pl.BlockSpec((ROWS, width), lambda i: (i, 0))


def cols_spec(height):
    return pl.BlockSpec((height, ROWS), lambda i: (0, i))


def whole_spec(height, width):
    return pl.BlockSpec((height, width), lambda i: (0, 0))


def params(mib):
    return pltpu.CompilerParams(
        dimension_semantics=("arbitrary",), vmem_limit_bytes=mib * 1024 * 1024
    )


def cost(micros):
    return pl.CostEstimate(
        flops=int(micros * 1e9), bytes_accessed=int(micros * 3e6), transcendentals=0
    )


def project(place, odd, chunks, member, bar, cosine, sine, emb, weights, earlier):
    frames = member.shape[0]
    low = jnp.bfloat16

    def rows(width):
        return pl.BlockSpec((ROWS, width), lambda i, p: ((2 * i + odd) ^ p[0], 0))

    def cols(height):
        return pl.BlockSpec((height, ROWS), lambda i, p: (0, (2 * i + odd) ^ p[0]))

    def whole(height, width):
        return pl.BlockSpec((height, width), lambda i, p: (0, 0))

    inputs = [place, *chunks, member, bar, cosine, sine, emb, weights, *earlier]
    first = len(inputs) - len(earlier)
    return pl.pallas_call(
        project_kernel,
        grid_spec=pltpu.PrefetchScalarGridSpec(
            num_scalar_prefetch=1,
            grid=(4,),
            in_specs=[whole(ROWS, D)] * 4 + [rows(TWO)] * 4
            + [whole(TWO, 2 * D),
               pl.BlockSpec((REPLICAS, ROWS, 3 * TWO), lambda i, p: (0, 0, 0))]
            + [pl.BlockSpec(memory_space=pl.ANY)] * len(earlier),
            out_specs=[rows(D), rows(D), rows(TWO), rows(2 * TWO), cols(TWO), rows(TWO),
                       cols(TWO)],
            scratch_shapes=[pltpu.VMEM((ROWS, D), low)],
        ),
        out_shape=[
            jax.ShapeDtypeStruct((frames, D), low),
            jax.ShapeDtypeStruct((frames, D), low),
            jax.ShapeDtypeStruct((frames, TWO), low),
            jax.ShapeDtypeStruct((frames, 2 * TWO), low),
            jax.ShapeDtypeStruct((TWO, frames), low),
            jax.ShapeDtypeStruct((frames, TWO), low),
            jax.ShapeDtypeStruct((TWO, frames), low),
        ],
        input_output_aliases={first + i: i for i in range(len(earlier))},
        compiler_params=params(30),
        cost_estimate=cost(2),
        name="project",
    )(*inputs)


def attend_kernel(q_ref, member_ref, k_ref, vt_ref, att_ref, low_ref, log_ref, *score_refs):
    frames = k_ref.shape[0]
    step = min(frames, 1024)
    queries = q_ref[...] * 0.125
    member = member_ref[...]
    bests, halves = [], []
    for head, score_ref in enumerate(score_refs):
        wide = jnp.concatenate([of_head(queries, head), member], axis=1)
        largest = jnp.full((1, BLOCK), -BIG, jnp.float32)
        for start in range(0, frames, step):
            scores = dot_t(k_ref[start:start + step, :], wide)
            score_ref[start:start + step, :] = scores
            largest = jnp.maximum(largest, jnp.max(scores, axis=0, keepdims=True))
        bests.append(largest)
    for head, score_ref in enumerate(score_refs):
        total = jnp.zeros((1, BLOCK), jnp.float32)
        out = jnp.zeros((TWO, BLOCK), jnp.float32)
        for start in range(0, frames, step):
            weights = jnp.exp(score_ref[start:start + step, :] - bests[head])
            total = total + jnp.sum(weights, axis=0, keepdims=True)
            out = out + matmul(vt_ref[:, start:start + step], weights.astype(jnp.bfloat16))
        halves.append(out[head * HEAD:(head + 1) * HEAD, :] / total)
        log_ref[head:head + 1, :] = bests[head] + jnp.log(total)
    attended = jnp.concatenate(halves, axis=0).T
    att_ref[...] = attended
    low_ref[...] = attended.astype(jnp.bfloat16)


def block_spec(width):
    return pl.BlockSpec((BLOCK, width), lambda i: (i, 0))


def attend(q, member, k, vt):
    frames = q.shape[0]
    return pl.pallas_call(
        attend_kernel,
        grid=(frames // BLOCK,),
        in_specs=[block_spec(TWO), block_spec(TWO), whole_spec(frames, 2 * TWO),
                  whole_spec(TWO, frames)],
        out_specs=[block_spec(TWO), block_spec(TWO), pl.BlockSpec((8, BLOCK), lambda i: (0, i))],
        out_shape=[
            jax.ShapeDtypeStruct((frames, TWO), jnp.float32),
            jax.ShapeDtypeStruct((frames, TWO), jnp.bfloat16),
            jax.ShapeDtypeStruct((8, frames), jnp.float32),
        ],
        scratch_shapes=[pltpu.VMEM((frames, BLOCK), jnp.float32)] * 2,
        compiler_params=params(26),
        cost_estimate=cost(18),
        name="attend",
    )(q, member, k, vt)


def attend_back_kernel(q_ref, member_ref, grad_ref, att_ref, log_ref, cos_ref, sin_ref, cos_all_ref,
                       sin_all_ref, k_ref, kt_ref, v_ref, g_ref, dk_ref, dv_ref):
    block = pl.program_id(0)
    frames = k_ref.shape[0]
    step = min(frames, 512)

    @pl.when(block == 0)
    def _():
        dk_ref[...] = jnp.zeros_like(dk_ref)
        dv_ref[...] = jnp.zeros_like(dv_ref)

    queries = q_ref[...] * 0.125
    member = member_ref[...]
    grad = grad_ref[...]
    mixed = (grad.astype(jnp.float32) * att_ref[...]).T
    halves = []
    wides, grads, deltas = [], [], []
    for head in range(2):
        wides.append(jnp.concatenate([of_head(queries, head), member], axis=1))
        grads.append(of_head(grad, head))
        deltas.append(jnp.sum(mixed[head * HEAD:(head + 1) * HEAD, :], axis=0, keepdims=True))
    totals = [jnp.zeros((TWO, ROWS), jnp.float32) for _ in range(2)]
    for start in range(0, frames, step):
        part = slice(start, start + step)
        dk = dk_ref[part, :]
        dv = dv_ref[part, :]
        for head in range(2):
            scores = dot_t(k_ref[part, :], wides[head])
            weights = jnp.exp(scores - log_ref[head:head + 1, :])
            grad_weights = dot_t(v_ref[part, :], grads[head])
            grad_scores = (weights * (grad_weights - deltas[head])).astype(jnp.bfloat16)
            dv = dv + matmul(weights.astype(jnp.bfloat16), grads[head])
            dk = dk + matmul(grad_scores, wides[head][:, :TWO])
            totals[head] = totals[head] + matmul(kt_ref[:, part], grad_scores)
        dk_ref[part, :] = dk
        dv_ref[part, :] = dv
    dq = jnp.concatenate([totals[0][:HEAD, :], totals[1][HEAD:, :]], axis=0).T * 0.125
    here = pl.ds(pl.multiple_of(block * ROWS, ROWS), ROWS)
    g_ref[here, :TWO] = turn(dq, cos_ref[...], -sin_ref[...]).astype(jnp.bfloat16)

    @pl.when(block == pl.num_programs(0) - 1)
    def _():
        turned = turn(dk_ref[...], cos_all_ref[...], -sin_all_ref[...])
        g_ref[:, TWO:2 * TWO] = turned.astype(jnp.bfloat16)
        g_ref[:, 2 * TWO:] = dv_ref[...].astype(jnp.bfloat16)


def attend_back(q, member, grad, att, log_total, cosine, sine, k, kt, v):
    frames = q.shape[0]
    return pl.pallas_call(
        attend_back_kernel,
        grid=(frames // ROWS,),
        in_specs=[rows_spec(TWO), rows_spec(TWO), rows_spec(TWO), rows_spec(TWO), cols_spec(8),
                  rows_spec(TWO), rows_spec(TWO), whole_spec(frames, TWO), whole_spec(frames, TWO),
                  whole_spec(frames, 2 * TWO), whole_spec(TWO, frames), whole_spec(frames, TWO)],
        out_specs=whole_spec(frames, 3 * TWO),
        out_shape=jax.ShapeDtypeStruct((frames, 3 * TWO), jnp.bfloat16),
        scratch_shapes=[pltpu.VMEM((frames, TWO), jnp.float32),
                        pltpu.VMEM((frames, TWO), jnp.float32)],
        compiler_params=params(VMEM_MIB),
        cost_estimate=cost(27),
        name="attend_back",
    )(q, member, grad, att, log_total, cosine, sine, cosine, sine, k, kt, v)


def three_terms(values):
    high = lax.reduce_precision(values, 8, 7)
    middle = lax.reduce_precision(values - high, 8, 7)
    return [high, middle, values - high - middle]


def standardize(rows):
    centered = rows - jnp.mean(rows, axis=1, keepdims=True)
    inverse = lax.rsqrt(jnp.mean(centered * centered, axis=1, keepdims=True) + 1e-06)
    return centered * inverse, inverse


def sum_of_clips(clip_ref, values):
    ids = lax.broadcasted_iota(jnp.int32, (CLIPS, clip_ref.shape[1]), 0)
    chosen = jnp.where(clip_ref[...] == ids, 1.0, 0.0).astype(jnp.bfloat16)
    high = values.astype(jnp.bfloat16)
    rest = values - high.astype(jnp.float32)
    middle = rest.astype(jnp.bfloat16)
    last = (rest - middle.astype(jnp.float32)).astype(jnp.bfloat16)
    return matmul(chosen, high) + matmul(chosen, middle) + matmul(chosen, last)


def beside(ref, tiles, rows):
    return jnp.concatenate([ref[tile, rows, :] for tile in tiles], axis=1)


def tile_index(away, apart):
    return 16 * (away % 2) + 8 * (away // 2) + 4 * (apart % 2) + apart // 2


def middle_kernel(mine_ref, x_ref, cot_ref, member_ref, clip_ref, emb_ref, *refs):
    *tile_refs, result_ref, grad_middle_ref, grad_att_ref, grad_emb_ref, left_ref, right_ref = refs[:-9]
    out_ref, up_ref, down_ref, sems, branch_ref, low_ref, act_ref, slope_ref, wide_ref = refs[-9:]
    low = jnp.bfloat16
    act_t_ref, ffn_t_ref = left_ref.at[:2 * D], left_ref.at[2 * D:3 * D]
    mine_t_ref = left_ref.at[3 * D:]
    g_ffn_ref, g_attn_ref = right_ref.at[:, :D], right_ref.at[:, 3 * D:]
    g_hidden_ref = right_ref.at[:, D:3 * D]
    pieces = ((out_ref, 0, 256), (up_ref, 256, 512), (down_ref, 768, 512))
    for i, (ref, start, size) in enumerate(pieces):
        first = 0
        for tile_ref in tile_refs:
            count = tile_ref.shape[0]
            pltpu.make_async_copy(
                tile_ref.at[:, pl.ds(start, size), :], ref.at[pl.ds(first, count)], sems.at[i]
            ).start()
            first += count
    copies = [
        pltpu.make_async_copy(ref, ref, sems.at[i]) for i, (ref, _, _) in enumerate(pieces)
    ]

    def tile(b, s):
        return SEQ * b + s

    member = member_ref[...]

    def modulation(index):
        return matmul(member, emb_ref[:, index * D:(index + 1) * D])

    def cols(n, width=256):
        return pl.ds(pl.multiple_of(n * width, width), width)

    every = slice(None)
    mine = jnp.concatenate([mine_ref[j] for j in range(SEQ)], axis=1)
    low_ref[...] = mine
    mine_t_ref[...] = mine.T
    gate_attn = modulation(2)
    copies[0].wait()

    @pl.loop(0, 4)
    def _(n):
        total = jnp.zeros((ROWS, 256), jnp.float32)
        for b in range(REPLICAS):
            weight = beside(out_ref, [tile(b, 2 * n), tile(b, 2 * n + 1)], every)
            total = total + matmul(low_ref[:, 256 * b:256 * b + 256], weight)
        branch_ref[:, cols(n)] = total

    branch = branch_ref[...]
    middle = x_ref[...].astype(jnp.float32) + gate_attn * branch
    normed, inverse = standardize(middle)
    scale_ffn = modulation(4)
    ffn_input = normed * (1.0 + scale_ffn) + modulation(3)
    low_ref[...] = ffn_input.astype(low)
    ffn_t_ref[...] = ffn_input.T.astype(low)
    gate_ffn = modulation(5)
    cot = cot_ref[...].astype(jnp.float32)
    g_ffn_ref[...] = (cot * gate_ffn).astype(low)
    copies[1].wait()

    @pl.loop(0, 8)
    def _(n):
        hidden = jnp.zeros((ROWS, 256), jnp.float32)
        for b in range(REPLICAS):
            index = tile(b, n)
            weight = jnp.concatenate([up_ref[index, :256, :], up_ref[index, 256:, :]], axis=1)
            hidden = hidden + matmul(low_ref[:, 256 * b:256 * b + 256], weight)
        root = math.sqrt(2.0 / math.pi)
        squared = hidden * hidden
        bent = jnp.tanh(root * (hidden + 0.044715 * (squared * hidden)))
        half = 0.5 * (1.0 + bent)
        activated = hidden * half
        slope = half + 0.5 * hidden * (1.0 - bent * bent) * (
            root * (1.0 + (3.0 * 0.044715) * squared)
        )
        act_ref[:, cols(n)] = activated.astype(low)
        act_t_ref[cols(n), :] = activated.T.astype(low)
        slope_ref[:, cols(n)] = slope

    copies[2].wait()

    @pl.loop(0, 4)
    def _(n):
        total = jnp.zeros((ROWS, 256), jnp.float32)
        for b in range(REPLICAS):
            weight = beside(down_ref, [tile(b, 2 * n), tile(b, 2 * n + 1)], every)
            total = total + matmul(act_ref[:, 512 * b:512 * b + 512], weight)
        wide_ref[:, cols(n)] = total

    ffn_branch = wide_ref[...]
    result_ref[...] = (middle + gate_ffn * ffn_branch).astype(low)
    grad_emb_ref[:, 3 * D:] = sum_of_clips(clip_ref, cot * ffn_branch)

    @pl.loop(0, REPLICAS)
    def _(b):
        weight = beside(down_ref, [tile(b, s) for s in range(SEQ)], every)
        grad = dot_t(g_ffn_ref[...], weight)
        here = cols(b, 512)
        g_hidden_ref[:, here] = (grad * slope_ref[:, here]).astype(low)

    @pl.loop(0, REPLICAS)
    def _(b):
        weight = jnp.concatenate(
            [up_ref[tile(b, s), 256 * k:256 * k + 256, :] for s in range(SEQ) for k in range(2)],
            axis=1,
        )
        wide_ref[:, cols(b)] = dot_t(g_hidden_ref[...], weight)

    grad_ffn_input = wide_ref[...]
    grad_emb_ref[:, D:2 * D] = sum_of_clips(clip_ref, grad_ffn_input)
    grad_emb_ref[:, 2 * D:3 * D] = sum_of_clips(clip_ref, grad_ffn_input * normed)
    spread = grad_ffn_input * (1.0 + scale_ffn)
    grad_middle = cot + inverse * (
        spread
        - jnp.mean(spread, axis=1, keepdims=True)
        - normed * jnp.mean(spread * normed, axis=1, keepdims=True)
    )
    grad_middle_ref[...] = grad_middle
    grad_emb_ref[:, :D] = sum_of_clips(clip_ref, grad_middle * branch)
    g_attn_ref[...] = (grad_middle * gate_attn).astype(low)

    @pl.loop(0, REPLICAS)
    def _(b):
        weight = beside(out_ref, [tile(b, s) for s in range(SEQ)], every)
        grad = dot_t(g_attn_ref[...], weight).astype(low)
        grad_att_ref[2 * b] = grad[:, :TWO]
        grad_att_ref[2 * b + 1] = grad[:, TWO:]


def middle_part(mine, x, cot, member, clip_row, emb, tiles):
    low = jnp.bfloat16
    shapes = [
        ((ROWS, D), low), ((ROWS, D), jnp.float32), ((SEQ, ROWS, TWO), low),
        ((CLIPS, 4 * D), jnp.float32),
        ((4 * D, ROWS), low), ((ROWS, 4 * D), low),
    ]
    vmem = pl.BlockSpec(memory_space=pltpu.VMEM)
    return pl.pallas_call(
        middle_kernel,
        in_specs=[vmem] * 6 + [pl.BlockSpec(memory_space=pl.ANY)] * len(tiles),
        out_specs=[vmem] * len(shapes),
        out_shape=[jax.ShapeDtypeStruct(shape, dtype) for shape, dtype in shapes],
        scratch_shapes=[
            pltpu.VMEM((32, 256, 128), low),
            pltpu.VMEM((32, 512, 128), low),
            pltpu.VMEM((32, 512, 128), low),
            pltpu.SemaphoreType.DMA((3,)),
            pltpu.VMEM((ROWS, D), jnp.float32),
            pltpu.VMEM((ROWS, D), low),
            pltpu.VMEM((ROWS, 2 * D), low),
            pltpu.VMEM((ROWS, 2 * D), jnp.float32),
            pltpu.VMEM((ROWS, D), jnp.float32),
        ],
        compiler_params=pltpu.CompilerParams(vmem_limit_bytes=VMEM_MIB * 1024 * 1024),
        cost_estimate=cost(20),
        name="middle",
    )(mine, x, cot, member, clip_row, emb, *tiles)


def weight_grads_kernel(place_ref, down_l, up_l, out_l, right_ref, down_o, up_o, out_o, other_ref,
                        away_d_ref, keep_d_ref, away_u_ref, keep_u_ref):
    low = jnp.bfloat16
    z, y = place_ref[2] // 2, place_ref[2] % 2
    lefts = [
        jnp.concatenate([mine[...], other[...]], axis=1)
        for mine, other in ((down_l, down_o), (up_l, up_o), (out_l, out_o))
    ]

    def product(left, first, block):
        here = pl.ds(pl.multiple_of(first + 256 * block, 256), 256)
        right = jnp.concatenate([right_ref[:, here], other_ref[:, here]], axis=0)
        return matmul(left, right).astype(low)

    def fill(ref):
        @pl.loop(0, 4)
        def _(k):
            block = z ^ k
            for left, first, rows in ((lefts[0], 0, slice(0, 512)), (lefts[2], 3 * D, slice(512, 768))):
                grad = product(left, first, block)
                ref[4 * y + k, rows, :] = grad[:, :128]
                ref[4 - 4 * y + k, rows, :] = grad[:, 128:]
            for side, up_ref in enumerate((keep_u_ref, away_u_ref)):
                grad = product(lefts[1], D, 2 * block + (y ^ side))
                up_ref[0, k, :256, :] = grad[:, :128]
                up_ref[0, k, 256:, :] = grad[:, 128:]

    @pl.when(pl.program_id(0) == 0)
    def _():
        fill(away_d_ref)

    @pl.when(pl.program_id(0) == 1)
    def _():
        fill(keep_d_ref)


def weight_grads(place, left, right, other_left, other_right):
    low = jnp.bfloat16

    def target(i, p):
        return 2 * jnp.where(i == 0, 1 - p[0], p[0]) + p[1]

    down = pl.BlockSpec((512, ROWS), lambda i, p: (target(i, p), 0))
    up = pl.BlockSpec((256, ROWS), lambda i, p: (8 + target(i, p), 0))
    out = pl.BlockSpec((256, ROWS), lambda i, p: (12 + target(i, p), 0))
    wide = pl.BlockSpec((ROWS, 4 * D), lambda i, p: (0, 0))
    whole = pl.BlockSpec((SEQ, 768, 128), lambda i, p: (0, 0, 0))
    part = pl.BlockSpec((1, 4, 512, 128), lambda i, p: (1 - i, 0, 0, 0))
    return pl.pallas_call(
        weight_grads_kernel,
        grid_spec=pltpu.PrefetchScalarGridSpec(
            num_scalar_prefetch=1,
            grid=(2,),
            in_specs=[down, up, out, wide] * 2,
            out_specs=[whole, whole, part, part],
        ),
        out_shape=[jax.ShapeDtypeStruct((SEQ, 768, 128), low)] * 2
        + [jax.ShapeDtypeStruct((2, 4, 512, 128), low)] * 2,
        compiler_params=params(VMEM_MIB),
        cost_estimate=cost(9),
        name="weight_grads",
    )(place, left, left, left, right, other_left, other_left, other_left, other_right)


def clip_grads_kernel(place_ref, x_ref, clip_ref, g_ref, w_ref, out_ref):
    @pl.when(pl.program_id(0) == 0)
    def _():
        out_ref[...] = jnp.zeros_like(out_ref)

    normed, _ = standardize(x_ref[...].astype(jnp.float32))
    grad = jnp.concatenate(
        [dot_t(g_ref[...], w_ref[b ^ place_ref[1]]) for b in range(REPLICAS)], axis=1
    )
    out_ref[:, :D] += sum_of_clips(clip_ref, grad)
    out_ref[:, D:] += sum_of_clips(clip_ref, grad * normed)


def clip_grads(places, x, clip_row, g_heads, heads_w):
    frames = x.shape[0]
    return pl.pallas_call(
        clip_grads_kernel,
        grid=(frames // ROWS,),
        in_specs=[pl.BlockSpec(memory_space=pltpu.SMEM), rows_spec(D), cols_spec(1),
                  rows_spec(3 * TWO),
                  pl.BlockSpec((REPLICAS, ROWS, 3 * TWO), lambda i: (0, 0, 0))],
        out_specs=whole_spec(CLIPS, 2 * D),
        out_shape=jax.ShapeDtypeStruct((CLIPS, 2 * D), jnp.float32),
        compiler_params=params(VMEM_MIB),
        cost_estimate=cost(9),
        name="clip_grads",
    )(places, x, clip_row, g_heads, heads_w)


def last_kernel(place_ref, own_ref, x_ref, grad_middle_ref, member_ref, emb_ref, *refs):
    *tile_refs, out_ref, wide_ref = refs
    grads = jnp.concatenate([own_ref[place_ref[2] ^ s] for s in range(SEQ)], axis=1)

    def tile(away, apart):
        index = tile_index(away, apart)
        for ref in tile_refs:
            if index < ref.shape[0]:
                return ref[index, ref.shape[1] - 768:, :]
            index -= ref.shape[0]

    for away in range(REPLICAS):
        weight = jnp.concatenate(
            [
                tile(away, s)[256 * k:256 * k + 256, :]
                for s in range(SEQ)
                for k in range(3)
            ],
            axis=1,
        )
        b = (2 * place_ref[0] + place_ref[1]) ^ away
        wide_ref[:, pl.ds(pl.multiple_of(b * 256, 256), 256)] = dot_t(grads, weight)

    normed, inverse = standardize(x_ref[...].astype(jnp.float32))
    spread = wide_ref[...] * (1.0 + matmul(member_ref[...], emb_ref[:, D:2 * D]))
    grad = grad_middle_ref[...] + inverse * (
        spread
        - jnp.mean(spread, axis=1, keepdims=True)
        - normed * jnp.mean(spread * normed, axis=1, keepdims=True)
    )
    out_ref[...] = grad.astype(jnp.bfloat16)


def last_part(place, own, x, grad_middle, member, emb, tiles):
    vmem = pl.BlockSpec(memory_space=pltpu.VMEM)
    return pl.pallas_call(
        last_kernel,
        in_specs=[pl.BlockSpec(memory_space=pltpu.SMEM)] + [vmem] * (5 + len(tiles)),
        out_specs=vmem,
        out_shape=jax.ShapeDtypeStruct((ROWS, D), jnp.bfloat16),
        scratch_shapes=[pltpu.VMEM((ROWS, D), jnp.float32)],
        compiler_params=pltpu.CompilerParams(vmem_limit_bytes=30 * 1024 * 1024),
        cost_estimate=cost(4),
        name="last",
    )(place, own, x, grad_middle, member, emb, *tiles)


def after(value, *others):
    return lax.optimization_barrier((value,) + others)[0]


def together(*values):
    return lax.optimization_barrier(values)


def plus(*terms):
    total = terms[0].astype(jnp.float32)
    for term in terms[1:]:
        total = total + term.astype(jnp.float32)
    return total


def clip_lanes(clip, terms):
    lane = jnp.arange(TWO, dtype=jnp.int32)[None, :]
    return (clip[:, None] == lane % CLIPS) & (lane < terms * CLIPS)


def body_fast(
    tokens, w_query, w_key, w_value, w_out, w_ada, w_up, w_down,
    segments, validity, timesteps, cotangent,
):
    highest = lax.Precision.HIGHEST
    low = jnp.bfloat16
    wide = jnp.float32
    replica = lax.axis_index("batch")
    x = tokens[0]
    frame_count = x.shape[0]
    frames = frame_count * SEQ
    segment = segments[0]

    seat = lax.axis_index("seq").astype(jnp.int32)
    z, y = seat // 2, seat % 2
    place = jnp.stack([replica // 2, replica % 2, seat]).astype(jnp.int32)
    mine_w = jnp.concatenate([w_out, w_up[:, :128], w_up[:, 128:], w_down], axis=0).astype(low)

    z1, z2, y0 = swap(x, "seq", 2), swap(x, "seq", 4), swap(x, "seq", 1)
    times = lax.all_gather(timesteps[0], "batch", axis=0, tiled=True)
    silu_all = jax.nn.silu(time_embedding(times)).astype(low)
    depth = w_ada.shape[0]
    silu_part = lax.dynamic_slice_in_dim(silu_all, replica * depth, depth, 1)
    emb_part = matmul(silu_part, w_ada.astype(low)).reshape(REPLICAS, CLIPS, -1)
    emb_cols = lax.all_to_all(emb_part, "batch", 0, 0, tiled=True)
    emb_cols = jnp.sum(emb_cols, axis=0)
    own_codes = (segment * 2 + (validity[0] == 1)).astype(wide)
    cols = emb_cols.shape[1]
    own_codes = jnp.pad(own_codes, (0, 8 * cols - frame_count)).reshape(8, cols)
    packed = jnp.concatenate([emb_cols, own_codes])
    packed = jnp.broadcast_to(packed[None], (SEQ,) + packed.shape)
    heads_w = jnp.concatenate([w_query, w_key, w_value], axis=1).astype(low)
    heads_w = jnp.stack([heads_w, swap(heads_w, "batch", 1)])
    z1, z2, y0, packed, heads_w, mine_w = together(z1, z2, y0, packed, heads_w, mine_w)
    tiles_w = (lax.all_gather(mine_w, ("batch", "seq"), axis=0),)
    packed = exchange(packed)
    z3 = swap(z2, "seq", 2)
    y1, y2 = swap(z1, "seq", 1), swap(z2, "seq", 1)
    heads_x = swap(heads_w, "batch", 2)
    z3, heads_x = together(z3, heads_x)
    y3 = swap(z3, "seq", 1)
    mine_h = jnp.concatenate([w_query, w_key, w_value], axis=0).astype(low)
    mine_h = after(mine_h, z3)
    h_z1, h_z2 = swap(mine_h, "seq", 2), swap(mine_h, "seq", 4)
    heads_w = jnp.concatenate([heads_w, heads_x])
    emb = packed[:, :CLIPS]
    codes = packed[:, CLIPS:].reshape(SEQ, -1)[:, :frame_count].reshape(frames).astype(jnp.int32)
    clip = codes // 2
    clip_row = clip[None, :]
    tri = jnp.arange(frame_count)[:, None] > jnp.arange(frame_count)[None, :]
    ids = jnp.arange(CLIPS, dtype=jnp.int32)
    one_hot = (clip.reshape(SEQ, frame_count)[:, :, None] == ids).astype(low)
    within = jnp.einsum("ij,njc->nic", tri.astype(low), one_hot, preferred_element_type=wide)
    counts = jnp.sum(one_hot.astype(wide), axis=1)
    offsets = jnp.cumsum(counts, axis=0) - counts
    position = jnp.sum(one_hot.astype(wide) * (within + offsets[:, None, :]), axis=2)
    half = HEAD // 2
    frequency = jnp.exp(-math.log(10000.0) * jnp.arange(half, dtype=wide) / half)
    angle = position.reshape(frames)[:, None] * jnp.tile(frequency, 4)[None, :]
    cosine, sine = jnp.cos(angle), jnp.sin(angle)
    member = clip_lanes(clip, 3).astype(low)
    allowed = clip_lanes(jnp.where(codes % 2 == 1, clip, -1), 1)
    inside = jnp.arange(TWO, dtype=jnp.int32)[None, :] < CLIPS
    bar = jnp.where(inside & ~allowed, -BIG, 0.0).astype(low)
    emb, y1, y2 = together(after(emb, heads_w, member, cosine), y1, y2)
    emb = emb.transpose(1, 0, 2).reshape(CLIPS, -1)
    emb = jnp.concatenate(
        [t.astype(low) for t in three_terms(emb)] + [jnp.zeros((TWO - 3 * CLIPS, 6 * D), low)],
        axis=0,
    )

    tables = (member, bar, cosine, sine, emb, heads_w)
    places = jnp.stack([seat, replica.astype(jnp.int32)])
    earlier = project(places, 0, (x, z1, z2, z3), *tables, ())
    y3, h_z1, h_z2, earlier = together(y3, h_z1, h_z2, earlier)
    h_z3 = swap(h_z2, "seq", 2)
    x_all, attn_input, q, k, kt, v, vt = project(places, 1, (y0, y1, y2, y3), *tables, earlier)
    attended, attended_low, log_total = attend(q, member, k, vt)
    attended_low, h_z3 = together(attended_low, h_z3)
    mine = exchange(attended_low.reshape(SEQ, frame_count, TWO))
    h_z = jnp.stack([mine_h, h_z1, h_z2, h_z3])
    mine, h_z = together(mine, h_z)
    h_y, h_x = swap(h_z, "seq", 1), swap(h_z, "batch", 2)

    own_member = clip_lanes(segment, 3).astype(low)
    result, grad_middle, grad_att, grad_emb, left, right = middle_part(
        mine, x, cotangent[0], own_member, segment[None, :], emb, tiles_w
    )
    left, h_y, h_x = together(left, h_y, h_x)
    other_left, other_right = swap(left, "batch", 1), swap(right, "batch", 1)
    h_first = jnp.concatenate([h_z, h_y, h_x])
    other_left, other_right, h_first = together(other_left, other_right, h_first)
    away_d, keep_d, away_u, keep_u = weight_grads(place, left, right, other_left, other_right)
    grad_heads = exchange(grad_att).reshape(frames, TWO)
    grad_heads, away_d, away_u = together(grad_heads, away_d, away_u)
    from_x = swap(away_d, "batch", 2)
    from_y = swap(away_u, "seq", 1)

    g_heads = attend_back(
        q, member, grad_heads, attended, log_total, cosine, sine, k, kt, v
    )
    own = exchange(g_heads.reshape(SEQ, frame_count, 3 * TWO))
    from_y = after(from_y, g_heads)
    to_x_u = plus(keep_u[1], from_y[1]).astype(low)
    from_x_u = swap(to_x_u, "batch", 2)
    from_x = after(from_x, to_x_u)
    to_y_d = plus(keep_d[4:], from_x[4:]).astype(low)
    from_y_d = swap(to_y_d, "seq", 1)
    h_yx = swap(after(h_y, to_y_d), "batch", 2)
    h_first_core = swap(after(h_first, to_x_u), "batch", 1)
    g_heads = after(g_heads, to_y_d, to_x_u)
    late = clip_grads(places, x_all, clip_row, g_heads, heads_w)
    grad_heads_w = matmul(attn_input.T, g_heads).astype(low).reshape(2, 2, ROWS, 3 * TWO)
    late, grad_heads_w, from_y_d, from_x_u, h_first_core = together(
        late, grad_heads_w, from_y_d, from_x_u, h_first_core
    )
    part = jnp.concatenate(
        [
            plus(keep_u[0], from_y[0], from_x_u).astype(low),
            plus(keep_d[:4], from_x[:4], from_y_d).astype(low),
        ],
        axis=1,
    )
    late, own = together(late, own)
    grad_emb = jnp.concatenate([late, grad_emb], axis=1)
    grad_emb = grad_emb.reshape(CLIPS, 4, 2, -1).transpose(2, 1, 0, 3)
    keep_e = lax.dynamic_index_in_dim(grad_emb, y, 0, False)
    other_e = swap(lax.dynamic_index_in_dim(grad_emb, 1 - y, 0, False), "seq", 1)
    x_place, core_place = replica // 2, replica % 2
    grad_emb = keep_e + other_e
    from_z_e = [
        swap(lax.dynamic_index_in_dim(grad_emb, z ^ k, 0, False), "seq", 2 * k) for k in range(1, 4)
    ]
    grad_emb = plus(lax.dynamic_index_in_dim(grad_emb, z, 0, False), *from_z_e)
    keep_h = lax.dynamic_index_in_dim(grad_heads_w, core_place, 1, False)
    other_h = swap(lax.dynamic_index_in_dim(grad_heads_w, 1 - core_place, 1, False), "batch", 1)
    h_yx_core = swap(after(h_yx, part), "batch", 1)
    from_z = [swap(part[k], "seq", 2 * k) for k in range(1, 4)]
    both_h = plus(keep_h, other_h).astype(low)
    away_h = swap(lax.dynamic_index_in_dim(both_h, 1 - x_place, 0, False), "batch", 2)

    grad_tokens = last_part(place, own, x, grad_middle, own_member, emb,
        (h_first, h_yx, h_first_core, h_yx_core),
    )
    grad_emb = lax.all_gather(grad_emb, "batch", axis=0, tiled=True)
    final_a = jnp.dot(silu_part.astype(wide).T, grad_emb, precision=highest)
    grad_tokens, final_a, away_h, *from_z = together(grad_tokens, final_a, away_h, *from_z)
    final_heads = plus(lax.dynamic_index_in_dim(both_h, x_place, 0, False), away_h)
    total = plus(part[0], *from_z)
    final_u = jnp.concatenate([total[:256], total[256:512]], axis=1)
    final_d, final_o = total[512:1024], total[1024:]
    width = w_query.shape[1]
    return (
        result[None],
        grad_tokens[None],
        final_heads[:, :width],
        final_heads[:, width:2 * width],
        final_heads[:, 2 * width:],
        final_o,
        final_a,
        final_u,
        final_d,
    )


def solution(mesh):
    fits = mesh.shape["seq"] == SEQ and mesh.shape["batch"] == REPLICAS
    chosen = body_fast if fits else body
    return jax.shard_map(
        chosen,
        mesh=mesh,
        in_specs=(
            P("batch", "seq", None),
            P("batch", "seq"),
            P("batch", "seq"),
            P("batch", "seq"),
            P("batch", "seq"),
            P("batch", "seq"),
            P("batch", "seq"),
            P("batch", "seq"),
            P("batch", "seq"),
            P("batch", "seq"),
            P("batch", None),
            P("batch", "seq", None),
        ),
        out_specs=(
            P("batch", "seq", None),
            P("batch", "seq", None),
            P("batch", "seq"),
            P("batch", "seq"),
            P("batch", "seq"),
            P("batch", "seq"),
            P("batch", "seq"),
            P("batch", "seq"),
            P("batch", "seq"),
        ),
        check_vma=False,
    )
```

profile of v0, /device:TPU:13, one launch (start us, length us, event | category | flops | bytes accessed | tf_op | source)
XLA Modules:
  0.0 316.5 jit_solution(9293224713805110329)
XLA Ops:
  12.6 5.4 %all-reduce.1 = s32[64]{0:T(128)S(1)} all-reduce(s32[64]{0:T(128)S(1)} %bitcast_dynamic-update-slice_fusion), channel_id=2, replica_groups=mesh['seq'=8,'batch'=4] {'batch'}, use_global_device_ids=true, to_apply=%add.1 | all-reduce | flops 64 | bytes 512
  20.7 4.5 %all-to-all-start = ((f32[4,16,768]{2,1,0:T(8,128)}), f32[4,16,768]{2,1,0:T(8,128)S(1)}, u32[]{:S(2)}, u32[]{:S(2)}) async-start(f32[4,16,768]{2,1,0:T(8,128)} %bitcast.5), calls=%async_computation | async-start | bytes 393216 | tf_op jit(solution)/shard_map/all_to_all | solution.py:967
  26.5 3.2 %all-to-all-done = f32[4,16,768]{2,1,0:T(8,128)S(1)} async-done(((f32[4,16,768]{2,1,0:T(8,128)}), f32[4,16,768]{2,1,0:T(8,128)S(1)}, u32[]{:S(2)}, u32[]{:S(2)}) %all-to-all-start) | async-done | bytes 196640 | tf_op jit(solution)/shard_map/all_to_all | solution.py:967
  33.5 4.4 %all-to-all-start.1 = ((f32[8,24,768]{2,1,0:T(8,128)}), f32[8,24,768]{2,1,0:T(8,128)}, u32[]{:S(2)}, u32[]{:S(2)}) async-start(f32[8,24,768]{2,1,0:T(8,128)} %broadcast_in_dim.16), calls=%async_computation.1 | async-start | bytes 1179648 | tf_op jit(solution)/shard_map/all_to_all | solution.py:357
  45.5 18.3 %collective-permute-done.4.d_ref = bf16[256,1024]{1,0:T(8,128)(2,1)} collective-permute-done((bf16[256,1024]{1,0:T(8,128)(2,1)S(1)}, bf16[256,1024]{1,0:T(8,128)(2,1)}, u32[]{:S(2)}, u32[]{:S(2)}) %collective-permute-start.4) | collective-permute-done | bytes 524320 | tf_op jit(solution)/shard_map/ppermute | solution.py:353
  72.4 3.7 %multiply_sine_fusion = (f32[2048,128]{1,0:T(8,128)S(1)}, f32[2048,128]{1,0:T(8,128)S(1)}) fusion(f32[128]{0:T(128)S(1)} %mul.62, f32[2048]{0:T(1024)S(1)} %bitcast.131), kind=kLoop, calls=%fused_computation.13 | loop fusion | flops 262144 | bytes 2105856 | tf_op jit(solution)/shard_map/sin | solution.py:1002
  78.8 6.3 %project.2 = (bf16[2048,1024]{1,0:T(8,128)(2,1)S(1)}, bf16[2048,1024]{1,0:T(8,128)(2,1)S(1)}, bf16[2048,128]{1,0:T(8,128)(2,1)S(1)}, bf16[2048,256]{1,0:T(8,128)...) custom-call(s32[2]{0:T(128)S(1)} %pad_add_fusion.place_ref, ...), custom_call_target="tpu_custom_call" | custom-call | flops 2000000000 | bytes 6000000 | tf_op jit(solution)/shard_map/project/pallas_call | solution.py:449
  87.3 6.3 %project.3 = (bf16[2048,1024]{1,0:T(8,128)(2,1)S(1)}, bf16[2048,1024]{1,0:T(8,128)(2,1)S(1)}, bf16[2048,128]{1,0:T(8,128)(2,1)S(1)}, bf16[2048,256]{1,0:T(8,128)...) custom-call(s32[2]{0:T(128)S(1)} %pad_add_fusion.place_ref, ...), custom_call_target="tpu_custom_call", output_to_operand_aliasing={{0}: (11, {}), {1}: (12, {}), {2}: (13, {}), {3}: (14, {}),... | custom-call | flops 2000000000 | bytes 6000000 | tf_op jit(solution)/shard_map/project/pallas_call | solution.py:449
  93.7 16.1 %attend.1 = (f32[2048,128]{1,0:T(8,128)S(1)}, bf16[2048,128]{1,0:T(8,128)(2,1)}, f32[8,2048]{1,0:T(8,128)S(1)}) custom-call(bf16[2048,128]{1,0:T(8,128)(2,1)S(1)} %get-tuple-element.118.q_ref, bf16[2048,128]{1,0:T(8,128)(2,1)S(1)} %and_convert_fusion.member_ref, bf16[2048,256]{1,0:T(8,128)(2,1)S(1)} %get-tuple-element.119.k_ref, ...), custom_call_target="tpu_custom_call" | custom-call | flops 17999998976 | bytes 54000000 | tf_op jit(solution)/shard_map/attend/pallas_call | solution.py:512
  112.1 5.2 %all-to-all-start.2 = ((bf16[8,256,128]{2,1,0:T(8,128)(2,1)}), bf16[8,256,128]{2,1,0:T(8,128)(2,1)S(1)}, u32[]{:S(2)}, u32[]{:S(2)}) async-start(bf16[8,256,128]{2,1,0:T(8,128)(2,1)} %bitcast.15), calls=%async_computation.2 | async-start | bytes 1048576 | tf_op jit(solution)/shard_map/all_to_all | solution.py:357
  119.3 18.5 %all-to-all-done.2.mine_ref = bf16[8,256,128]{2,1,0:T(8,128)(2,1)S(1)} async-done(((bf16[8,256,128]{2,1,0:T(8,128)(2,1)}), bf16[8,256,128]{2,1,0:T(8,128)(2,1)S(1)}, u32[]{:S(2)}, u32[]{:S(2)}) %all-to-all-start.2) | async-done | bytes 524320 | tf_op jit(solution)/shard_map/all_to_all | solution.py:357
  139.1 20.8 %middle.1 = (bf16[256,1024]{1,0:T(8,128)(2,1)}, f32[256,1024]{1,0:T(8,128)}, bf16[8,256,128]{2,1,0:T(8,128)(2,1)}, f32[16,4096]{1,0:T(8,128)}, bf16[4096,256]{1,0:T(8,128)(2,1)}, /*index=5*/bf16[256,4096]{1,0:T(8,128)(2,1)}) custom-call(bf16[8,256,128]{2,1,0:T(8,128)(2,1)} %copy-done.33, bf16[256,1024]{1,0:T(8,128)(2,1)} %bitcast.115, ...), custom_call_target="tpu_custom_call" | custom-call | flops 20000000000 | bytes 60000000 | tf_op jit(solution)/shard_map/middle/pallas_call | solution.py:761
  160.0 4.0 %collective-permute-start.14 = (bf16[4096,256]{1,0:T(8,128)(2,1)}, bf16[4096,256]{1,0:T(8,128)(2,1)}, u32[]{:S(2)}, u32[]{:S(2)}) collective-permute-start(bf16[4096,256]{1,0:T(8,128)(2,1)} %get-tuple-element.133.down_l.up_l.out_l), channel_id=1, source_target_pairs={{0,1},{1,0},{2,3},{3,2},{4,5},{5,4},{6,7},{7,6},{8,9},{9,8},{10,11... | collective-permute-start | bytes 6291464 | tf_op jit(solution)/shard_map/ppermute | solution.py:353
  164.7 5.9 %all-to-all-start.3 = ((bf16[8,256,128]{2,1,0:T(8,128)(2,1)}), bf16[8,256,128]{2,1,0:T(8,128)(2,1)}, u32[]{:S(2)}, u32[]{:S(2)}) async-start(bf16[8,256,128]{2,1,0:T(8,128)(2,1)} %get-tuple-element.130), calls=%async_computation.3 | async-start | bytes 1048576 | tf_op jit(solution)/shard_map/all_to_all | solution.py:357
  172.3 9.9 %weight_grads.1 = (bf16[8,768,128]{2,1,0:T(8,128)(2,1)}, bf16[8,768,128]{2,1,0:T(8,128)(2,1)}, bf16[2,4,512,128]{3,2,1,0:T(8,128)(2,1)}, bf16[2,4,512,128]{3,2,1,0:T(8,128)(2,1)}) custom-call(s32[3]{0:T(128)} %pad_add_fusion.1.place_ref, bf16[4096,256]{1,0:T(8,128)(2,1)} %get-tuple-element.133.down_l.up_l.out_l, ...), custom_call_target="tpu_custom_call" | custom-call | flops 8999999488 | bytes 27000000 | tf_op jit(solution)/shard_map/weight_grads/pallas_call | solution.py:831
  183.1 28.5 %attend_back.1.g_ref = bf16[2048,384]{1,0:T(8,128)(2,1)} custom-call(bf16[2048,128]{1,0:T(8,128)(2,1)} %copy-done.9, bf16[2048,128]{1,0:T(8,128)(2,1)} %copy-done.5, bf16[2048,128]{1,0:T(8,128)(2,1)} %bitcast.25.grad_ref, f32[2048,128]{1,0:T(8,128)} %copy-done.22, f32[8,2048]{1,0:T(8,128)} %copy-done.23, f32[2048,128]{1,0:T(8,128)} %copy-done.3, ...), custom_call_target="tpu_custom_call" | custom-call | flops 27000000512 | bytes 81000000 | tf_op jit(solution)/shard_map/attend_back/pallas_call | solution.py:579
  211.5 7.8 %all-to-all-start.4 = ((bf16[8,256,384]{2,1,0:T(8,128)(2,1)}), bf16[8,256,384]{2,1,0:T(8,128)(2,1)}, u32[]{:S(2)}, u32[]{:S(2)}) async-start(bf16[8,256,384]{2,1,0:T(8,128)(2,1)} %bitcast.118), calls=%async_computation.4 | async-start | bytes 3145728 | tf_op jit(solution)/shard_map/all_to_all | solution.py:357
  228.3 11.0 %clip_grads.1 = f32[16,2048]{1,0:T(8,128)} custom-call(s32[2]{0:T(128)} %copy-done.19, bf16[2048,1024]{1,0:T(8,128)(2,1)} %copy-done.6, s32[1,2048]{1,0:T(1,128)} %and_select_fusion.clip_ref, bf16[2048,384]{1,0:T(8,128)(2,1)} %attend_back.1.g_ref, bf16[4,256,384]{2,1,0:T(8,128)(2,1)} %copy-done.4), custom_call_target="tpu_custom_call" | custom-call | flops 8999999488 | bytes 27000000 | tf_op jit(solution)/shard_map/clip_grads/pallas_call | solution.py:862
  239.3 6.0 %convolution_convert_fusion = bf16[1024,384]{1,0:T(8,128)(2,1)} fusion(bf16[2048,1024]{1,0:T(8,128)(2,1)} %copy-done.7, bf16[2048,384]{1,0:T(8,128)(2,1)} %attend_back.1.g_ref), kind=kOutput, calls=%fused_computation.15 | convolution fusion | flops 1611005952 | bytes 6553600 | tf_op jit(solution)/shard_map/dot_general | solution.py:29
  245.3 9.6 %collective-permute-done.21.refs_1_ = bf16[4,768,128]{2,1,0:T(8,128)(2,1)S(1)} collective-permute-done((bf16[4,768,128]{2,1,0:T(8,128)(2,1)}, bf16[4,768,128]{2,1,0:T(8,128)(2,1)S(1)}, u32[]{:S(2)}, u32[]{:S(2)}) %collective-permute-start.21) | collective-permute-done | bytes 786464 | tf_op jit(solution)/shard_map/ppermute | solution.py:353
  269.7 5.5 %last.1 = bf16[256,1024]{1,0:T(8,128)(2,1)} custom-call(s32[3]{0:T(128)S(1)} %copy-done.20, bf16[8,256,384]{2,1,0:T(8,128)(2,1)} %all-to-all-done.4.own_ref, bf16[256,1024]{1,0:T(8,128)(2,1)S(1)} %bitcast.117, f32[256,1024]{1,0:T(8,128)S(1)} %copy-done.21, bf16[256,128]{1,0:T(8,128)(2,1)S(1)} %copy-done.18, bf16[128,6144]{1,0:T(8,128)(2,1)S(1)} %copy-done.1, ...), custom_call_target="tpu_custom_call" | custom-call | flops 4000000000 | bytes 12000000 | tf_op jit(solution)/shard_map/last/pallas_call | solution.py:911
  279.1 7.0 %all_gather.15 = f32[64,768]{1,0:T(8,128)S(1)} all-gather(f32[16,768]{1,0:T(8,128)S(1)} %fusion.26), channel_id=1, replica_groups=mesh['seq'=8,'batch'=4] {'batch'}, dimensions={0}, use_global_device_ids=true | all-gather | bytes 245760 | tf_op jit(solution)/shard_map/all_gather | solution.py:1087
  288.5 9.8 %collective-permute-done.30 = bf16[1280,128]{1,0:T(8,128)(2,1)S(1)} collective-permute-done((bf16[1280,128]{1,0:T(8,128)(2,1)S(1)}, bf16[1280,128]{1,0:T(8,128)(2,1)S(1)}, u32[]{:S(2)}, u32[]{:S(2)}) %collective-permute-start.30) | collective-permute-done | bytes 327712 | tf_op jit(solution)/shard_map/ppermute | solution.py:353
  298.3 8.8 %collective-permute-done.31 = bf16[1280,128]{1,0:T(8,128)(2,1)S(1)} collective-permute-done((bf16[1280,128]{1,0:T(8,128)(2,1)S(1)}, bf16[1280,128]{1,0:T(8,128)(2,1)S(1)}, u32[]{:S(2)}, u32[]{:S(2)}) %collective-permute-start.31) | collective-permute-done | bytes 327712 | tf_op jit(solution)/shard_map/ppermute | solution.py:353
  (244 shorter events, 74.2 us)
Async XLA Ops:
  7.2 23.3 %collective-permute-start = (bf16[256,1024]{1,0:T(8,128)(2,1)}, bf16[256,1024]{1,0:T(8,128)(2,1)S(1)}, u32[]{:S(2)}, u32[]{:S(2)}) collective-permute-start(bf16[256,1024]{1,0:T(8,128)(2,1)} %bitcast.112), channel_id=1, source_target_pairs={{0,8},{4,12},{8,0},{12,4},{16,24},{20,28},{24,16},{28,20},{1,9},{5... | collective-permute-start | bytes 1572872 | tf_op jit(solution)/shard_map/ppermute | solution.py:353
  7.4 25.1 %collective-permute-start.1 = (bf16[256,1024]{1,0:T(8,128)(2,1)}, bf16[256,1024]{1,0:T(8,128)(2,1)S(1)}, u32[]{:S(2)}, u32[]{:S(2)}) collective-permute-start(bf16[256,1024]{1,0:T(8,128)(2,1)} %bitcast.113), channel_id=1, source_target_pairs={{0,16},{4,20},{8,24},{12,28},{16,0},{20,4},{24,8},{28,12},{1,17},{... | collective-permute-start | bytes 1572872 | tf_op jit(solution)/shard_map/ppermute | solution.py:353
  9.8 22.8 %collective-permute-start.2 = (bf16[256,1024]{1,0:T(8,128)(2,1)}, bf16[256,1024]{1,0:T(8,128)(2,1)S(1)}, u32[]{:S(2)}, u32[]{:S(2)}) collective-permute-start(bf16[256,1024]{1,0:T(8,128)(2,1)} %bitcast.114), channel_id=1, source_target_pairs={{0,4},{4,0},{8,12},{12,8},{16,20},{20,16},{24,28},{28,24},{1,5},{5... | collective-permute-start | bytes 1572872 | tf_op jit(solution)/shard_map/ppermute | solution.py:353
  25.2 113.8 %all-gather.4.cloned.1.call-start = ((), (), s32[]{:S(2)}) async-start(), calls=%async_computation.5 | async-start | bytes 10813440 | tf_op jit(solution)/shard_map/all_gather | solution.py:977
  33.5 35.8 %all-to-all-start.1 = ((f32[8,24,768]{2,1,0:T(8,128)}), f32[8,24,768]{2,1,0:T(8,128)}, u32[]{:S(2)}, u32[]{:S(2)}) async-start(f32[8,24,768]{2,1,0:T(8,128)} %broadcast_in_dim.16), calls=%async_computation.1 | async-start | bytes 1179648 | tf_op jit(solution)/shard_map/all_to_all | solution.py:357
  37.9 25.8 %collective-permute-start.4 = (bf16[256,1024]{1,0:T(8,128)(2,1)S(1)}, bf16[256,1024]{1,0:T(8,128)(2,1)}, u32[]{:S(2)}, u32[]{:S(2)}) collective-permute-start(bf16[256,1024]{1,0:T(8,128)(2,1)S(1)} %collective-permute-done.1.c_ref), channel_id=1, source_target_pairs={{0,8},{4,12},{8,0},{12,4},{16,24},{20,28},{24,16},{28,20},{1,9},{5... | collective-permute-start | bytes 1572872 | tf_op jit(solution)/shard_map/ppermute | solution.py:353
  40.0 36.1 %collective-permute-start.7 = (bf16[256,1024]{1,0:T(8,128)(2,1)S(1)}, bf16[256,1024]{1,0:T(8,128)(2,1)S(1)}, u32[]{:S(2)}, u32[]{:S(2)}) collective-permute-start(bf16[256,1024]{1,0:T(8,128)(2,1)S(1)} %collective-permute-done.1.c_ref), channel_id=1, source_target_pairs={{0,4},{4,0},{8,12},{12,8},{16,20},{20,16},{24,28},{28,24},{1,5},{5... | collective-permute-start | bytes 1572872 | tf_op jit(solution)/shard_map/ppermute | solution.py:353
  40.2 35.9 %collective-permute-start.6 = (bf16[256,1024]{1,0:T(8,128)(2,1)S(1)}, bf16[256,1024]{1,0:T(8,128)(2,1)S(1)}, u32[]{:S(2)}, u32[]{:S(2)}) collective-permute-start(bf16[256,1024]{1,0:T(8,128)(2,1)S(1)} %collective-permute-done.b_ref), channel_id=1, source_target_pairs={{0,4},{4,0},{8,12},{12,8},{16,20},{20,16},{24,28},{28,24},{1,5},{5... | collective-permute-start | bytes 1572872 | tf_op jit(solution)/shard_map/ppermute | solution.py:353
  63.7 22.4 %collective-permute-start.8 = (bf16[256,1024]{1,0:T(8,128)(2,1)}, bf16[256,1024]{1,0:T(8,128)(2,1)}, u32[]{:S(2)}, u32[]{:S(2)}) collective-permute-start(bf16[256,1024]{1,0:T(8,128)(2,1)} %collective-permute-done.4.d_ref), channel_id=1, source_target_pairs={{0,4},{4,0},{8,12},{12,8},{16,20},{20,16},{24,28},{28,24},{1,5},{5... | collective-permute-start | bytes 1572872 | tf_op jit(solution)/shard_map/ppermute | solution.py:353
  86.1 25.3 %collective-permute-start.11 = (bf16[768,128]{1,0:T(8,128)(2,1)}, bf16[768,128]{1,0:T(8,128)(2,1)S(1)}, u32[]{:S(2)}, u32[]{:S(2)}) collective-permute-start(bf16[768,128]{1,0:T(8,128)(2,1)} %collective-permute-done.10), channel_id=1, source_target_pairs={{0,8},{4,12},{8,0},{12,4},{16,24},{20,28},{24,16},{28,20},{1,9},{5... | collective-permute-start | bytes 589832 | tf_op jit(solution)/shard_map/ppermute | solution.py:353
  112.1 25.7 %all-to-all-start.2 = ((bf16[8,256,128]{2,1,0:T(8,128)(2,1)}), bf16[8,256,128]{2,1,0:T(8,128)(2,1)S(1)}, u32[]{:S(2)}, u32[]{:S(2)}) async-start(bf16[8,256,128]{2,1,0:T(8,128)(2,1)} %bitcast.15), calls=%async_computation.2 | async-start | bytes 1048576 | tf_op jit(solution)/shard_map/all_to_all | solution.py:357
  137.9 22.0 %collective-permute-start.12 = (bf16[4,768,128]{2,1,0:T(8,128)(2,1)S(1)}, bf16[4,768,128]{2,1,0:T(8,128)(2,1)S(1)}, u32[]{:S(2)}, u32[]{:S(2)}) collective-permute-start(bf16[4,768,128]{2,1,0:T(8,128)(2,1)S(1)} %pad_maximum_fusion.2), channel_id=1, source_target_pairs={{0,4},{4,0},{8,12},{12,8},{16,20},{20,16},{24,28},{28,24},{1,5},{5... | collective-permute-start | bytes 2359304 | tf_op jit(solution)/shard_map/ppermute | solution.py:353
  137.9 22.1 %collective-permute-start.13 = (bf16[4,768,128]{2,1,0:T(8,128)(2,1)S(1)}, bf16[4,768,128]{2,1,0:T(8,128)(2,1)S(1)}, u32[]{:S(2)}, u32[]{:S(2)}) collective-permute-start(bf16[4,768,128]{2,1,0:T(8,128)(2,1)S(1)} %pad_maximum_fusion.2), channel_id=1, source_target_pairs={{0,2},{1,3},{2,0},{3,1},{4,6},{5,7},{6,4},{7,5},{8,10},{9,11},{10,... | collective-permute-start | bytes 2359304 | tf_op jit(solution)/shard_map/ppermute | solution.py:353
  182.6 42.5 %collective-permute-start.16 = (bf16[8,768,128]{2,1,0:T(8,128)(2,1)}, bf16[8,768,128]{2,1,0:T(8,128)(2,1)}, u32[]{:S(2)}, u32[]{:S(2)}) collective-permute-start(bf16[8,768,128]{2,1,0:T(8,128)(2,1)} %get-tuple-element.147), channel_id=1, source_target_pairs={{0,2},{1,3},{2,0},{3,1},{4,6},{5,7},{6,4},{7,5},{8,10},{9,11},{10,... | collective-permute-start | bytes 4718600 | tf_op jit(solution)/shard_map/ppermute | solution.py:353
  183.1 36.3 %collective-permute-start.17 = (bf16[2,4,512,128]{3,2,1,0:T(8,128)(2,1)}, bf16[2,4,512,128]{3,2,1,0:T(8,128)(2,1)}, u32[]{:S(2)}, u32[]{:S(2)}) collective-permute-start(bf16[2,4,512,128]{3,2,1,0:T(8,128)(2,1)} %get-tuple-element.149), channel_id=1, source_target_pairs={{0,4},{4,0},{8,12},{12,8},{16,20},{20,16},{24,28},{28,24},{1,5},{5... | collective-permute-start | bytes 3145736 | tf_op jit(solution)/shard_map/ppermute | solution.py:353
  211.5 44.8 %all-to-all-start.4 = ((bf16[8,256,384]{2,1,0:T(8,128)(2,1)}), bf16[8,256,384]{2,1,0:T(8,128)(2,1)}, u32[]{:S(2)}, u32[]{:S(2)}) async-start(bf16[8,256,384]{2,1,0:T(8,128)(2,1)} %bitcast.118), calls=%async_computation.4 | async-start | bytes 3145728 | tf_op jit(solution)/shard_map/all_to_all | solution.py:357
  221.4 34.2 %collective-permute-start.20 = (bf16[12,768,128]{2,1,0:T(8,128)(2,1)S(1)}, bf16[12,768,128]{2,1,0:T(8,128)(2,1)}, u32[]{:S(2)}, u32[]{:S(2)}) collective-permute-start(bf16[12,768,128]{2,1,0:T(8,128)(2,1)S(1)} %pad_maximum_fusion.refs_0_), channel_id=1, source_target_pairs={{0,1},{1,0},{2,3},{3,2},{4,5},{5,4},{6,7},{7,6},{8,9},{9,8},{10,11... | collective-permute-start | bytes 7077896 | tf_op jit(solution)/shard_map/ppermute | solution.py:353
  224.1 31.4 %collective-permute-start.19 = (bf16[4,512,128]{2,1,0:T(8,128)(2,1)}, bf16[4,512,128]{2,1,0:T(8,128)(2,1)S(1)}, u32[]{:S(2)}, u32[]{:S(2)}) collective-permute-start(bf16[4,512,128]{2,1,0:T(8,128)(2,1)} %fusion.7), channel_id=1, source_target_pairs={{0,2},{1,3},{2,0},{3,1},{4,6},{5,7},{6,4},{7,5},{8,10},{9,11},{10,... | collective-permute-start | bytes 1572872 | tf_op jit(solution)/shard_map/ppermute | solution.py:353
  227.6 27.9 %collective-permute-start.18 = (bf16[4,768,128]{2,1,0:T(8,128)(2,1)}, bf16[4,768,128]{2,1,0:T(8,128)(2,1)}, u32[]{:S(2)}, u32[]{:S(2)}) collective-permute-start(bf16[4,768,128]{2,1,0:T(8,128)(2,1)} %add_convert_fusion.1), channel_id=1, source_target_pairs={{0,4},{4,0},{8,12},{12,8},{16,20},{20,16},{24,28},{28,24},{1,5},{5... | collective-permute-start | bytes 2359304 | tf_op jit(solution)/shard_map/ppermute | solution.py:353
  227.9 27.0 %collective-permute-start.21 = (bf16[4,768,128]{2,1,0:T(8,128)(2,1)}, bf16[4,768,128]{2,1,0:T(8,128)(2,1)S(1)}, u32[]{:S(2)}, u32[]{:S(2)}) collective-permute-start(bf16[4,768,128]{2,1,0:T(8,128)(2,1)} %copy-done.27), channel_id=1, source_target_pairs={{0,2},{1,3},{2,0},{3,1},{4,6},{5,7},{6,4},{7,5},{8,10},{9,11},{10,... | collective-permute-start | bytes 2359304 | tf_op jit(solution)/shard_map/ppermute | solution.py:353
  260.3 25.9 %collective-permute-start.27 = (bf16[2,256,384]{2,1,0:T(8,128)(2,1)S(1)}, bf16[2,256,384]{2,1,0:T(8,128)(2,1)S(1)}, u32[]{:S(2)}, u32[]{:S(2)}) collective-permute-start(bf16[2,256,384]{2,1,0:T(8,128)(2,1)S(1)} %dynamic-slice_bitcast_fusion), channel_id=1, source_target_pairs={{0,1},{1,0},{2,3},{3,2},{4,5},{5,4},{6,7},{7,6},{8,9},{9,8},{10,11... | collective-permute-start | bytes 1179656 | tf_op jit(solution)/shard_map/ppermute | solution.py:353
  263.8 24.7 %collective-permute-start.29 = (bf16[1280,128]{1,0:T(8,128)(2,1)S(1)}, bf16[1280,128]{1,0:T(8,128)(2,1)S(1)}, u32[]{:S(2)}, u32[]{:S(2)}) collective-permute-start(bf16[1280,128]{1,0:T(8,128)(2,1)S(1)} %get-tuple-element.175), channel_id=1, source_target_pairs={{0,8},{4,12},{8,0},{12,4},{16,24},{20,28},{24,16},{28,20},{1,9},{5... | collective-permute-start | bytes 983048 | tf_op jit(solution)/shard_map/ppermute | solution.py:353
  275.3 23.0 %collective-permute-start.30 = (bf16[1280,128]{1,0:T(8,128)(2,1)S(1)}, bf16[1280,128]{1,0:T(8,128)(2,1)S(1)}, u32[]{:S(2)}, u32[]{:S(2)}) collective-permute-start(bf16[1280,128]{1,0:T(8,128)(2,1)S(1)} %get-tuple-element.174), channel_id=1, source_target_pairs={{0,16},{4,20},{8,24},{12,28},{16,0},{20,4},{24,8},{28,12},{1,17},{... | collective-permute-start | bytes 983048 | tf_op jit(solution)/shard_map/ppermute | solution.py:353
  277.8 29.3 %collective-permute-start.31 = (bf16[1280,128]{1,0:T(8,128)(2,1)S(1)}, bf16[1280,128]{1,0:T(8,128)(2,1)S(1)}, u32[]{:S(2)}, u32[]{:S(2)}) collective-permute-start(bf16[1280,128]{1,0:T(8,128)(2,1)S(1)} %get-tuple-element.173), channel_id=1, source_target_pairs={{0,24},{4,28},{8,16},{12,20},{16,8},{20,12},{24,0},{28,4},{1,25},{... | collective-permute-start | bytes 983048 | tf_op jit(solution)/shard_map/ppermute | solution.py:353
  (60 other events, 618.9 us)
Sparse Core Ops, SparseCore 0:
  33.6 105.3 all-gather.3
where the time goes:
time: 318 us; the launch traced here: 316 us
  Pallas kernels  105 us (33%)
  waiting for transfers between devices  75.7 us (24%)
  starting transfers between devices  59.1 us (19%)
  other arithmetic  22.3 us (7%)
  local copies, waits for them, and re-layouts  17.2 us (5%)
  between operations  15.6 us (5%)
  blocking collectives  12.4 us (4%)
  matrix products  9.66 us (3%)
    ppermute x32, waiting for transfers between devices, swap(): return lax.ppermute(part, axis, [(i, i ^ distance) for i in range(size)])  53.6 us
    ppermute x32, starting transfers between devices, swap(): return lax.ppermute(part, axis, [(i, i ^ distance) for i in range(size)])  31.3 us
    pallas_call x1, Pallas kernels, attend_back(): pl.pallas_call(attend_back_kernel, grid=(frames // ROWS,), in_specs=[rows...  28.5 us
    all_to_all x4, starting transfers between devices, exchange(): return lax.all_to_all(blocks, 'seq', 0, 0, tiled=True)  23.3 us
    pallas_call x1, Pallas kernels, middle_part(): pl.pallas_call(middle_kernel, in_specs=[vmem] * 6 + [pl.BlockSpec(memory_...  20.8 us
    all_to_all x4, waiting for transfers between devices, exchange(): return lax.all_to_all(blocks, 'seq', 0, 0, tiled=True)  18.9 us
    pallas_call x1, Pallas kernels, attend(): pl.pallas_call(attend_kernel, grid=(frames // BLOCK,), in_specs=[block_sp...  16.1 us
    pallas_call x2, Pallas kernels, project(): pl.pallas_call(project_kernel, grid_spec=pltpu.PrefetchScalarGridSpec(num...  12.7 us
  transfers between devices with their start and end apart: 38, of which 12 were waited for; matrix products, arithmetic and copies ran while one was open for 13% of the time, Pallas kernels for 33%

commit v1 on v0

--- a/solution.py
+++ b/solution.py
@@ -622,25 +622,38 @@
     return 16 * (away % 2) + 8 * (away // 2) + 4 * (apart % 2) + apart // 2
 
 
-def middle_kernel(mine_ref, x_ref, cot_ref, member_ref, clip_ref, emb_ref, *refs):
-    *tile_refs, result_ref, grad_middle_ref, grad_att_ref, grad_emb_ref, left_ref, right_ref = refs[:-9]
-    out_ref, up_ref, down_ref, sems, branch_ref, low_ref, act_ref, slope_ref, wide_ref = refs[-9:]
+def middle_kernel(mine_ref, x_ref, member_ref, clip_ref, cot_any, emb_any, tiles_ref,
+                  result_any, grad_middle_ref, grad_att_ref, grad_emb_ref, left_any, right_any,
+                  out_ref, up_ref, down_ref, cot_ref, emb_ref, result_ref, left_ref, right_ref,
+                  sems, branch_ref, low_ref, act_ref, slope_ref, wide_ref):
     low = jnp.bfloat16
     act_t_ref, ffn_t_ref = left_ref.at[:2 * D], left_ref.at[2 * D:3 * D]
     mine_t_ref = left_ref.at[3 * D:]
     g_ffn_ref, g_attn_ref = right_ref.at[:, :D], right_ref.at[:, 3 * D:]
     g_hidden_ref = right_ref.at[:, D:3 * D]
-    pieces = ((out_ref, 0, 256), (up_ref, 256, 512), (down_ref, 768, 512))
-    for i, (ref, start, size) in enumerate(pieces):
-        first = 0
-        for tile_ref in tile_refs:
-            count = tile_ref.shape[0]
-            pltpu.make_async_copy(
-                tile_ref.at[:, pl.ds(start, size), :], ref.at[pl.ds(first, count)], sems.at[i]
-            ).start()
-            first += count
     copies = [
-        pltpu.make_async_copy(ref, ref, sems.at[i]) for i, (ref, _, _) in enumerate(pieces)
+        pltpu.make_async_copy(source, target, sems.at[i])
+        for i, (source, target) in enumerate((
+            (tiles_ref.at[:, pl.ds(0, 256), :], out_ref),
+            (emb_any, emb_ref),
+            (cot_any, cot_ref),
+            (tiles_ref.at[:, pl.ds(256, 512), :], up_ref),
+            (tiles_ref.at[:, pl.ds(768, 512), :], down_ref),
+        ))
+    ]
+    for copy in copies:
+        copy.start()
+    stores = [
+        pltpu.make_async_copy(source, target, sems.at[len(copies) + i])
+        for i, (source, target) in enumerate((
+            (mine_t_ref, left_any.at[3 * D:]),
+            (ffn_t_ref, left_any.at[2 * D:3 * D]),
+            (g_ffn_ref, right_any.at[:, :D]),
+            (act_t_ref, left_any.at[:2 * D]),
+            (result_ref, result_any),
+            (g_hidden_ref, right_any.at[:, D:3 * D]),
+            (g_attn_ref, right_any.at[:, 3 * D:]),
+        ))
     ]
 
     def tile(b, s):
@@ -658,7 +671,7 @@
     mine = jnp.concatenate([mine_ref[j] for j in range(SEQ)], axis=1)
     low_ref[...] = mine
     mine_t_ref[...] = mine.T
-    gate_attn = modulation(2)
+    stores[0].start()
     copies[0].wait()
 
     @pl.loop(0, 4)
@@ -669,6 +682,8 @@
             total = total + matmul(low_ref[:, 256 * b:256 * b + 256], weight)
         branch_ref[:, cols(n)] = total
 
+    copies[1].wait()
+    gate_attn = modulation(2)
     branch = branch_ref[...]
     middle = x_ref[...].astype(jnp.float32) + gate_attn * branch
     normed, inverse = standardize(middle)
@@ -677,9 +692,12 @@
     low_ref[...] = ffn_input.astype(low)
     ffn_t_ref[...] = ffn_input.T.astype(low)
     gate_ffn = modulation(5)
+    copies[2].wait()
     cot = cot_ref[...].astype(jnp.float32)
     g_ffn_ref[...] = (cot * gate_ffn).astype(low)
-    copies[1].wait()
+    stores[1].start()
+    stores[2].start()
+    copies[3].wait()
 
     @pl.loop(0, 8)
     def _(n):
@@ -700,7 +718,8 @@
         act_t_ref[cols(n), :] = activated.T.astype(low)
         slope_ref[:, cols(n)] = slope
 
-    copies[2].wait()
+    stores[3].start()
+    copies[4].wait()
 
     @pl.loop(0, 4)
     def _(n):
@@ -712,6 +731,7 @@
 
     ffn_branch = wide_ref[...]
     result_ref[...] = (middle + gate_ffn * ffn_branch).astype(low)
+    stores[4].start()
     grad_emb_ref[:, 3 * D:] = sum_of_clips(clip_ref, cot * ffn_branch)
 
     @pl.loop(0, REPLICAS)
@@ -720,6 +740,8 @@
         grad = dot_t(g_ffn_ref[...], weight)
         here = cols(b, 512)
         g_hidden_ref[:, here] = (grad * slope_ref[:, here]).astype(low)
+
+    stores[5].start()
 
     @pl.loop(0, REPLICAS)
     def _(b):
@@ -741,6 +763,7 @@
     grad_middle_ref[...] = grad_middle
     grad_emb_ref[:, :D] = sum_of_clips(clip_ref, grad_middle * branch)
     g_attn_ref[...] = (grad_middle * gate_attn).astype(low)
+    stores[6].start()
 
     @pl.loop(0, REPLICAS)
     def _(b):
@@ -749,25 +772,32 @@
         grad_att_ref[2 * b] = grad[:, :TWO]
         grad_att_ref[2 * b + 1] = grad[:, TWO:]
 
+    for store in stores:
+        store.wait()
+
 
 def middle_part(mine, x, cot, member, clip_row, emb, tiles):
     low = jnp.bfloat16
     shapes = [
         ((ROWS, D), low), ((ROWS, D), jnp.float32), ((SEQ, ROWS, TWO), low),
-        ((CLIPS, 4 * D), jnp.float32),
-        ((4 * D, ROWS), low), ((ROWS, 4 * D), low),
+        ((CLIPS, 4 * D), jnp.float32), ((4 * D, ROWS), low), ((ROWS, 4 * D), low),
     ]
-    vmem = pl.BlockSpec(memory_space=pltpu.VMEM)
+    vmem, anywhere = pl.BlockSpec(memory_space=pltpu.VMEM), pl.BlockSpec(memory_space=pl.ANY)
     return pl.pallas_call(
         middle_kernel,
-        in_specs=[vmem] * 6 + [pl.BlockSpec(memory_space=pl.ANY)] * len(tiles),
-        out_specs=[vmem] * len(shapes),
+        in_specs=[vmem] * 4 + [anywhere] * 3,
+        out_specs=[anywhere, vmem, vmem, vmem, anywhere, anywhere],
         out_shape=[jax.ShapeDtypeStruct(shape, dtype) for shape, dtype in shapes],
         scratch_shapes=[
             pltpu.VMEM((32, 256, 128), low),
             pltpu.VMEM((32, 512, 128), low),
             pltpu.VMEM((32, 512, 128), low),
-            pltpu.SemaphoreType.DMA((3,)),
+            pltpu.VMEM((ROWS, D), low),
+            pltpu.VMEM((TWO, 6 * D), low),
+            pltpu.VMEM((ROWS, D), low),
+            pltpu.VMEM((4 * D, ROWS), low),
+            pltpu.VMEM((ROWS, 4 * D), low),
+            pltpu.SemaphoreType.DMA((12,)),
             pltpu.VMEM((ROWS, D), jnp.float32),
             pltpu.VMEM((ROWS, D), low),
             pltpu.VMEM((ROWS, 2 * D), low),
@@ -777,7 +807,7 @@
         compiler_params=pltpu.CompilerParams(vmem_limit_bytes=VMEM_MIB * 1024 * 1024),
         cost_estimate=cost(20),
         name="middle",
-    )(mine, x, cot, member, clip_row, emb, *tiles)
+    )(mine, x, member, clip_row, cot, emb, *tiles)
 
 
 def weight_grads_kernel(place_ref, down_l, up_l, out_l, right_ref, down_o, up_o, out_o, other_ref,
@@ -1034,9 +1064,9 @@
     other_left, other_right, h_first = together(other_left, other_right, h_first)
     away_d, keep_d, away_u, keep_u = weight_grads(place, left, right, other_left, other_right)
     grad_heads = exchange(grad_att).reshape(frames, TWO)
-    grad_heads, away_d, away_u = together(grad_heads, away_d, away_u)
     from_x = swap(away_d, "batch", 2)
     from_y = swap(away_u, "seq", 1)
+    grad_heads = after(grad_heads, away_d, away_u)
 
     g_heads = attend_back(
         q, member, grad_heads, attended, log_total, cosine, sine, k, kt, v

time: 318 us -> 315 us (level)
  transfers between devices with their start and end apart: 38 -> 38, of which waited for: 12 -> 10; matrix products, arithmetic and copies ran while one was open for 13% -> 13% of each run, Pallas kernels for 33% -> 33%
where the time goes in v1:
time: 315 us; the launch traced here: 313 us
  Pallas kernels  103 us (33%)
  waiting for transfers between devices  75.1 us (24%)
  starting transfers between devices  58.2 us (18%)
  other arithmetic  22.2 us (7%)
  local copies, waits for them, and re-layouts  17.2 us (5%)
  between operations  15.6 us (5%)
  blocking collectives  12.4 us (4%)
  matrix products  9.66 us (3%)
    ppermute x32, waiting for transfers between devices, swap(): return lax.ppermute(part, axis, [(i, i ^ distance) for i in range(size)])  53.3 us
    ppermute x32, starting transfers between devices, swap(): return lax.ppermute(part, axis, [(i, i ^ distance) for i in range(size)])  32.1 us
    pallas_call x1, Pallas kernels, attend_back(): pl.pallas_call(attend_back_kernel, grid=(frames // ROWS,), in_specs=[rows...  28.5 us
    all_to_all x4, starting transfers between devices, exchange(): return lax.all_to_all(blocks, 'seq', 0, 0, tiled=True)  21.5 us
    pallas_call x1, Pallas kernels, middle_part(): pl.pallas_call(middle_kernel, in_specs=[vmem] * 4 + [anywhere] * 3, out_s...  19.3 us
    all_to_all x4, waiting for transfers between devices, exchange(): return lax.all_to_all(blocks, 'seq', 0, 0, tiled=True)  18.5 us
    pallas_call x1, Pallas kernels, attend(): pl.pallas_call(attend_kernel, grid=(frames // BLOCK,), in_specs=[block_sp...  16.1 us
    pallas_call x2, Pallas kernels, project(): pl.pallas_call(project_kernel, grid_spec=pltpu.PrefetchScalarGridSpec(num...  12.7 us
  transfers between devices with their start and end apart: 38, of which 10 were waited for; matrix products, arithmetic and copies ran while one was open for 13% of the time, Pallas kernels for 33%

profile of v1, /device:TPU:13, one launch (start us, length us, event | category | flops | bytes accessed | tf_op | source)
XLA Modules:
  0.0 313.3 jit_solution(7820521079754426805)
XLA Ops:
  12.6 5.4 %all-reduce.1 = s32[64]{0:T(128)S(1)} all-reduce(s32[64]{0:T(128)S(1)} %bitcast_dynamic-update-slice_fusion), channel_id=2, replica_groups=mesh['seq'=8,'batch'=4] {'batch'}, use_global_device_ids=true, to_apply=%add.1 | all-reduce | flops 64 | bytes 512
  20.7 4.5 %all-to-all-start = ((f32[4,16,768]{2,1,0:T(8,128)}), f32[4,16,768]{2,1,0:T(8,128)S(1)}, u32[]{:S(2)}, u32[]{:S(2)}) async-start(f32[4,16,768]{2,1,0:T(8,128)} %bitcast.5), calls=%async_computation | async-start | bytes 393216 | tf_op jit(solution)/shard_map/all_to_all | solution.py:997
  26.5 3.2 %all-to-all-done = f32[4,16,768]{2,1,0:T(8,128)S(1)} async-done(((f32[4,16,768]{2,1,0:T(8,128)}), f32[4,16,768]{2,1,0:T(8,128)S(1)}, u32[]{:S(2)}, u32[]{:S(2)}) %all-to-all-start) | async-done | bytes 196640 | tf_op jit(solution)/shard_map/all_to_all | solution.py:997
  33.5 4.4 %all-to-all-start.1 = ((f32[8,24,768]{2,1,0:T(8,128)}), f32[8,24,768]{2,1,0:T(8,128)}, u32[]{:S(2)}, u32[]{:S(2)}) async-start(f32[8,24,768]{2,1,0:T(8,128)} %broadcast_in_dim.16), calls=%async_computation.1 | async-start | bytes 1179648 | tf_op jit(solution)/shard_map/all_to_all | solution.py:357
  45.5 18.3 %collective-permute-done.4.d_ref = bf16[256,1024]{1,0:T(8,128)(2,1)} collective-permute-done((bf16[256,1024]{1,0:T(8,128)(2,1)S(1)}, bf16[256,1024]{1,0:T(8,128)(2,1)}, u32[]{:S(2)}, u32[]{:S(2)}) %collective-permute-start.4) | collective-permute-done | bytes 524320 | tf_op jit(solution)/shard_map/ppermute | solution.py:353
  72.4 3.7 %multiply_sine_fusion = (f32[2048,128]{1,0:T(8,128)S(1)}, f32[2048,128]{1,0:T(8,128)S(1)}) fusion(f32[128]{0:T(128)S(1)} %mul.62, f32[2048]{0:T(1024)S(1)} %bitcast.131), kind=kLoop, calls=%fused_computation.13 | loop fusion | flops 262144 | bytes 2105856 | tf_op jit(solution)/shard_map/sin | solution.py:1032
  78.8 6.3 %project.2 = (bf16[2048,1024]{1,0:T(8,128)(2,1)S(1)}, bf16[2048,1024]{1,0:T(8,128)(2,1)S(1)}, bf16[2048,128]{1,0:T(8,128)(2,1)S(1)}, bf16[2048,256]{1,0:T(8,128)...) custom-call(s32[2]{0:T(128)S(1)} %pad_add_fusion.place_ref, ...), custom_call_target="tpu_custom_call" | custom-call | flops 2000000000 | bytes 6000000 | tf_op jit(solution)/shard_map/project/pallas_call | solution.py:449
  87.3 6.3 %project.3 = (bf16[2048,1024]{1,0:T(8,128)(2,1)S(1)}, bf16[2048,1024]{1,0:T(8,128)(2,1)S(1)}, bf16[2048,128]{1,0:T(8,128)(2,1)S(1)}, bf16[2048,256]{1,0:T(8,128)...) custom-call(s32[2]{0:T(128)S(1)} %pad_add_fusion.place_ref, ...), custom_call_target="tpu_custom_call", output_to_operand_aliasing={{0}: (11, {}), {1}: (12, {}), {2}: (13, {}), {3}: (14, {}),... | custom-call | flops 2000000000 | bytes 6000000 | tf_op jit(solution)/shard_map/project/pallas_call | solution.py:449
  93.7 16.1 %attend.1 = (f32[2048,128]{1,0:T(8,128)S(1)}, bf16[2048,128]{1,0:T(8,128)(2,1)}, f32[8,2048]{1,0:T(8,128)S(1)}) custom-call(bf16[2048,128]{1,0:T(8,128)(2,1)S(1)} %get-tuple-element.116.q_ref, bf16[2048,128]{1,0:T(8,128)(2,1)S(1)} %and_convert_fusion.member_ref, bf16[2048,256]{1,0:T(8,128)(2,1)S(1)} %get-tuple-element.117.k_ref, ...), custom_call_target="tpu_custom_call" | custom-call | flops 17999998976 | bytes 54000000 | tf_op jit(solution)/shard_map/attend/pallas_call | solution.py:512
  112.1 5.2 %all-to-all-start.2 = ((bf16[8,256,128]{2,1,0:T(8,128)(2,1)}), bf16[8,256,128]{2,1,0:T(8,128)(2,1)S(1)}, u32[]{:S(2)}, u32[]{:S(2)}) async-start(bf16[8,256,128]{2,1,0:T(8,128)(2,1)} %bitcast.15), calls=%async_computation.2 | async-start | bytes 1048576 | tf_op jit(solution)/shard_map/all_to_all | solution.py:357
  119.3 18.5 %all-to-all-done.2.mine_ref = bf16[8,256,128]{2,1,0:T(8,128)(2,1)S(1)} async-done(((bf16[8,256,128]{2,1,0:T(8,128)(2,1)}), bf16[8,256,128]{2,1,0:T(8,128)(2,1)S(1)}, u32[]{:S(2)}, u32[]{:S(2)}) %all-to-all-start.2) | async-done | bytes 524320 | tf_op jit(solution)/shard_map/all_to_all | solution.py:357
  139.1 19.3 %middle.1 = (bf16[256,1024]{1,0:T(8,128)(2,1)}, f32[256,1024]{1,0:T(8,128)}, bf16[8,256,128]{2,1,0:T(8,128)(2,1)}, f32[16,4096]{1,0:T(8,128)}, bf16[4096,256]{1,0:T(8,128)(2,1)}, /*index=5*/bf16[256,4096]{1,0:T(8,128)(2,1)}) custom-call(bf16[8,256,128]{2,1,0:T(8,128)(2,1)} %copy-done.33, bf16[256,1024]{1,0:T(8,128)(2,1)} %bitcast.115, ...), custom_call_target="tpu_custom_call" | custom-call | flops 20000000000 | bytes 60000000 | tf_op jit(solution)/shard_map/middle/pallas_call | solution.py:786
  158.4 4.0 %collective-permute-start.14 = (bf16[4096,256]{1,0:T(8,128)(2,1)}, bf16[4096,256]{1,0:T(8,128)(2,1)}, u32[]{:S(2)}, u32[]{:S(2)}) collective-permute-start(bf16[4096,256]{1,0:T(8,128)(2,1)} %get-tuple-element.131.down_l.up_l.out_l), channel_id=1, source_target_pairs={{0,1},{1,0},{2,3},{3,2},{4,5},{5,4},{6,7},{7,6},{8,9},{9,8},{10,11... | collective-permute-start | bytes 6291464 | tf_op jit(solution)/shard_map/ppermute | solution.py:353
  163.2 5.9 %all-to-all-start.3 = ((bf16[8,256,128]{2,1,0:T(8,128)(2,1)}), bf16[8,256,128]{2,1,0:T(8,128)(2,1)}, u32[]{:S(2)}, u32[]{:S(2)}) async-start(bf16[8,256,128]{2,1,0:T(8,128)(2,1)} %get-tuple-element.128), calls=%async_computation.3 | async-start | bytes 1048576 | tf_op jit(solution)/shard_map/all_to_all | solution.py:357
  170.8 9.9 %weight_grads.1 = (bf16[8,768,128]{2,1,0:T(8,128)(2,1)}, bf16[8,768,128]{2,1,0:T(8,128)(2,1)}, bf16[2,4,512,128]{3,2,1,0:T(8,128)(2,1)}, bf16[2,4,512,128]{3,2,1,0:T(8,128)(2,1)}) custom-call(s32[3]{0:T(128)} %pad_add_fusion.1.place_ref, bf16[4096,256]{1,0:T(8,128)(2,1)} %get-tuple-element.131.down_l.up_l.out_l, ...), custom_call_target="tpu_custom_call" | custom-call | flops 8999999488 | bytes 27000000 | tf_op jit(solution)/shard_map/weight_grads/pallas_call | solution.py:861
  181.5 28.5 %attend_back.1.g_ref = bf16[2048,384]{1,0:T(8,128)(2,1)} custom-call(bf16[2048,128]{1,0:T(8,128)(2,1)} %copy-done.9, bf16[2048,128]{1,0:T(8,128)(2,1)} %copy-done.5, bf16[2048,128]{1,0:T(8,128)(2,1)} %bitcast.25.grad_ref, f32[2048,128]{1,0:T(8,128)} %copy-done.22, f32[8,2048]{1,0:T(8,128)} %copy-done.23, f32[2048,128]{1,0:T(8,128)} %copy-done.3, ...), custom_call_target="tpu_custom_call" | custom-call | flops 27000000512 | bytes 81000000 | tf_op jit(solution)/shard_map/attend_back/pallas_call | solution.py:579
  210.0 6.1 %all-to-all-start.4 = ((bf16[8,256,384]{2,1,0:T(8,128)(2,1)}), bf16[8,256,384]{2,1,0:T(8,128)(2,1)}, u32[]{:S(2)}, u32[]{:S(2)}) async-start(bf16[8,256,384]{2,1,0:T(8,128)(2,1)} %bitcast.118), calls=%async_computation.4 | async-start | bytes 3145728 | tf_op jit(solution)/shard_map/all_to_all | solution.py:357
  224.6 11.0 %clip_grads.1 = f32[16,2048]{1,0:T(8,128)} custom-call(s32[2]{0:T(128)} %copy-done.19, bf16[2048,1024]{1,0:T(8,128)(2,1)} %copy-done.6, s32[1,2048]{1,0:T(1,128)} %and_select_fusion.clip_ref, bf16[2048,384]{1,0:T(8,128)(2,1)} %attend_back.1.g_ref, bf16[4,256,384]{2,1,0:T(8,128)(2,1)} %copy-done.4), custom_call_target="tpu_custom_call" | custom-call | flops 8999999488 | bytes 27000000 | tf_op jit(solution)/shard_map/clip_grads/pallas_call | solution.py:892
  235.5 6.0 %convolution_convert_fusion = bf16[1024,384]{1,0:T(8,128)(2,1)} fusion(bf16[2048,1024]{1,0:T(8,128)(2,1)} %copy-done.7, bf16[2048,384]{1,0:T(8,128)(2,1)} %attend_back.1.g_ref), kind=kOutput, calls=%fused_computation.15 | convolution fusion | flops 1611005952 | bytes 6553600 | tf_op jit(solution)/shard_map/dot_general | solution.py:29
  241.5 9.6 %collective-permute-done.21.refs_1_ = bf16[4,768,128]{2,1,0:T(8,128)(2,1)S(1)} collective-permute-done((bf16[4,768,128]{2,1,0:T(8,128)(2,1)}, bf16[4,768,128]{2,1,0:T(8,128)(2,1)S(1)}, u32[]{:S(2)}, u32[]{:S(2)}) %collective-permute-start.21) | collective-permute-done | bytes 786464 | tf_op jit(solution)/shard_map/ppermute | solution.py:353
  266.5 5.5 %last.1 = bf16[256,1024]{1,0:T(8,128)(2,1)} custom-call(s32[3]{0:T(128)S(1)} %copy-done.20, bf16[8,256,384]{2,1,0:T(8,128)(2,1)} %all-to-all-done.4.own_ref, bf16[256,1024]{1,0:T(8,128)(2,1)S(1)} %bitcast.117, f32[256,1024]{1,0:T(8,128)S(1)} %copy-done.21, bf16[256,128]{1,0:T(8,128)(2,1)S(1)} %copy-done.18, bf16[128,6144]{1,0:T(8,128)(2,1)S(1)} %copy-done.1, ...), custom_call_target="tpu_custom_call" | custom-call | flops 4000000000 | bytes 12000000 | tf_op jit(solution)/shard_map/last/pallas_call | solution.py:941
  276.0 7.0 %all_gather.15 = f32[64,768]{1,0:T(8,128)S(1)} all-gather(f32[16,768]{1,0:T(8,128)S(1)} %fusion.26), channel_id=1, replica_groups=mesh['seq'=8,'batch'=4] {'batch'}, dimensions={0}, use_global_device_ids=true | all-gather | bytes 245760 | tf_op jit(solution)/shard_map/all_gather | solution.py:1117
  285.0 10.1 %collective-permute-done.30 = bf16[1280,128]{1,0:T(8,128)(2,1)S(1)} collective-permute-done((bf16[1280,128]{1,0:T(8,128)(2,1)S(1)}, bf16[1280,128]{1,0:T(8,128)(2,1)S(1)}, u32[]{:S(2)}, u32[]{:S(2)}) %collective-permute-start.30) | collective-permute-done | bytes 327712 | tf_op jit(solution)/shard_map/ppermute | solution.py:353
  295.1 8.8 %collective-permute-done.31 = bf16[1280,128]{1,0:T(8,128)(2,1)S(1)} collective-permute-done((bf16[1280,128]{1,0:T(8,128)(2,1)S(1)}, bf16[1280,128]{1,0:T(8,128)(2,1)S(1)}, u32[]{:S(2)}, u32[]{:S(2)}) %collective-permute-start.31) | collective-permute-done | bytes 327712 | tf_op jit(solution)/shard_map/ppermute | solution.py:353
  (244 shorter events, 74.0 us)
Async XLA Ops:
  7.2 23.3 %collective-permute-start = (bf16[256,1024]{1,0:T(8,128)(2,1)}, bf16[256,1024]{1,0:T(8,128)(2,1)S(1)}, u32[]{:S(2)}, u32[]{:S(2)}) collective-permute-start(bf16[256,1024]{1,0:T(8,128)(2,1)} %bitcast.112), channel_id=1, source_target_pairs={{0,8},{4,12},{8,0},{12,4},{16,24},{20,28},{24,16},{28,20},{1,9},{5... | collective-permute-start | bytes 1572872 | tf_op jit(solution)/shard_map/ppermute | solution.py:353
  7.4 25.1 %collective-permute-start.1 = (bf16[256,1024]{1,0:T(8,128)(2,1)}, bf16[256,1024]{1,0:T(8,128)(2,1)S(1)}, u32[]{:S(2)}, u32[]{:S(2)}) collective-permute-start(bf16[256,1024]{1,0:T(8,128)(2,1)} %bitcast.113), channel_id=1, source_target_pairs={{0,16},{4,20},{8,24},{12,28},{16,0},{20,4},{24,8},{28,12},{1,17},{... | collective-permute-start | bytes 1572872 | tf_op jit(solution)/shard_map/ppermute | solution.py:353
  9.8 22.8 %collective-permute-start.2 = (bf16[256,1024]{1,0:T(8,128)(2,1)}, bf16[256,1024]{1,0:T(8,128)(2,1)S(1)}, u32[]{:S(2)}, u32[]{:S(2)}) collective-permute-start(bf16[256,1024]{1,0:T(8,128)(2,1)} %bitcast.114), channel_id=1, source_target_pairs={{0,4},{4,0},{8,12},{12,8},{16,20},{20,16},{24,28},{28,24},{1,5},{5... | collective-permute-start | bytes 1572872 | tf_op jit(solution)/shard_map/ppermute | solution.py:353
  25.2 113.8 %all-gather.4.cloned.1.call-start = ((), (), s32[]{:S(2)}) async-start(), calls=%async_computation.5 | async-start | bytes 10813440 | tf_op jit(solution)/shard_map/all_gather | solution.py:1007
  33.5 35.8 %all-to-all-start.1 = ((f32[8,24,768]{2,1,0:T(8,128)}), f32[8,24,768]{2,1,0:T(8,128)}, u32[]{:S(2)}, u32[]{:S(2)}) async-start(f32[8,24,768]{2,1,0:T(8,128)} %broadcast_in_dim.16), calls=%async_computation.1 | async-start | bytes 1179648 | tf_op jit(solution)/shard_map/all_to_all | solution.py:357
  37.9 25.8 %collective-permute-start.4 = (bf16[256,1024]{1,0:T(8,128)(2,1)S(1)}, bf16[256,1024]{1,0:T(8,128)(2,1)}, u32[]{:S(2)}, u32[]{:S(2)}) collective-permute-start(bf16[256,1024]{1,0:T(8,128)(2,1)S(1)} %collective-permute-done.1.c_ref), channel_id=1, source_target_pairs={{0,8},{4,12},{8,0},{12,4},{16,24},{20,28},{24,16},{28,20},{1,9},{5... | collective-permute-start | bytes 1572872 | tf_op jit(solution)/shard_map/ppermute | solution.py:353
  40.0 36.1 %collective-permute-start.7 = (bf16[256,1024]{1,0:T(8,128)(2,1)S(1)}, bf16[256,1024]{1,0:T(8,128)(2,1)S(1)}, u32[]{:S(2)}, u32[]{:S(2)}) collective-permute-start(bf16[256,1024]{1,0:T(8,128)(2,1)S(1)} %collective-permute-done.1.c_ref), channel_id=1, source_target_pairs={{0,4},{4,0},{8,12},{12,8},{16,20},{20,16},{24,28},{28,24},{1,5},{5... | collective-permute-start | bytes 1572872 | tf_op jit(solution)/shard_map/ppermute | solution.py:353
  40.2 35.9 %collective-permute-start.6 = (bf16[256,1024]{1,0:T(8,128)(2,1)S(1)}, bf16[256,1024]{1,0:T(8,128)(2,1)S(1)}, u32[]{:S(2)}, u32[]{:S(2)}) collective-permute-start(bf16[256,1024]{1,0:T(8,128)(2,1)S(1)} %collective-permute-done.b_ref), channel_id=1, source_target_pairs={{0,4},{4,0},{8,12},{12,8},{16,20},{20,16},{24,28},{28,24},{1,5},{5... | collective-permute-start | bytes 1572872 | tf_op jit(solution)/shard_map/ppermute | solution.py:353
  63.7 22.4 %collective-permute-start.8 = (bf16[256,1024]{1,0:T(8,128)(2,1)}, bf16[256,1024]{1,0:T(8,128)(2,1)}, u32[]{:S(2)}, u32[]{:S(2)}) collective-permute-start(bf16[256,1024]{1,0:T(8,128)(2,1)} %collective-permute-done.4.d_ref), channel_id=1, source_target_pairs={{0,4},{4,0},{8,12},{12,8},{16,20},{20,16},{24,28},{28,24},{1,5},{5... | collective-permute-start | bytes 1572872 | tf_op jit(solution)/shard_map/ppermute | solution.py:353
  64.1 21.0 %collective-permute-start.9 = (bf16[768,128]{1,0:T(8,128)(2,1)}, bf16[768,128]{1,0:T(8,128)(2,1)}, u32[]{:S(2)}, u32[]{:S(2)}) collective-permute-start(bf16[768,128]{1,0:T(8,128)(2,1)} %pad_maximum_fusion.8), channel_id=1, source_target_pairs={{0,8},{4,12},{8,0},{12,4},{16,24},{20,28},{24,16},{28,20},{1,9},{5... | collective-permute-start | bytes 589832 | tf_op jit(solution)/shard_map/ppermute | solution.py:353
  86.1 25.3 %collective-permute-start.11 = (bf16[768,128]{1,0:T(8,128)(2,1)}, bf16[768,128]{1,0:T(8,128)(2,1)S(1)}, u32[]{:S(2)}, u32[]{:S(2)}) collective-permute-start(bf16[768,128]{1,0:T(8,128)(2,1)} %collective-permute-done.10), channel_id=1, source_target_pairs={{0,8},{4,12},{8,0},{12,4},{16,24},{20,28},{24,16},{28,20},{1,9},{5... | collective-permute-start | bytes 589832 | tf_op jit(solution)/shard_map/ppermute | solution.py:353
  112.1 25.7 %all-to-all-start.2 = ((bf16[8,256,128]{2,1,0:T(8,128)(2,1)}), bf16[8,256,128]{2,1,0:T(8,128)(2,1)S(1)}, u32[]{:S(2)}, u32[]{:S(2)}) async-start(bf16[8,256,128]{2,1,0:T(8,128)(2,1)} %bitcast.15), calls=%async_computation.2 | async-start | bytes 1048576 | tf_op jit(solution)/shard_map/all_to_all | solution.py:357
  180.7 40.4 %collective-permute-start.16 = (bf16[8,768,128]{2,1,0:T(8,128)(2,1)}, bf16[8,768,128]{2,1,0:T(8,128)(2,1)}, u32[]{:S(2)}, u32[]{:S(2)}) collective-permute-start(bf16[8,768,128]{2,1,0:T(8,128)(2,1)} %get-tuple-element.137), channel_id=1, source_target_pairs={{0,2},{1,3},{2,0},{3,1},{4,6},{5,7},{6,4},{7,5},{8,10},{9,11},{10,... | collective-permute-start | bytes 4718600 | tf_op jit(solution)/shard_map/ppermute | solution.py:353
  181.2 34.9 %collective-permute-start.17 = (bf16[2,4,512,128]{3,2,1,0:T(8,128)(2,1)}, bf16[2,4,512,128]{3,2,1,0:T(8,128)(2,1)}, u32[]{:S(2)}, u32[]{:S(2)}) collective-permute-start(bf16[2,4,512,128]{3,2,1,0:T(8,128)(2,1)} %get-tuple-element.138), channel_id=1, source_target_pairs={{0,4},{4,0},{8,12},{12,8},{16,20},{20,16},{24,28},{28,24},{1,5},{5... | collective-permute-start | bytes 3145736 | tf_op jit(solution)/shard_map/ppermute | solution.py:353
  210.0 42.6 %all-to-all-start.4 = ((bf16[8,256,384]{2,1,0:T(8,128)(2,1)}), bf16[8,256,384]{2,1,0:T(8,128)(2,1)}, u32[]{:S(2)}, u32[]{:S(2)}) async-start(bf16[8,256,384]{2,1,0:T(8,128)(2,1)} %bitcast.118), calls=%async_computation.4 | async-start | bytes 3145728 | tf_op jit(solution)/shard_map/all_to_all | solution.py:357
  218.1 33.7 %collective-permute-start.20 = (bf16[12,768,128]{2,1,0:T(8,128)(2,1)S(1)}, bf16[12,768,128]{2,1,0:T(8,128)(2,1)}, u32[]{:S(2)}, u32[]{:S(2)}) collective-permute-start(bf16[12,768,128]{2,1,0:T(8,128)(2,1)S(1)} %pad_maximum_fusion.refs_0_), channel_id=1, source_target_pairs={{0,1},{1,0},{2,3},{3,2},{4,5},{5,4},{6,7},{7,6},{8,9},{9,8},{10,11... | collective-permute-start | bytes 7077896 | tf_op jit(solution)/shard_map/ppermute | solution.py:353
  220.4 31.4 %collective-permute-start.19 = (bf16[4,512,128]{2,1,0:T(8,128)(2,1)}, bf16[4,512,128]{2,1,0:T(8,128)(2,1)S(1)}, u32[]{:S(2)}, u32[]{:S(2)}) collective-permute-start(bf16[4,512,128]{2,1,0:T(8,128)(2,1)} %fusion.7), channel_id=1, source_target_pairs={{0,2},{1,3},{2,0},{3,1},{4,6},{5,7},{6,4},{7,5},{8,10},{9,11},{10,... | collective-permute-start | bytes 1572872 | tf_op jit(solution)/shard_map/ppermute | solution.py:353
  223.5 28.3 %collective-permute-start.18 = (bf16[4,768,128]{2,1,0:T(8,128)(2,1)}, bf16[4,768,128]{2,1,0:T(8,128)(2,1)}, u32[]{:S(2)}, u32[]{:S(2)}) collective-permute-start(bf16[4,768,128]{2,1,0:T(8,128)(2,1)} %add_convert_fusion.1), channel_id=1, source_target_pairs={{0,4},{4,0},{8,12},{12,8},{16,20},{20,16},{24,28},{28,24},{1,5},{5... | collective-permute-start | bytes 2359304 | tf_op jit(solution)/shard_map/ppermute | solution.py:353
  223.8 27.3 %collective-permute-start.21 = (bf16[4,768,128]{2,1,0:T(8,128)(2,1)}, bf16[4,768,128]{2,1,0:T(8,128)(2,1)S(1)}, u32[]{:S(2)}, u32[]{:S(2)}) collective-permute-start(bf16[4,768,128]{2,1,0:T(8,128)(2,1)} %copy-done.27), channel_id=1, source_target_pairs={{0,2},{1,3},{2,0},{3,1},{4,6},{5,7},{6,4},{7,5},{8,10},{9,11},{10,... | collective-permute-start | bytes 2359304 | tf_op jit(solution)/shard_map/ppermute | solution.py:353
  256.5 26.4 %collective-permute-start.27 = (bf16[2,256,384]{2,1,0:T(8,128)(2,1)S(1)}, bf16[2,256,384]{2,1,0:T(8,128)(2,1)S(1)}, u32[]{:S(2)}, u32[]{:S(2)}) collective-permute-start(bf16[2,256,384]{2,1,0:T(8,128)(2,1)S(1)} %dynamic-slice_bitcast_fusion), channel_id=1, source_target_pairs={{0,1},{1,0},{2,3},{3,2},{4,5},{5,4},{6,7},{7,6},{8,9},{9,8},{10,11... | collective-permute-start | bytes 1179656 | tf_op jit(solution)/shard_map/ppermute | solution.py:353
  260.4 24.7 %collective-permute-start.29 = (bf16[1280,128]{1,0:T(8,128)(2,1)S(1)}, bf16[1280,128]{1,0:T(8,128)(2,1)S(1)}, u32[]{:S(2)}, u32[]{:S(2)}) collective-permute-start(bf16[1280,128]{1,0:T(8,128)(2,1)S(1)} %get-tuple-element.171), channel_id=1, source_target_pairs={{0,8},{4,12},{8,0},{12,4},{16,24},{20,28},{24,16},{28,20},{1,9},{5... | collective-permute-start | bytes 983048 | tf_op jit(solution)/shard_map/ppermute | solution.py:353
  272.1 23.0 %collective-permute-start.30 = (bf16[1280,128]{1,0:T(8,128)(2,1)S(1)}, bf16[1280,128]{1,0:T(8,128)(2,1)S(1)}, u32[]{:S(2)}, u32[]{:S(2)}) collective-permute-start(bf16[1280,128]{1,0:T(8,128)(2,1)S(1)} %get-tuple-element.170), channel_id=1, source_target_pairs={{0,16},{4,20},{8,24},{12,28},{16,0},{20,4},{24,8},{28,12},{1,17},{... | collective-permute-start | bytes 983048 | tf_op jit(solution)/shard_map/ppermute | solution.py:353
  274.6 29.3 %collective-permute-start.31 = (bf16[1280,128]{1,0:T(8,128)(2,1)S(1)}, bf16[1280,128]{1,0:T(8,128)(2,1)S(1)}, u32[]{:S(2)}, u32[]{:S(2)}) collective-permute-start(bf16[1280,128]{1,0:T(8,128)(2,1)S(1)} %get-tuple-element.169), channel_id=1, source_target_pairs={{0,24},{4,28},{8,16},{12,20},{16,8},{20,12},{24,0},{28,4},{1,25},{... | collective-permute-start | bytes 983048 | tf_op jit(solution)/shard_map/ppermute | solution.py:353
  283.1 20.9 %collective-permute-start.28 = (bf16[256,384]{1,0:T(8,128)(2,1)S(1)}, bf16[256,384]{1,0:T(8,128)(2,1)S(1)}, u32[]{:S(2)}, u32[]{:S(2)}) collective-permute-start(bf16[256,384]{1,0:T(8,128)(2,1)S(1)} %dynamic-slice_bitcast_fusion.1), channel_id=1, source_target_pairs={{0,2},{1,3},{2,0},{3,1},{4,6},{5,7},{6,4},{7,5},{8,10},{9,11},{10,... | collective-permute-start | bytes 589832 | tf_op jit(solution)/shard_map/ppermute | solution.py:353
  (60 other events, 619.9 us)
Sparse Core Ops, SparseCore 0:
  33.6 105.3 all-gather.3

commit v2 on v1

--- a/solution.py
+++ b/solution.py
@@ -1095,15 +1095,9 @@
     )
     late, own = together(late, own)
     grad_emb = jnp.concatenate([late, grad_emb], axis=1)
-    grad_emb = grad_emb.reshape(CLIPS, 4, 2, -1).transpose(2, 1, 0, 3)
-    keep_e = lax.dynamic_index_in_dim(grad_emb, y, 0, False)
-    other_e = swap(lax.dynamic_index_in_dim(grad_emb, 1 - y, 0, False), "seq", 1)
+    grad_emb = exchange(grad_emb.reshape(CLIPS, SEQ, -1).transpose(1, 0, 2))
+    grad_emb = jnp.sum(grad_emb, axis=0)
     x_place, core_place = replica // 2, replica % 2
-    grad_emb = keep_e + other_e
-    from_z_e = [
-        swap(lax.dynamic_index_in_dim(grad_emb, z ^ k, 0, False), "seq", 2 * k) for k in range(1, 4)
-    ]
-    grad_emb = plus(lax.dynamic_index_in_dim(grad_emb, z, 0, False), *from_z_e)
     keep_h = lax.dynamic_index_in_dim(grad_heads_w, core_place, 1, False)
     other_h = swap(lax.dynamic_index_in_dim(grad_heads_w, 1 - core_place, 1, False), "batch", 1)
     h_yx_core = swap(after(h_yx, part), "batch", 1)

time: 315 us -> 311 us (0.987)
  waiting for transfers between devices: 75.1 us -> 68.3 us
    ppermute x32 -> x28, waiting for transfers between devices: 53.3 us -> 46.5 us  [swap(): return lax.ppermute(part, axis, [(i, i ^ distance) for i in range(size)])]
    ppermute x32 -> x28, starting transfers between devices: 32.1 us -> 25.8 us  [swap(): return lax.ppermute(part, axis, [(i, i ^ distance) for i in range(size)])]
    all_to_all x4 -> x5, starting transfers between devices: 21.5 us -> 27.8 us  [exchange(): return lax.all_to_all(blocks, 'seq', 0, 0, tiled=True)]
    all_to_all x4 -> x5, waiting for transfers between devices: 18.5 us -> 18.6 us  [exchange(): return lax.all_to_all(blocks, 'seq', 0, 0, tiled=True)]
  transfers between devices with their start and end apart: 38 -> 35, of which waited for: 10 -> 9; matrix products, arithmetic and copies ran while one was open for 13% -> 13% of each run, Pallas kernels for 33% -> 33%
where the time goes in v2:
time: 311 us; the launch traced here: 309 us
  Pallas kernels  103 us (33%)
  waiting for transfers between devices  68.3 us (22%)
  starting transfers between devices  58.1 us (19%)
  other arithmetic  23.9 us (8%)
  local copies, waits for them, and re-layouts  16.2 us (5%)
  between operations  15.6 us (5%)
  blocking collectives  13.9 us (4%)
  matrix products  9.64 us (3%)
    ppermute x28, waiting for transfers between devices, swap(): return lax.ppermute(part, axis, [(i, i ^ distance) for i in range(size)])  46.5 us
    pallas_call x1, Pallas kernels, attend_back(): pl.pallas_call(attend_back_kernel, grid=(frames // ROWS,), in_specs=[rows...  28.5 us
    all_to_all x5, starting transfers between devices, exchange(): return lax.all_to_all(blocks, 'seq', 0, 0, tiled=True)  27.8 us
    ppermute x28, starting transfers between devices, swap(): return lax.ppermute(part, axis, [(i, i ^ distance) for i in range(size)])  25.8 us
    pallas_call x1, Pallas kernels, middle_part(): pl.pallas_call(middle_kernel, in_specs=[vmem] * 4 + [anywhere] * 3, out_s...  19.3 us
    all_to_all x5, waiting for transfers between devices, exchange(): return lax.all_to_all(blocks, 'seq', 0, 0, tiled=True)  18.6 us
    pallas_call x1, Pallas kernels, attend(): pl.pallas_call(attend_kernel, grid=(frames // BLOCK,), in_specs=[block_sp...  16.1 us
    pallas_call x2, Pallas kernels, project(): pl.pallas_call(project_kernel, grid_spec=pltpu.PrefetchScalarGridSpec(num...  12.7 us
  transfers between devices with their start and end apart: 35, of which 9 were waited for; matrix products, arithmetic and copies ran while one was open for 13% of the time, Pallas kernels for 33%

profile of v2, /device:TPU:13, one launch (start us, length us, event | category | flops | bytes accessed | tf_op | source)
XLA Modules:
  0.0 308.9 jit_solution(17968540881130995670)
XLA Ops:
  12.6 5.4 %all-reduce.1 = s32[64]{0:T(128)S(1)} all-reduce(s32[64]{0:T(128)S(1)} %bitcast_dynamic-update-slice_fusion), channel_id=2, replica_groups=mesh['seq'=8,'batch'=4] {'batch'}, use_global_device_ids=true, to_apply=%add.1 | all-reduce | flops 64 | bytes 512
  20.7 4.5 %all-to-all-start = ((f32[4,16,768]{2,1,0:T(8,128)}), f32[4,16,768]{2,1,0:T(8,128)S(1)}, u32[]{:S(2)}, u32[]{:S(2)}) async-start(f32[4,16,768]{2,1,0:T(8,128)} %bitcast.5), calls=%async_computation | async-start | bytes 393216 | tf_op jit(solution)/shard_map/all_to_all | solution.py:997
  33.5 4.4 %all-to-all-start.1 = ((f32[8,24,768]{2,1,0:T(8,128)}), f32[8,24,768]{2,1,0:T(8,128)}, u32[]{:S(2)}, u32[]{:S(2)}) async-start(f32[8,24,768]{2,1,0:T(8,128)} %broadcast_in_dim.16), calls=%async_computation.1 | async-start | bytes 1179648 | tf_op jit(solution)/shard_map/all_to_all | solution.py:357
  45.5 18.3 %collective-permute-done.4.d_ref = bf16[256,1024]{1,0:T(8,128)(2,1)} collective-permute-done((bf16[256,1024]{1,0:T(8,128)(2,1)S(1)}, bf16[256,1024]{1,0:T(8,128)(2,1)}, u32[]{:S(2)}, u32[]{:S(2)}) %collective-permute-start.4) | collective-permute-done | bytes 524320 | tf_op jit(solution)/shard_map/ppermute | solution.py:353
  72.4 3.7 %multiply_sine_fusion = (f32[2048,128]{1,0:T(8,128)S(1)}, f32[2048,128]{1,0:T(8,128)S(1)}) fusion(f32[128]{0:T(128)S(1)} %mul.62, f32[2048]{0:T(1024)S(1)} %bitcast.110), kind=kLoop, calls=%fused_computation.13 | loop fusion | flops 262144 | bytes 2105856 | tf_op jit(solution)/shard_map/sin | solution.py:1032
  78.8 6.3 %project.2 = (bf16[2048,1024]{1,0:T(8,128)(2,1)S(1)}, bf16[2048,1024]{1,0:T(8,128)(2,1)S(1)}, bf16[2048,128]{1,0:T(8,128)(2,1)S(1)}, bf16[2048,256]{1,0:T(8,128)...) custom-call(s32[2]{0:T(128)S(1)} %pad_add_fusion.place_ref, ...), custom_call_target="tpu_custom_call" | custom-call | flops 2000000000 | bytes 6000000 | tf_op jit(solution)/shard_map/project/pallas_call | solution.py:449
  87.2 6.4 %project.3 = (bf16[2048,1024]{1,0:T(8,128)(2,1)S(1)}, bf16[2048,1024]{1,0:T(8,128)(2,1)S(1)}, bf16[2048,128]{1,0:T(8,128)(2,1)S(1)}, bf16[2048,256]{1,0:T(8,128)...) custom-call(s32[2]{0:T(128)S(1)} %pad_add_fusion.place_ref, ...), custom_call_target="tpu_custom_call", output_to_operand_aliasing={{0}: (11, {}), {1}: (12, {}), {2}: (13, {}), {3}: (14, {}),... | custom-call | flops 2000000000 | bytes 6000000 | tf_op jit(solution)/shard_map/project/pallas_call | solution.py:449
  93.7 16.1 %attend.1 = (f32[2048,128]{1,0:T(8,128)S(1)}, bf16[2048,128]{1,0:T(8,128)(2,1)}, f32[8,2048]{1,0:T(8,128)S(1)}) custom-call(bf16[2048,128]{1,0:T(8,128)(2,1)S(1)} %get-tuple-element.116.q_ref, bf16[2048,128]{1,0:T(8,128)(2,1)S(1)} %and_convert_fusion.member_ref, bf16[2048,256]{1,0:T(8,128)(2,1)S(1)} %get-tuple-element.117.k_ref, ...), custom_call_target="tpu_custom_call" | custom-call | flops 17999998976 | bytes 54000000 | tf_op jit(solution)/shard_map/attend/pallas_call | solution.py:512
  112.2 5.2 %all-to-all-start.2 = ((bf16[8,256,128]{2,1,0:T(8,128)(2,1)}), bf16[8,256,128]{2,1,0:T(8,128)(2,1)S(1)}, u32[]{:S(2)}, u32[]{:S(2)}) async-start(bf16[8,256,128]{2,1,0:T(8,128)(2,1)} %bitcast.15), calls=%async_computation.2 | async-start | bytes 1048576 | tf_op jit(solution)/shard_map/all_to_all | solution.py:357
  119.4 18.6 %all-to-all-done.2.mine_ref = bf16[8,256,128]{2,1,0:T(8,128)(2,1)S(1)} async-done(((bf16[8,256,128]{2,1,0:T(8,128)(2,1)}), bf16[8,256,128]{2,1,0:T(8,128)(2,1)S(1)}, u32[]{:S(2)}, u32[]{:S(2)}) %all-to-all-start.2) | async-done | bytes 524320 | tf_op jit(solution)/shard_map/all_to_all | solution.py:357
  139.2 19.3 %middle.1 = (bf16[256,1024]{1,0:T(8,128)(2,1)}, f32[256,1024]{1,0:T(8,128)}, bf16[8,256,128]{2,1,0:T(8,128)(2,1)}, f32[16,4096]{1,0:T(8,128)}, bf16[4096,256]{1,0:T(8,128)(2,1)}, /*index=5*/bf16[256,4096]{1,0:T(8,128)(2,1)}) custom-call(bf16[8,256,128]{2,1,0:T(8,128)(2,1)} %copy-done.36, bf16[256,1024]{1,0:T(8,128)(2,1)} %bitcast.96, ...), custom_call_target="tpu_custom_call" | custom-call | flops 20000000000 | bytes 60000000 | tf_op jit(solution)/shard_map/middle/pallas_call | solution.py:786
  158.6 4.0 %collective-permute-start.14 = (bf16[4096,256]{1,0:T(8,128)(2,1)}, bf16[4096,256]{1,0:T(8,128)(2,1)}, u32[]{:S(2)}, u32[]{:S(2)}) collective-permute-start(bf16[4096,256]{1,0:T(8,128)(2,1)} %get-tuple-element.131.down_l.up_l.out_l), channel_id=1, source_target_pairs={{0,1},{1,0},{2,3},{3,2},{4,5},{5,4},{6,7},{7,6},{8,9},{9,8},{10,11... | collective-permute-start | bytes 6291464 | tf_op jit(solution)/shard_map/ppermute | solution.py:353
  163.2 5.9 %all-to-all-start.3 = ((bf16[8,256,128]{2,1,0:T(8,128)(2,1)}), bf16[8,256,128]{2,1,0:T(8,128)(2,1)}, u32[]{:S(2)}, u32[]{:S(2)}) async-start(bf16[8,256,128]{2,1,0:T(8,128)(2,1)} %get-tuple-element.128), calls=%async_computation.3 | async-start | bytes 1048576 | tf_op jit(solution)/shard_map/all_to_all | solution.py:357
  170.8 10.0 %weight_grads.1 = (bf16[8,768,128]{2,1,0:T(8,128)(2,1)}, bf16[8,768,128]{2,1,0:T(8,128)(2,1)}, bf16[2,4,512,128]{3,2,1,0:T(8,128)(2,1)}, bf16[2,4,512,128]{3,2,1,0:T(8,128)(2,1)}) custom-call(s32[3]{0:T(128)} %pad_add_fusion.1.place_ref, bf16[4096,256]{1,0:T(8,128)(2,1)} %get-tuple-element.131.down_l.up_l.out_l, ...), custom_call_target="tpu_custom_call" | custom-call | flops 8999999488 | bytes 27000000 | tf_op jit(solution)/shard_map/weight_grads/pallas_call | solution.py:861
  181.6 28.5 %attend_back.1.g_ref = bf16[2048,384]{1,0:T(8,128)(2,1)} custom-call(bf16[2048,128]{1,0:T(8,128)(2,1)} %copy-done.9, bf16[2048,128]{1,0:T(8,128)(2,1)} %copy-done.5, bf16[2048,128]{1,0:T(8,128)(2,1)} %bitcast.25.grad_ref, f32[2048,128]{1,0:T(8,128)} %copy-done.22, f32[8,2048]{1,0:T(8,128)} %copy-done.23, f32[2048,128]{1,0:T(8,128)} %copy-done.3, ...), custom_call_target="tpu_custom_call" | custom-call | flops 27000000512 | bytes 81000000 | tf_op jit(solution)/shard_map/attend_back/pallas_call | solution.py:579
  210.1 6.1 %all-to-all-start.4 = ((bf16[8,256,384]{2,1,0:T(8,128)(2,1)}), bf16[8,256,384]{2,1,0:T(8,128)(2,1)}, u32[]{:S(2)}, u32[]{:S(2)}) async-start(bf16[8,256,384]{2,1,0:T(8,128)(2,1)} %bitcast.99), calls=%async_computation.4 | async-start | bytes 3145728 | tf_op jit(solution)/shard_map/all_to_all | solution.py:357
  224.7 10.9 %clip_grads.1 = f32[16,2048]{1,0:T(8,128)} custom-call(s32[2]{0:T(128)} %copy-done.19, bf16[2048,1024]{1,0:T(8,128)(2,1)} %copy-done.6, s32[1,2048]{1,0:T(1,128)} %and_select_fusion.clip_ref, bf16[2048,384]{1,0:T(8,128)(2,1)} %attend_back.1.g_ref, bf16[4,256,384]{2,1,0:T(8,128)(2,1)} %copy-done.4), custom_call_target="tpu_custom_call" | custom-call | flops 8999999488 | bytes 27000000 | tf_op jit(solution)/shard_map/clip_grads/pallas_call | solution.py:892
  235.6 6.0 %convolution_convert_fusion = bf16[1024,384]{1,0:T(8,128)(2,1)} fusion(bf16[2048,1024]{1,0:T(8,128)(2,1)} %copy-done.7, bf16[2048,384]{1,0:T(8,128)(2,1)} %attend_back.1.g_ref), kind=kOutput, calls=%fused_computation.15 | convolution fusion | flops 1611005952 | bytes 6553600 | tf_op jit(solution)/shard_map/dot_general | solution.py:29
  241.6 9.6 %collective-permute-done.21.refs_1_ = bf16[4,768,128]{2,1,0:T(8,128)(2,1)S(1)} collective-permute-done((bf16[4,768,128]{2,1,0:T(8,128)(2,1)}, bf16[4,768,128]{2,1,0:T(8,128)(2,1)S(1)}, u32[]{:S(2)}, u32[]{:S(2)}) %collective-permute-start.21) | collective-permute-done | bytes 786464 | tf_op jit(solution)/shard_map/ppermute | solution.py:353
  253.5 6.3 %all-to-all-start.5 = ((f32[8,16,768]{2,1,0:T(8,128)}), f32[8,16,768]{2,1,0:T(8,128)S(1)}, u32[]{:S(2)}, u32[]{:S(2)}) async-start(f32[8,16,768]{2,1,0:T(8,128)} %bitcast.100), calls=%async_computation.5 | async-start | bytes 786432 | tf_op jit(solution)/shard_map/all_to_all | solution.py:357
  269.5 5.5 %last.1 = bf16[256,1024]{1,0:T(8,128)(2,1)} custom-call(s32[3]{0:T(128)S(1)} %copy-done.20, bf16[8,256,384]{2,1,0:T(8,128)(2,1)} %all-to-all-done.4.own_ref, bf16[256,1024]{1,0:T(8,128)(2,1)S(1)} %bitcast.98, f32[256,1024]{1,0:T(8,128)S(1)} %copy-done.21, bf16[256,128]{1,0:T(8,128)(2,1)S(1)} %copy-done.18, bf16[128,6144]{1,0:T(8,128)(2,1)S(1)} %copy-done.1, ...), custom_call_target="tpu_custom_call" | custom-call | flops 4000000000 | bytes 12000000 | tf_op jit(solution)/shard_map/last/pallas_call | solution.py:941
  275.8 8.6 %all_gather.15 = f32[64,768]{1,0:T(8,128)S(1)} all-gather(f32[16,768]{1,0:T(8,128)S(1)} %reduce_sum.39), channel_id=1, replica_groups=mesh['seq'=8,'batch'=4] {'batch'}, dimensions={0}, use_global_device_ids=true | all-gather | bytes 245760 | tf_op jit(solution)/shard_map/all_gather | solution.py:1111
  285.7 4.5 %collective-permute-done.26 = bf16[1280,128]{1,0:T(8,128)(2,1)} collective-permute-done((bf16[1280,128]{1,0:T(8,128)(2,1)}, bf16[1280,128]{1,0:T(8,128)(2,1)}, u32[]{:S(2)}, u32[]{:S(2)}) %collective-permute-start.26) | collective-permute-done | bytes 327712 | tf_op jit(solution)/shard_map/ppermute | solution.py:353
  290.2 8.1 %collective-permute-done.27 = bf16[1280,128]{1,0:T(8,128)(2,1)} collective-permute-done((bf16[1280,128]{1,0:T(8,128)(2,1)}, bf16[1280,128]{1,0:T(8,128)(2,1)}, u32[]{:S(2)}, u32[]{:S(2)}) %collective-permute-start.27) | collective-permute-done | bytes 327712 | tf_op jit(solution)/shard_map/ppermute | solution.py:353
  (235 shorter events, 71.2 us)
Async XLA Ops:
  7.2 23.3 %collective-permute-start = (bf16[256,1024]{1,0:T(8,128)(2,1)}, bf16[256,1024]{1,0:T(8,128)(2,1)S(1)}, u32[]{:S(2)}, u32[]{:S(2)}) collective-permute-start(bf16[256,1024]{1,0:T(8,128)(2,1)} %bitcast.93), channel_id=1, source_target_pairs={{0,8},{4,12},{8,0},{12,4},{16,24},{20,28},{24,16},{28,20},{1,9},{5... | collective-permute-start | bytes 1572872 | tf_op jit(solution)/shard_map/ppermute | solution.py:353
  7.4 25.1 %collective-permute-start.1 = (bf16[256,1024]{1,0:T(8,128)(2,1)}, bf16[256,1024]{1,0:T(8,128)(2,1)S(1)}, u32[]{:S(2)}, u32[]{:S(2)}) collective-permute-start(bf16[256,1024]{1,0:T(8,128)(2,1)} %bitcast.94), channel_id=1, source_target_pairs={{0,16},{4,20},{8,24},{12,28},{16,0},{20,4},{24,8},{28,12},{1,17},{... | collective-permute-start | bytes 1572872 | tf_op jit(solution)/shard_map/ppermute | solution.py:353
  9.8 22.8 %collective-permute-start.2 = (bf16[256,1024]{1,0:T(8,128)(2,1)}, bf16[256,1024]{1,0:T(8,128)(2,1)S(1)}, u32[]{:S(2)}, u32[]{:S(2)}) collective-permute-start(bf16[256,1024]{1,0:T(8,128)(2,1)} %bitcast.95), channel_id=1, source_target_pairs={{0,4},{4,0},{8,12},{12,8},{16,20},{20,16},{24,28},{28,24},{1,5},{5... | collective-permute-start | bytes 1572872 | tf_op jit(solution)/shard_map/ppermute | solution.py:353
  25.2 114.0 %all-gather.4.cloned.1.call-start = ((), (), s32[]{:S(2)}) async-start(), calls=%async_computation.6 | async-start | bytes 10813440 | tf_op jit(solution)/shard_map/all_gather | solution.py:1007
  33.5 35.8 %all-to-all-start.1 = ((f32[8,24,768]{2,1,0:T(8,128)}), f32[8,24,768]{2,1,0:T(8,128)}, u32[]{:S(2)}, u32[]{:S(2)}) async-start(f32[8,24,768]{2,1,0:T(8,128)} %broadcast_in_dim.16), calls=%async_computation.1 | async-start | bytes 1179648 | tf_op jit(solution)/shard_map/all_to_all | solution.py:357
  37.9 25.8 %collective-permute-start.4 = (bf16[256,1024]{1,0:T(8,128)(2,1)S(1)}, bf16[256,1024]{1,0:T(8,128)(2,1)}, u32[]{:S(2)}, u32[]{:S(2)}) collective-permute-start(bf16[256,1024]{1,0:T(8,128)(2,1)S(1)} %collective-permute-done.1.c_ref), channel_id=1, source_target_pairs={{0,8},{4,12},{8,0},{12,4},{16,24},{20,28},{24,16},{28,20},{1,9},{5... | collective-permute-start | bytes 1572872 | tf_op jit(solution)/shard_map/ppermute | solution.py:353
  40.0 36.1 %collective-permute-start.7 = (bf16[256,1024]{1,0:T(8,128)(2,1)S(1)}, bf16[256,1024]{1,0:T(8,128)(2,1)S(1)}, u32[]{:S(2)}, u32[]{:S(2)}) collective-permute-start(bf16[256,1024]{1,0:T(8,128)(2,1)S(1)} %collective-permute-done.1.c_ref), channel_id=1, source_target_pairs={{0,4},{4,0},{8,12},{12,8},{16,20},{20,16},{24,28},{28,24},{1,5},{5... | collective-permute-start | bytes 1572872 | tf_op jit(solution)/shard_map/ppermute | solution.py:353
  40.2 35.9 %collective-permute-start.6 = (bf16[256,1024]{1,0:T(8,128)(2,1)S(1)}, bf16[256,1024]{1,0:T(8,128)(2,1)S(1)}, u32[]{:S(2)}, u32[]{:S(2)}) collective-permute-start(bf16[256,1024]{1,0:T(8,128)(2,1)S(1)} %collective-permute-done.b_ref), channel_id=1, source_target_pairs={{0,4},{4,0},{8,12},{12,8},{16,20},{20,16},{24,28},{28,24},{1,5},{5... | collective-permute-start | bytes 1572872 | tf_op jit(solution)/shard_map/ppermute | solution.py:353
  63.7 22.4 %collective-permute-start.8 = (bf16[256,1024]{1,0:T(8,128)(2,1)}, bf16[256,1024]{1,0:T(8,128)(2,1)}, u32[]{:S(2)}, u32[]{:S(2)}) collective-permute-start(bf16[256,1024]{1,0:T(8,128)(2,1)} %collective-permute-done.4.d_ref), channel_id=1, source_target_pairs={{0,4},{4,0},{8,12},{12,8},{16,20},{20,16},{24,28},{28,24},{1,5},{5... | collective-permute-start | bytes 1572872 | tf_op jit(solution)/shard_map/ppermute | solution.py:353
  64.1 21.0 %collective-permute-start.9 = (bf16[768,128]{1,0:T(8,128)(2,1)}, bf16[768,128]{1,0:T(8,128)(2,1)}, u32[]{:S(2)}, u32[]{:S(2)}) collective-permute-start(bf16[768,128]{1,0:T(8,128)(2,1)} %pad_maximum_fusion.8), channel_id=1, source_target_pairs={{0,8},{4,12},{8,0},{12,4},{16,24},{20,28},{24,16},{28,20},{1,9},{5... | collective-permute-start | bytes 589832 | tf_op jit(solution)/shard_map/ppermute | solution.py:353
  86.1 25.4 %collective-permute-start.11 = (bf16[768,128]{1,0:T(8,128)(2,1)}, bf16[768,128]{1,0:T(8,128)(2,1)S(1)}, u32[]{:S(2)}, u32[]{:S(2)}) collective-permute-start(bf16[768,128]{1,0:T(8,128)(2,1)} %collective-permute-done.10), channel_id=1, source_target_pairs={{0,8},{4,12},{8,0},{12,4},{16,24},{20,28},{24,16},{28,20},{1,9},{5... | collective-permute-start | bytes 589832 | tf_op jit(solution)/shard_map/ppermute | solution.py:353
  112.2 25.8 %all-to-all-start.2 = ((bf16[8,256,128]{2,1,0:T(8,128)(2,1)}), bf16[8,256,128]{2,1,0:T(8,128)(2,1)S(1)}, u32[]{:S(2)}, u32[]{:S(2)}) async-start(bf16[8,256,128]{2,1,0:T(8,128)(2,1)} %bitcast.15), calls=%async_computation.2 | async-start | bytes 1048576 | tf_op jit(solution)/shard_map/all_to_all | solution.py:357
  138.0 20.5 %collective-permute-start.13 = (bf16[4,768,128]{2,1,0:T(8,128)(2,1)S(1)}, bf16[4,768,128]{2,1,0:T(8,128)(2,1)S(1)}, u32[]{:S(2)}, u32[]{:S(2)}) collective-permute-start(bf16[4,768,128]{2,1,0:T(8,128)(2,1)S(1)} %pad_maximum_fusion.2), channel_id=1, source_target_pairs={{0,2},{1,3},{2,0},{3,1},{4,6},{5,7},{6,4},{7,5},{8,10},{9,11},{10,... | collective-permute-start | bytes 2359304 | tf_op jit(solution)/shard_map/ppermute | solution.py:353
  180.8 40.4 %collective-permute-start.16 = (bf16[8,768,128]{2,1,0:T(8,128)(2,1)}, bf16[8,768,128]{2,1,0:T(8,128)(2,1)}, u32[]{:S(2)}, u32[]{:S(2)}) collective-permute-start(bf16[8,768,128]{2,1,0:T(8,128)(2,1)} %get-tuple-element.137), channel_id=1, source_target_pairs={{0,2},{1,3},{2,0},{3,1},{4,6},{5,7},{6,4},{7,5},{8,10},{9,11},{10,... | collective-permute-start | bytes 4718600 | tf_op jit(solution)/shard_map/ppermute | solution.py:353
  181.3 34.9 %collective-permute-start.17 = (bf16[2,4,512,128]{3,2,1,0:T(8,128)(2,1)}, bf16[2,4,512,128]{3,2,1,0:T(8,128)(2,1)}, u32[]{:S(2)}, u32[]{:S(2)}) collective-permute-start(bf16[2,4,512,128]{3,2,1,0:T(8,128)(2,1)} %get-tuple-element.138), channel_id=1, source_target_pairs={{0,4},{4,0},{8,12},{12,8},{16,20},{20,16},{24,28},{28,24},{1,5},{5... | collective-permute-start | bytes 3145736 | tf_op jit(solution)/shard_map/ppermute | solution.py:353
  210.1 42.5 %all-to-all-start.4 = ((bf16[8,256,384]{2,1,0:T(8,128)(2,1)}), bf16[8,256,384]{2,1,0:T(8,128)(2,1)}, u32[]{:S(2)}, u32[]{:S(2)}) async-start(bf16[8,256,384]{2,1,0:T(8,128)(2,1)} %bitcast.99), calls=%async_computation.4 | async-start | bytes 3145728 | tf_op jit(solution)/shard_map/all_to_all | solution.py:357
  218.2 33.7 %collective-permute-start.20 = (bf16[12,768,128]{2,1,0:T(8,128)(2,1)S(1)}, bf16[12,768,128]{2,1,0:T(8,128)(2,1)}, u32[]{:S(2)}, u32[]{:S(2)}) collective-permute-start(bf16[12,768,128]{2,1,0:T(8,128)(2,1)S(1)} %pad_maximum_fusion.refs_0_), channel_id=1, source_target_pairs={{0,1},{1,0},{2,3},{3,2},{4,5},{5,4},{6,7},{7,6},{8,9},{9,8},{10,11... | collective-permute-start | bytes 7077896 | tf_op jit(solution)/shard_map/ppermute | solution.py:353
  220.5 31.4 %collective-permute-start.19 = (bf16[4,512,128]{2,1,0:T(8,128)(2,1)}, bf16[4,512,128]{2,1,0:T(8,128)(2,1)S(1)}, u32[]{:S(2)}, u32[]{:S(2)}) collective-permute-start(bf16[4,512,128]{2,1,0:T(8,128)(2,1)} %fusion.7), channel_id=1, source_target_pairs={{0,2},{1,3},{2,0},{3,1},{4,6},{5,7},{6,4},{7,5},{8,10},{9,11},{10,... | collective-permute-start | bytes 1572872 | tf_op jit(solution)/shard_map/ppermute | solution.py:353
  223.6 28.2 %collective-permute-start.18 = (bf16[4,768,128]{2,1,0:T(8,128)(2,1)}, bf16[4,768,128]{2,1,0:T(8,128)(2,1)}, u32[]{:S(2)}, u32[]{:S(2)}) collective-permute-start(bf16[4,768,128]{2,1,0:T(8,128)(2,1)} %add_convert_fusion.1), channel_id=1, source_target_pairs={{0,4},{4,0},{8,12},{12,8},{16,20},{20,16},{24,28},{28,24},{1,5},{5... | collective-permute-start | bytes 2359304 | tf_op jit(solution)/shard_map/ppermute | solution.py:353
  223.9 27.3 %collective-permute-start.21 = (bf16[4,768,128]{2,1,0:T(8,128)(2,1)}, bf16[4,768,128]{2,1,0:T(8,128)(2,1)S(1)}, u32[]{:S(2)}, u32[]{:S(2)}) collective-permute-start(bf16[4,768,128]{2,1,0:T(8,128)(2,1)} %copy-done.30), channel_id=1, source_target_pairs={{0,2},{1,3},{2,0},{3,1},{4,6},{5,7},{6,4},{7,5},{8,10},{9,11},{10,... | collective-permute-start | bytes 2359304 | tf_op jit(solution)/shard_map/ppermute | solution.py:353
  253.5 22.2 %all-to-all-start.5 = ((f32[8,16,768]{2,1,0:T(8,128)}), f32[8,16,768]{2,1,0:T(8,128)S(1)}, u32[]{:S(2)}, u32[]{:S(2)}) async-start(f32[8,16,768]{2,1,0:T(8,128)} %bitcast.100), calls=%async_computation.5 | async-start | bytes 786432 | tf_op jit(solution)/shard_map/all_to_all | solution.py:357
  267.1 23.2 %collective-permute-start.26 = (bf16[1280,128]{1,0:T(8,128)(2,1)}, bf16[1280,128]{1,0:T(8,128)(2,1)}, u32[]{:S(2)}, u32[]{:S(2)}) collective-permute-start(bf16[1280,128]{1,0:T(8,128)(2,1)} %get-tuple-element.170), channel_id=1, source_target_pairs={{0,16},{4,20},{8,24},{12,28},{16,0},{20,4},{24,8},{28,12},{1,17},{... | collective-permute-start | bytes 983048 | tf_op jit(solution)/shard_map/ppermute | solution.py:353
  269.2 29.2 %collective-permute-start.27 = (bf16[1280,128]{1,0:T(8,128)(2,1)}, bf16[1280,128]{1,0:T(8,128)(2,1)}, u32[]{:S(2)}, u32[]{:S(2)}) collective-permute-start(bf16[1280,128]{1,0:T(8,128)(2,1)} %get-tuple-element.169), channel_id=1, source_target_pairs={{0,24},{4,28},{8,16},{12,20},{16,8},{20,12},{24,0},{28,4},{1,25},{... | collective-permute-start | bytes 983048 | tf_op jit(solution)/shard_map/ppermute | solution.py:353
  275.2 23.2 %collective-permute-start.24 = (bf16[256,384]{1,0:T(8,128)(2,1)S(1)}, bf16[256,384]{1,0:T(8,128)(2,1)S(1)}, u32[]{:S(2)}, u32[]{:S(2)}) collective-permute-start(bf16[256,384]{1,0:T(8,128)(2,1)S(1)} %dynamic-slice_bitcast_fusion.1), channel_id=1, source_target_pairs={{0,2},{1,3},{2,0},{3,1},{4,6},{5,7},{6,4},{7,5},{8,10},{9,11},{10,... | collective-permute-start | bytes 589832 | tf_op jit(solution)/shard_map/ppermute | solution.py:353
  (59 other events, 629.6 us)
Sparse Core Ops, SparseCore 0:
  33.6 105.3 all-gather.3

commit v3 on v2

--- a/solution.py
+++ b/solution.py
@@ -1081,21 +1081,17 @@
     h_yx = swap(after(h_y, to_y_d), "batch", 2)
     h_first_core = swap(after(h_first, to_x_u), "batch", 1)
     g_heads = after(g_heads, to_y_d, to_x_u)
-    late = clip_grads(places, x_all, clip_row, g_heads, heads_w)
     grad_heads_w = matmul(attn_input.T, g_heads).astype(low).reshape(2, 2, ROWS, 3 * TWO)
-    late, grad_heads_w, from_y_d, from_x_u, h_first_core = together(
-        late, grad_heads_w, from_y_d, from_x_u, h_first_core
-    )
-    part = jnp.concatenate(
-        [
-            plus(keep_u[0], from_y[0], from_x_u).astype(low),
-            plus(keep_d[:4], from_x[:4], from_y_d).astype(low),
-        ],
-        axis=1,
-    )
+    grad_heads_w, from_x_u = together(grad_heads_w, from_x_u)
+    part_u = plus(keep_u[0], from_y[0], from_x_u).astype(low)
+    from_z_u = [swap(part_u[k], "seq", 2 * k) for k in range(1, 4)]
+    late = clip_grads(places, x_all, clip_row, after(g_heads, part_u), heads_w)
+    late, from_y_d, h_first_core = together(late, from_y_d, h_first_core)
+    part = plus(keep_d[:4], from_x[:4], from_y_d).astype(low)
     late, own = together(late, own)
     grad_emb = jnp.concatenate([late, grad_emb], axis=1)
     grad_emb = exchange(grad_emb.reshape(CLIPS, SEQ, -1).transpose(1, 0, 2))
+    grad_emb, *from_z_u = together(grad_emb, *from_z_u)
     grad_emb = jnp.sum(grad_emb, axis=0)
     x_place, core_place = replica // 2, replica % 2
     keep_h = lax.dynamic_index_in_dim(grad_heads_w, core_place, 1, False)
@@ -1113,8 +1109,9 @@
     grad_tokens, final_a, away_h, *from_z = together(grad_tokens, final_a, away_h, *from_z)
     final_heads = plus(lax.dynamic_index_in_dim(both_h, x_place, 0, False), away_h)
     total = plus(part[0], *from_z)
-    final_u = jnp.concatenate([total[:256], total[256:512]], axis=1)
-    final_d, final_o = total[512:1024], total[1024:]
+    final_d, final_o = total[:512], total[512:]
+    total = plus(part_u[0], *from_z_u)
+    final_u = jnp.concatenate([total[:256], total[256:]], axis=1)
     width = w_query.shape[1]
     return (
         result[None],

time: 311 us -> 307 us (0.987)
  waiting for transfers between devices: 68.3 us -> 52.1 us
  starting transfers between devices: 58.1 us -> 65.9 us
  local copies, waits for them, and re-layouts: 16.2 us -> 19.4 us
    ppermute x28 -> x31, waiting for transfers between devices: 46.5 us -> 30.2 us  [swap(): return lax.ppermute(part, axis, [(i, i ^ distance) for i in range(size)])]
    ppermute x28 -> x31, starting transfers between devices: 25.8 us -> 31.9 us  [swap(): return lax.ppermute(part, axis, [(i, i ^ distance) for i in range(size)])]
    unnamed x105 -> x101, local copies, waits for them, and re-layouts: 9.53 us -> 10 us
  transfers between devices with their start and end apart: 35 -> 38, of which waited for: 9 -> 8; matrix products, arithmetic and copies ran while one was open for 13% -> 14% of each run, Pallas kernels for 33% -> 34%
where the time goes in v3:
time: 307 us; the launch traced here: 304 us
  Pallas kernels  103 us (34%)
  starting transfers between devices  65.9 us (21%)
  waiting for transfers between devices  52.1 us (17%)
  other arithmetic  26.4 us (9%)
  local copies, waits for them, and re-layouts  19.4 us (6%)
  between operations  15.6 us (5%)
  blocking collectives  12.8 us (4%)
  matrix products  8.99 us (3%)
    ppermute x31, starting transfers between devices, swap(): return lax.ppermute(part, axis, [(i, i ^ distance) for i in range(size)])  31.9 us
    ppermute x31, waiting for transfers between devices, swap(): return lax.ppermute(part, axis, [(i, i ^ distance) for i in range(size)])  30.2 us
    all_to_all x5, starting transfers between devices, exchange(): return lax.all_to_all(blocks, 'seq', 0, 0, tiled=True)  29.5 us
    pallas_call x1, Pallas kernels, attend_back(): pl.pallas_call(attend_back_kernel, grid=(frames // ROWS,), in_specs=[rows...  28.5 us
    pallas_call x1, Pallas kernels, middle_part(): pl.pallas_call(middle_kernel, in_specs=[vmem] * 4 + [anywhere] * 3, out_s...  19.3 us
    all_to_all x5, waiting for transfers between devices, exchange(): return lax.all_to_all(blocks, 'seq', 0, 0, tiled=True)  18.6 us
    pallas_call x1, Pallas kernels, attend(): pl.pallas_call(attend_kernel, grid=(frames // BLOCK,), in_specs=[block_sp...  16.1 us
    pallas_call x2, Pallas kernels, project(): pl.pallas_call(project_kernel, grid_spec=pltpu.PrefetchScalarGridSpec(num...  12.7 us
  transfers between devices with their start and end apart: 38, of which 8 were waited for; matrix products, arithmetic and copies ran while one was open for 14% of the time, Pallas kernels for 34%

profile of v3, /device:TPU:13, one launch (start us, length us, event | category | flops | bytes accessed | tf_op | source)
XLA Modules:
  0.0 304.2 jit_solution(16181390962381780368)
XLA Ops:
  12.6 5.4 %all-reduce.1 = s32[64]{0:T(128)S(1)} all-reduce(s32[64]{0:T(128)S(1)} %bitcast_dynamic-update-slice_fusion), channel_id=2, replica_groups=mesh['seq'=8,'batch'=4] {'batch'}, use_global_device_ids=true, to_apply=%add.1 | all-reduce | flops 64 | bytes 512
  20.7 4.5 %all-to-all-start = ((f32[4,16,768]{2,1,0:T(8,128)}), f32[4,16,768]{2,1,0:T(8,128)S(1)}, u32[]{:S(2)}, u32[]{:S(2)}) async-start(f32[4,16,768]{2,1,0:T(8,128)} %bitcast.5), calls=%async_computation | async-start | bytes 393216 | tf_op jit(solution)/shard_map/all_to_all | solution.py:997
  26.5 3.2 %all-to-all-done = f32[4,16,768]{2,1,0:T(8,128)S(1)} async-done(((f32[4,16,768]{2,1,0:T(8,128)}), f32[4,16,768]{2,1,0:T(8,128)S(1)}, u32[]{:S(2)}, u32[]{:S(2)}) %all-to-all-start) | async-done | bytes 196640 | tf_op jit(solution)/shard_map/all_to_all | solution.py:997
  33.5 4.4 %all-to-all-start.1 = ((f32[8,24,768]{2,1,0:T(8,128)}), f32[8,24,768]{2,1,0:T(8,128)}, u32[]{:S(2)}, u32[]{:S(2)}) async-start(f32[8,24,768]{2,1,0:T(8,128)} %broadcast_in_dim.16), calls=%async_computation.1 | async-start | bytes 1179648 | tf_op jit(solution)/shard_map/all_to_all | solution.py:357
  42.5 2.9 collective-permute-done.5
  45.5 18.3 %collective-permute-done.4.d_ref = bf16[256,1024]{1,0:T(8,128)(2,1)} collective-permute-done((bf16[256,1024]{1,0:T(8,128)(2,1)S(1)}, bf16[256,1024]{1,0:T(8,128)(2,1)}, u32[]{:S(2)}, u32[]{:S(2)}) %collective-permute-start.4) | collective-permute-done | bytes 524320 | tf_op jit(solution)/shard_map/ppermute | solution.py:353
  72.4 3.7 %multiply_sine_fusion = (f32[2048,128]{1,0:T(8,128)S(1)}, f32[2048,128]{1,0:T(8,128)S(1)}) fusion(f32[128]{0:T(128)S(1)} %mul.62, f32[2048]{0:T(1024)S(1)} %bitcast.121), kind=kLoop, calls=%fused_computation.4 | loop fusion | flops 262144 | bytes 2105856 | tf_op jit(solution)/shard_map/sin | solution.py:1032
  78.8 6.3 %project.2 = (bf16[2048,1024]{1,0:T(8,128)(2,1)S(1)}, bf16[2048,1024]{1,0:T(8,128)(2,1)S(1)}, bf16[2048,128]{1,0:T(8,128)(2,1)S(1)}, bf16[2048,256]{1,0:T(8,128)...) custom-call(s32[2]{0:T(128)S(1)} %pad_add_fusion.place_ref, ...), custom_call_target="tpu_custom_call" | custom-call | flops 2000000000 | bytes 6000000 | tf_op jit(solution)/shard_map/project/pallas_call | solution.py:449
  87.3 6.4 %project.3 = (bf16[2048,1024]{1,0:T(8,128)(2,1)S(1)}, bf16[2048,1024]{1,0:T(8,128)(2,1)S(1)}, bf16[2048,128]{1,0:T(8,128)(2,1)S(1)}, bf16[2048,256]{1,0:T(8,128)...) custom-call(s32[2]{0:T(128)S(1)} %pad_add_fusion.place_ref, ...), custom_call_target="tpu_custom_call", output_to_operand_aliasing={{0}: (11, {}), {1}: (12, {}), {2}: (13, {}), {3}: (14, {}),... | custom-call | flops 2000000000 | bytes 6000000 | tf_op jit(solution)/shard_map/project/pallas_call | solution.py:449
  93.7 16.1 %attend.1 = (f32[2048,128]{1,0:T(8,128)S(1)}, bf16[2048,128]{1,0:T(8,128)(2,1)}, f32[8,2048]{1,0:T(8,128)S(1)}) custom-call(bf16[2048,128]{1,0:T(8,128)(2,1)S(1)} %get-tuple-element.121.q_ref, bf16[2048,128]{1,0:T(8,128)(2,1)S(1)} %and_convert_fusion.member_ref, bf16[2048,256]{1,0:T(8,128)(2,1)S(1)} %get-tuple-element.122.k_ref, ...), custom_call_target="tpu_custom_call" | custom-call | flops 17999998976 | bytes 54000000 | tf_op jit(solution)/shard_map/attend/pallas_call | solution.py:512
  112.2 5.2 %all-to-all-start.2 = ((bf16[8,256,128]{2,1,0:T(8,128)(2,1)}), bf16[8,256,128]{2,1,0:T(8,128)(2,1)S(1)}, u32[]{:S(2)}, u32[]{:S(2)}) async-start(bf16[8,256,128]{2,1,0:T(8,128)(2,1)} %bitcast.15), calls=%async_computation.2 | async-start | bytes 1048576 | tf_op jit(solution)/shard_map/all_to_all | solution.py:357
  119.4 18.6 %all-to-all-done.2.mine_ref = bf16[8,256,128]{2,1,0:T(8,128)(2,1)S(1)} async-done(((bf16[8,256,128]{2,1,0:T(8,128)(2,1)}), bf16[8,256,128]{2,1,0:T(8,128)(2,1)S(1)}, u32[]{:S(2)}, u32[]{:S(2)}) %all-to-all-start.2) | async-done | bytes 524320 | tf_op jit(solution)/shard_map/all_to_all | solution.py:357
  139.2 19.3 %middle.1 = (bf16[256,1024]{1,0:T(8,128)(2,1)}, f32[256,1024]{1,0:T(8,128)}, bf16[8,256,128]{2,1,0:T(8,128)(2,1)}, f32[16,4096]{1,0:T(8,128)}, bf16[4096,256]{1,0:T(8,128)(2,1)}, /*index=5*/bf16[256,4096]{1,0:T(8,128)(2,1)}) custom-call(bf16[8,256,128]{2,1,0:T(8,128)(2,1)} %copy-done.37, bf16[256,1024]{1,0:T(8,128)(2,1)} %bitcast.107, ...), custom_call_target="tpu_custom_call" | custom-call | flops 20000000000 | bytes 60000000 | tf_op jit(solution)/shard_map/middle/pallas_call | solution.py:786
  158.5 4.0 %collective-permute-start.14 = (bf16[4096,256]{1,0:T(8,128)(2,1)}, bf16[4096,256]{1,0:T(8,128)(2,1)}, u32[]{:S(2)}, u32[]{:S(2)}) collective-permute-start(bf16[4096,256]{1,0:T(8,128)(2,1)} %get-tuple-element.136.down_l.up_l.out_l), channel_id=1, source_target_pairs={{0,1},{1,0},{2,3},{3,2},{4,5},{5,4},{6,7},{7,6},{8,9},{9,8},{10,11... | collective-permute-start | bytes 6291464 | tf_op jit(solution)/shard_map/ppermute | solution.py:353
  163.3 5.9 %all-to-all-start.3 = ((bf16[8,256,128]{2,1,0:T(8,128)(2,1)}), bf16[8,256,128]{2,1,0:T(8,128)(2,1)}, u32[]{:S(2)}, u32[]{:S(2)}) async-start(bf16[8,256,128]{2,1,0:T(8,128)(2,1)} %get-tuple-element.133), calls=%async_computation.3 | async-start | bytes 1048576 | tf_op jit(solution)/shard_map/all_to_all | solution.py:357
  170.8 10.0 %weight_grads.1 = (bf16[8,768,128]{2,1,0:T(8,128)(2,1)}, bf16[8,768,128]{2,1,0:T(8,128)(2,1)}, bf16[2,4,512,128]{3,2,1,0:T(8,128)(2,1)}, bf16[2,4,512,128]{3,2,1,0:T(8,128)(2,1)}) custom-call(s32[3]{0:T(128)} %pad_add_fusion.1.place_ref, bf16[4096,256]{1,0:T(8,128)(2,1)} %get-tuple-element.136.down_l.up_l.out_l, ...), custom_call_target="tpu_custom_call" | custom-call | flops 8999999488 | bytes 27000000 | tf_op jit(solution)/shard_map/weight_grads/pallas_call | solution.py:861
  181.6 28.5 %attend_back.1.g_ref = bf16[2048,384]{1,0:T(8,128)(2,1)} custom-call(bf16[2048,128]{1,0:T(8,128)(2,1)} %copy-done.9, bf16[2048,128]{1,0:T(8,128)(2,1)} %copy-done.5, bf16[2048,128]{1,0:T(8,128)(2,1)} %bitcast.25.grad_ref, f32[2048,128]{1,0:T(8,128)} %copy-done.22, f32[8,2048]{1,0:T(8,128)} %copy-done.23, f32[2048,128]{1,0:T(8,128)} %copy-done.3, ...), custom_call_target="tpu_custom_call" | custom-call | flops 27000000512 | bytes 81000000 | tf_op jit(solution)/shard_map/attend_back/pallas_call | solution.py:579
  210.2 6.1 %all-to-all-start.4 = ((bf16[8,256,384]{2,1,0:T(8,128)(2,1)}), bf16[8,256,384]{2,1,0:T(8,128)(2,1)}, u32[]{:S(2)}, u32[]{:S(2)}) async-start(bf16[8,256,384]{2,1,0:T(8,128)(2,1)} %bitcast.110), calls=%async_computation.4 | async-start | bytes 3145728 | tf_op jit(solution)/shard_map/all_to_all | solution.py:357
  223.2 4.6 %convolution_convert_fusion = bf16[1024,384]{1,0:T(8,128)(2,1)S(1)} fusion(bf16[2048,1024]{1,0:T(8,128)(2,1)} %copy-done.7, bf16[2048,384]{1,0:T(8,128)(2,1)S(1)} %copy-done.26), kind=kOutput, calls=%fused_computation.6 | convolution fusion | flops 1611005952 | bytes 6553600 | tf_op jit(solution)/shard_map/dot_general | solution.py:29
  227.7 5.8 %collective-permute-done.18 = bf16[4,512,128]{2,1,0:T(8,128)(2,1)S(1)} collective-permute-done((bf16[4,512,128]{2,1,0:T(8,128)(2,1)S(1)}, bf16[4,512,128]{2,1,0:T(8,128)(2,1)S(1)}, u32[]{:S(2)}, u32[]{:S(2)}) %collective-permute-start.18) | collective-permute-done | bytes 524320 | tf_op jit(solution)/shard_map/ppermute | solution.py:353
  239.6 11.0 %clip_grads.1 = f32[16,2048]{1,0:T(8,128)} custom-call(s32[2]{0:T(128)} %copy-done.19, bf16[2048,1024]{1,0:T(8,128)(2,1)} %copy-done.6, s32[1,2048]{1,0:T(1,128)} %and_select_fusion.clip_ref, bf16[2048,384]{1,0:T(8,128)(2,1)} %attend_back.1.g_ref, bf16[4,256,384]{2,1,0:T(8,128)(2,1)} %copy-done.4), custom_call_target="tpu_custom_call" | custom-call | flops 8999999488 | bytes 27000000 | tf_op jit(solution)/shard_map/clip_grads/pallas_call | solution.py:892
  255.4 8.0 %all-to-all-start.5 = ((f32[8,16,768]{2,1,0:T(8,128)}), f32[8,16,768]{2,1,0:T(8,128)S(1)}, u32[]{:S(2)}, u32[]{:S(2)}) async-start(f32[8,16,768]{2,1,0:T(8,128)} %bitcast.111), calls=%async_computation.5 | async-start | bytes 786432 | tf_op jit(solution)/shard_map/all_to_all | solution.py:357
  274.7 7.4 %all_gather.15 = f32[64,768]{1,0:T(8,128)S(1)} all-gather(f32[16,768]{1,0:T(8,128)} %reduce_sum.39), channel_id=1, replica_groups=mesh['seq'=8,'batch'=4] {'batch'}, dimensions={0}, use_global_device_ids=true | all-gather | bytes 245760 | tf_op jit(solution)/shard_map/all_gather | solution.py:1107
  287.4 5.5 %last.1 = bf16[256,1024]{1,0:T(8,128)(2,1)} custom-call(s32[3]{0:T(128)S(1)} %copy-done.20, bf16[8,256,384]{2,1,0:T(8,128)(2,1)} %all-to-all-done.4.own_ref, bf16[256,1024]{1,0:T(8,128)(2,1)S(1)} %bitcast.109, f32[256,1024]{1,0:T(8,128)S(1)} %copy-done.21, bf16[256,128]{1,0:T(8,128)(2,1)S(1)} %copy-done.18, bf16[128,6144]{1,0:T(8,128)(2,1)S(1)} %copy-done.1, ...), custom_call_target="tpu_custom_call" | custom-call | flops 4000000000 | bytes 12000000 | tf_op jit(solution)/shard_map/last/pallas_call | solution.py:941
  (241 shorter events, 77.7 us)
Async XLA Ops:
  7.2 23.3 %collective-permute-start = (bf16[256,1024]{1,0:T(8,128)(2,1)}, bf16[256,1024]{1,0:T(8,128)(2,1)S(1)}, u32[]{:S(2)}, u32[]{:S(2)}) collective-permute-start(bf16[256,1024]{1,0:T(8,128)(2,1)} %bitcast.104), channel_id=1, source_target_pairs={{0,8},{4,12},{8,0},{12,4},{16,24},{20,28},{24,16},{28,20},{1,9},{5... | collective-permute-start | bytes 1572872 | tf_op jit(solution)/shard_map/ppermute | solution.py:353
  7.4 25.1 %collective-permute-start.1 = (bf16[256,1024]{1,0:T(8,128)(2,1)}, bf16[256,1024]{1,0:T(8,128)(2,1)S(1)}, u32[]{:S(2)}, u32[]{:S(2)}) collective-permute-start(bf16[256,1024]{1,0:T(8,128)(2,1)} %bitcast.105), channel_id=1, source_target_pairs={{0,16},{4,20},{8,24},{12,28},{16,0},{20,4},{24,8},{28,12},{1,17},{... | collective-permute-start | bytes 1572872 | tf_op jit(solution)/shard_map/ppermute | solution.py:353
  9.8 22.8 %collective-permute-start.2 = (bf16[256,1024]{1,0:T(8,128)(2,1)}, bf16[256,1024]{1,0:T(8,128)(2,1)S(1)}, u32[]{:S(2)}, u32[]{:S(2)}) collective-permute-start(bf16[256,1024]{1,0:T(8,128)(2,1)} %bitcast.106), channel_id=1, source_target_pairs={{0,4},{4,0},{8,12},{12,8},{16,20},{20,16},{24,28},{28,24},{1,5},{5... | collective-permute-start | bytes 1572872 | tf_op jit(solution)/shard_map/ppermute | solution.py:353
  25.2 113.9 %all-gather.4.cloned.1.call-start = ((), (), s32[]{:S(2)}) async-start(), calls=%async_computation.6 | async-start | bytes 10813440 | tf_op jit(solution)/shard_map/all_gather | solution.py:1007
  33.5 35.8 %all-to-all-start.1 = ((f32[8,24,768]{2,1,0:T(8,128)}), f32[8,24,768]{2,1,0:T(8,128)}, u32[]{:S(2)}, u32[]{:S(2)}) async-start(f32[8,24,768]{2,1,0:T(8,128)} %broadcast_in_dim.16), calls=%async_computation.1 | async-start | bytes 1179648 | tf_op jit(solution)/shard_map/all_to_all | solution.py:357
  37.9 25.8 %collective-permute-start.4 = (bf16[256,1024]{1,0:T(8,128)(2,1)S(1)}, bf16[256,1024]{1,0:T(8,128)(2,1)}, u32[]{:S(2)}, u32[]{:S(2)}) collective-permute-start(bf16[256,1024]{1,0:T(8,128)(2,1)S(1)} %collective-permute-done.1.c_ref), channel_id=1, source_target_pairs={{0,8},{4,12},{8,0},{12,4},{16,24},{20,28},{24,16},{28,20},{1,9},{5... | collective-permute-start | bytes 1572872 | tf_op jit(solution)/shard_map/ppermute | solution.py:353
  40.0 36.1 %collective-permute-start.7 = (bf16[256,1024]{1,0:T(8,128)(2,1)S(1)}, bf16[256,1024]{1,0:T(8,128)(2,1)S(1)}, u32[]{:S(2)}, u32[]{:S(2)}) collective-permute-start(bf16[256,1024]{1,0:T(8,128)(2,1)S(1)} %collective-permute-done.1.c_ref), channel_id=1, source_target_pairs={{0,4},{4,0},{8,12},{12,8},{16,20},{20,16},{24,28},{28,24},{1,5},{5... | collective-permute-start | bytes 1572872 | tf_op jit(solution)/shard_map/ppermute | solution.py:353
  40.2 35.9 %collective-permute-start.6 = (bf16[256,1024]{1,0:T(8,128)(2,1)S(1)}, bf16[256,1024]{1,0:T(8,128)(2,1)S(1)}, u32[]{:S(2)}, u32[]{:S(2)}) collective-permute-start(bf16[256,1024]{1,0:T(8,128)(2,1)S(1)} %collective-permute-done.b_ref), channel_id=1, source_target_pairs={{0,4},{4,0},{8,12},{12,8},{16,20},{20,16},{24,28},{28,24},{1,5},{5... | collective-permute-start | bytes 1572872 | tf_op jit(solution)/shard_map/ppermute | solution.py:353
  63.7 22.4 %collective-permute-start.8 = (bf16[256,1024]{1,0:T(8,128)(2,1)}, bf16[256,1024]{1,0:T(8,128)(2,1)}, u32[]{:S(2)}, u32[]{:S(2)}) collective-permute-start(bf16[256,1024]{1,0:T(8,128)(2,1)} %collective-permute-done.4.d_ref), channel_id=1, source_target_pairs={{0,4},{4,0},{8,12},{12,8},{16,20},{20,16},{24,28},{28,24},{1,5},{5... | collective-permute-start | bytes 1572872 | tf_op jit(solution)/shard_map/ppermute | solution.py:353
  64.1 21.0 %collective-permute-start.9 = (bf16[768,128]{1,0:T(8,128)(2,1)}, bf16[768,128]{1,0:T(8,128)(2,1)}, u32[]{:S(2)}, u32[]{:S(2)}) collective-permute-start(bf16[768,128]{1,0:T(8,128)(2,1)} %pad_maximum_fusion.7), channel_id=1, source_target_pairs={{0,8},{4,12},{8,0},{12,4},{16,24},{20,28},{24,16},{28,20},{1,9},{5... | collective-permute-start | bytes 589832 | tf_op jit(solution)/shard_map/ppermute | solution.py:353
  86.1 25.4 %collective-permute-start.11 = (bf16[768,128]{1,0:T(8,128)(2,1)}, bf16[768,128]{1,0:T(8,128)(2,1)S(1)}, u32[]{:S(2)}, u32[]{:S(2)}) collective-permute-start(bf16[768,128]{1,0:T(8,128)(2,1)} %collective-permute-done.10), channel_id=1, source_target_pairs={{0,8},{4,12},{8,0},{12,4},{16,24},{20,28},{24,16},{28,20},{1,9},{5... | collective-permute-start | bytes 589832 | tf_op jit(solution)/shard_map/ppermute | solution.py:353
  112.2 25.8 %all-to-all-start.2 = ((bf16[8,256,128]{2,1,0:T(8,128)(2,1)}), bf16[8,256,128]{2,1,0:T(8,128)(2,1)S(1)}, u32[]{:S(2)}, u32[]{:S(2)}) async-start(bf16[8,256,128]{2,1,0:T(8,128)(2,1)} %bitcast.15), calls=%async_computation.2 | async-start | bytes 1048576 | tf_op jit(solution)/shard_map/all_to_all | solution.py:357
  180.8 39.8 %collective-permute-start.16 = (bf16[8,768,128]{2,1,0:T(8,128)(2,1)}, bf16[8,768,128]{2,1,0:T(8,128)(2,1)}, u32[]{:S(2)}, u32[]{:S(2)}) collective-permute-start(bf16[8,768,128]{2,1,0:T(8,128)(2,1)} %get-tuple-element.142), channel_id=1, source_target_pairs={{0,2},{1,3},{2,0},{3,1},{4,6},{5,7},{6,4},{7,5},{8,10},{9,11},{10,... | collective-permute-start | bytes 4718600 | tf_op jit(solution)/shard_map/ppermute | solution.py:353
  181.4 34.9 %collective-permute-start.17 = (bf16[2,4,512,128]{3,2,1,0:T(8,128)(2,1)}, bf16[2,4,512,128]{3,2,1,0:T(8,128)(2,1)}, u32[]{:S(2)}, u32[]{:S(2)}) collective-permute-start(bf16[2,4,512,128]{3,2,1,0:T(8,128)(2,1)} %get-tuple-element.143), channel_id=1, source_target_pairs={{0,4},{4,0},{8,12},{12,8},{16,20},{20,16},{24,28},{28,24},{1,5},{5... | collective-permute-start | bytes 3145736 | tf_op jit(solution)/shard_map/ppermute | solution.py:353
  210.2 43.5 %all-to-all-start.4 = ((bf16[8,256,384]{2,1,0:T(8,128)(2,1)}), bf16[8,256,384]{2,1,0:T(8,128)(2,1)}, u32[]{:S(2)}, u32[]{:S(2)}) async-start(bf16[8,256,384]{2,1,0:T(8,128)(2,1)} %bitcast.110), calls=%async_computation.4 | async-start | bytes 3145728 | tf_op jit(solution)/shard_map/all_to_all | solution.py:357
  217.6 34.4 %collective-permute-start.20 = (bf16[12,768,128]{2,1,0:T(8,128)(2,1)S(1)}, bf16[12,768,128]{2,1,0:T(8,128)(2,1)}, u32[]{:S(2)}, u32[]{:S(2)}) collective-permute-start(bf16[12,768,128]{2,1,0:T(8,128)(2,1)S(1)} %pad_maximum_fusion.refs_0_), channel_id=1, source_target_pairs={{0,1},{1,0},{2,3},{3,2},{4,5},{5,4},{6,7},{7,6},{8,9},{9,8},{10,11... | collective-permute-start | bytes 7077896 | tf_op jit(solution)/shard_map/ppermute | solution.py:353
  222.9 27.9 %collective-permute-start.19 = (bf16[4,768,128]{2,1,0:T(8,128)(2,1)}, bf16[4,768,128]{2,1,0:T(8,128)(2,1)}, u32[]{:S(2)}, u32[]{:S(2)}) collective-permute-start(bf16[4,768,128]{2,1,0:T(8,128)(2,1)} %add_convert_fusion.1), channel_id=1, source_target_pairs={{0,4},{4,0},{8,12},{12,8},{16,20},{20,16},{24,28},{28,24},{1,5},{5... | collective-permute-start | bytes 2359304 | tf_op jit(solution)/shard_map/ppermute | solution.py:353
  234.8 32.9 %collective-permute-start.21 = (bf16[4,768,128]{2,1,0:T(8,128)(2,1)}, bf16[4,768,128]{2,1,0:T(8,128)(2,1)S(1)}, u32[]{:S(2)}, u32[]{:S(2)}) collective-permute-start(bf16[4,768,128]{2,1,0:T(8,128)(2,1)} %collective-permute-done.12), channel_id=1, source_target_pairs={{0,2},{1,3},{2,0},{3,1},{4,6},{5,7},{6,4},{7,5},{8,10},{9,11},{10,... | collective-permute-start | bytes 2359304 | tf_op jit(solution)/shard_map/ppermute | solution.py:353
  236.4 35.0 %collective-permute-start.23 = (bf16[512,128]{1,0:T(8,128)(2,1)}, bf16[512,128]{1,0:T(8,128)(2,1)}, u32[]{:S(2)}, u32[]{:S(2)}) collective-permute-start(bf16[512,128]{1,0:T(8,128)(2,1)} %get-tuple-element.184), channel_id=1, source_target_pairs={{0,8},{4,12},{8,0},{12,4},{16,24},{20,28},{24,16},{28,20},{1,9},{5... | collective-permute-start | bytes 393224 | tf_op jit(solution)/shard_map/ppermute | solution.py:353
  236.7 35.1 %collective-permute-start.24 = (bf16[512,128]{1,0:T(8,128)(2,1)}, bf16[512,128]{1,0:T(8,128)(2,1)}, u32[]{:S(2)}, u32[]{:S(2)}) collective-permute-start(bf16[512,128]{1,0:T(8,128)(2,1)} %get-tuple-element.183), channel_id=1, source_target_pairs={{0,16},{4,20},{8,24},{12,28},{16,0},{20,4},{24,8},{28,12},{1,17},{... | collective-permute-start | bytes 393224 | tf_op jit(solution)/shard_map/ppermute | solution.py:353
  250.7 23.0 %collective-permute-start.25 = (bf16[512,128]{1,0:T(8,128)(2,1)}, bf16[512,128]{1,0:T(8,128)(2,1)}, u32[]{:S(2)}, u32[]{:S(2)}) collective-permute-start(bf16[512,128]{1,0:T(8,128)(2,1)} %get-tuple-element.182), channel_id=1, source_target_pairs={{0,24},{4,28},{8,16},{12,20},{16,8},{20,12},{24,0},{28,4},{1,25},{... | collective-permute-start | bytes 393224 | tf_op jit(solution)/shard_map/ppermute | solution.py:353
  265.6 27.3 %collective-permute-start.27 = (bf16[256,384]{1,0:T(8,128)(2,1)}, bf16[256,384]{1,0:T(8,128)(2,1)}, u32[]{:S(2)}, u32[]{:S(2)}) collective-permute-start(bf16[256,384]{1,0:T(8,128)(2,1)} %dynamic-slice_bitcast_fusion.1), channel_id=1, source_target_pairs={{0,2},{1,3},{2,0},{3,1},{4,6},{5,7},{6,4},{7,5},{8,10},{9,11},{10,... | collective-permute-start | bytes 589832 | tf_op jit(solution)/shard_map/ppermute | solution.py:353
  271.4 21.5 %collective-permute-start.28 = (bf16[768,128]{1,0:T(8,128)(2,1)}, bf16[768,128]{1,0:T(8,128)(2,1)}, u32[]{:S(2)}, u32[]{:S(2)}) collective-permute-start(bf16[768,128]{1,0:T(8,128)(2,1)} %get-tuple-element.181), channel_id=1, source_target_pairs={{0,8},{4,12},{8,0},{12,4},{16,24},{20,28},{24,16},{28,20},{1,9},{5... | collective-permute-start | bytes 589832 | tf_op jit(solution)/shard_map/ppermute | solution.py:353
  271.8 21.1 %collective-permute-start.29 = (bf16[768,128]{1,0:T(8,128)(2,1)}, bf16[768,128]{1,0:T(8,128)(2,1)}, u32[]{:S(2)}, u32[]{:S(2)}) collective-permute-start(bf16[768,128]{1,0:T(8,128)(2,1)} %get-tuple-element.180), channel_id=1, source_target_pairs={{0,16},{4,20},{8,24},{12,28},{16,0},{20,4},{24,8},{28,12},{1,17},{... | collective-permute-start | bytes 589832 | tf_op jit(solution)/shard_map/ppermute | solution.py:353
  (60 other events, 636.7 us)
Sparse Core Ops, SparseCore 0:
  33.6 105.3 all-gather.3

commit v4 on v3

--- a/solution.py
+++ b/solution.py
@@ -1104,7 +1104,7 @@
     grad_tokens = last_part(place, own, x, grad_middle, own_member, emb,
         (h_first, h_yx, h_first_core, h_yx_core),
     )
-    grad_emb = lax.all_gather(grad_emb, "batch", axis=0, tiled=True)
+    grad_emb = lax.all_gather(after(grad_emb, grad_tokens), "batch", axis=0, tiled=True)
     final_a = jnp.dot(silu_part.astype(wide).T, grad_emb, precision=highest)
     grad_tokens, final_a, away_h, *from_z = together(grad_tokens, final_a, away_h, *from_z)
     final_heads = plus(lax.dynamic_index_in_dim(both_h, x_place, 0, False), away_h)

time: 307 us -> 306 us (level)
  no operation moved by 1% of the time
where the time goes in v4:
time: 306 us; the launch traced here: 303 us
  Pallas kernels  103 us (34%)
  starting transfers between devices  65.6 us (21%)
  waiting for transfers between devices  50.9 us (17%)
  other arithmetic  26.8 us (9%)
  local copies, waits for them, and re-layouts  19.7 us (6%)
  between operations  15.6 us (5%)
  blocking collectives  12.5 us (4%)
  matrix products  8.34 us (3%)
    ppermute x31, starting transfers between devices, swap(): return lax.ppermute(part, axis, [(i, i ^ distance) for i in range(size)])  32.3 us
    ppermute x31, waiting for transfers between devices, swap(): return lax.ppermute(part, axis, [(i, i ^ distance) for i in range(size)])  30 us
    all_to_all x5, starting transfers between devices, exchange(): return lax.all_to_all(blocks, 'seq', 0, 0, tiled=True)  28.9 us
    pallas_call x1, Pallas kernels, attend_back(): pl.pallas_call(attend_back_kernel, grid=(frames // ROWS,), in_specs=[rows...  28.5 us
    pallas_call x1, Pallas kernels, middle_part(): pl.pallas_call(middle_kernel, in_specs=[vmem] * 4 + [anywhere] * 3, out_s...  19.3 us
    all_to_all x5, waiting for transfers between devices, exchange(): return lax.all_to_all(blocks, 'seq', 0, 0, tiled=True)  18.4 us
    pallas_call x1, Pallas kernels, attend(): pl.pallas_call(attend_kernel, grid=(frames // BLOCK,), in_specs=[block_sp...  16.1 us
    pallas_call x2, Pallas kernels, project(): pl.pallas_call(project_kernel, grid_spec=pltpu.PrefetchScalarGridSpec(num...  12.7 us
  transfers between devices with their start and end apart: 38, of which 8 were waited for; matrix products, arithmetic and copies ran while one was open for 14% of the time, Pallas kernels for 34%

profile of v4, /device:TPU:13, one launch (start us, length us, event | category | flops | bytes accessed | tf_op | source)
XLA Modules:
  0.0 302.5 jit_solution(8401321310473924166)
XLA Ops:
  12.6 5.4 %all-reduce.1 = s32[64]{0:T(128)S(1)} all-reduce(s32[64]{0:T(128)S(1)} %bitcast_dynamic-update-slice_fusion), channel_id=2, replica_groups=mesh['seq'=8,'batch'=4] {'batch'}, use_global_device_ids=true, to_apply=%add.1 | all-reduce | flops 64 | bytes 512
  20.7 4.4 %all-to-all-start = ((f32[4,16,768]{2,1,0:T(8,128)}), f32[4,16,768]{2,1,0:T(8,128)S(1)}, u32[]{:S(2)}, u32[]{:S(2)}) async-start(f32[4,16,768]{2,1,0:T(8,128)} %bitcast.5), calls=%async_computation | async-start | bytes 393216 | tf_op jit(solution)/shard_map/all_to_all | solution.py:997
  33.5 4.2 %all-to-all-start.1 = ((f32[8,24,768]{2,1,0:T(8,128)}), f32[8,24,768]{2,1,0:T(8,128)}, u32[]{:S(2)}, u32[]{:S(2)}) async-start(f32[8,24,768]{2,1,0:T(8,128)} %broadcast_in_dim.16), calls=%async_computation.1 | async-start | bytes 1179648 | tf_op jit(solution)/shard_map/all_to_all | solution.py:357
  42.5 2.8 collective-permute-done.5
  45.3 18.1 %collective-permute-done.4.d_ref = bf16[256,1024]{1,0:T(8,128)(2,1)} collective-permute-done((bf16[256,1024]{1,0:T(8,128)(2,1)S(1)}, bf16[256,1024]{1,0:T(8,128)(2,1)}, u32[]{:S(2)}, u32[]{:S(2)}) %collective-permute-start.4) | collective-permute-done | bytes 524320 | tf_op jit(solution)/shard_map/ppermute | solution.py:353
  72.1 3.7 %multiply_sine_fusion = (f32[2048,128]{1,0:T(8,128)S(1)}, f32[2048,128]{1,0:T(8,128)S(1)}) fusion(f32[128]{0:T(128)S(1)} %mul.62, f32[2048]{0:T(1024)S(1)} %bitcast.120), kind=kLoop, calls=%fused_computation.4 | loop fusion | flops 262144 | bytes 2105856 | tf_op jit(solution)/shard_map/sin | solution.py:1032
  78.5 6.3 %project.2 = (bf16[2048,1024]{1,0:T(8,128)(2,1)S(1)}, bf16[2048,1024]{1,0:T(8,128)(2,1)S(1)}, bf16[2048,128]{1,0:T(8,128)(2,1)S(1)}, bf16[2048,256]{1,0:T(8,128)...) custom-call(s32[2]{0:T(128)S(1)} %pad_add_fusion.place_ref, ...), custom_call_target="tpu_custom_call" | custom-call | flops 2000000000 | bytes 6000000 | tf_op jit(solution)/shard_map/project/pallas_call | solution.py:449
  87.3 6.4 %project.3 = (bf16[2048,1024]{1,0:T(8,128)(2,1)S(1)}, bf16[2048,1024]{1,0:T(8,128)(2,1)S(1)}, bf16[2048,128]{1,0:T(8,128)(2,1)S(1)}, bf16[2048,256]{1,0:T(8,128)...) custom-call(s32[2]{0:T(128)S(1)} %pad_add_fusion.place_ref, ...), custom_call_target="tpu_custom_call", output_to_operand_aliasing={{0}: (11, {}), {1}: (12, {}), {2}: (13, {}), {3}: (14, {}),... | custom-call | flops 2000000000 | bytes 6000000 | tf_op jit(solution)/shard_map/project/pallas_call | solution.py:449
  93.7 16.1 %attend.1 = (f32[2048,128]{1,0:T(8,128)S(1)}, bf16[2048,128]{1,0:T(8,128)(2,1)}, f32[8,2048]{1,0:T(8,128)S(1)}) custom-call(bf16[2048,128]{1,0:T(8,128)(2,1)S(1)} %get-tuple-element.122.q_ref, bf16[2048,128]{1,0:T(8,128)(2,1)S(1)} %and_convert_fusion.member_ref, bf16[2048,256]{1,0:T(8,128)(2,1)S(1)} %get-tuple-element.123.k_ref, ...), custom_call_target="tpu_custom_call" | custom-call | flops 17999998976 | bytes 54000000 | tf_op jit(solution)/shard_map/attend/pallas_call | solution.py:512
  112.2 5.0 %all-to-all-start.2 = ((bf16[8,256,128]{2,1,0:T(8,128)(2,1)}), bf16[8,256,128]{2,1,0:T(8,128)(2,1)S(1)}, u32[]{:S(2)}, u32[]{:S(2)}) async-start(bf16[8,256,128]{2,1,0:T(8,128)(2,1)} %bitcast.15), calls=%async_computation.2 | async-start | bytes 1048576 | tf_op jit(solution)/shard_map/all_to_all | solution.py:357
  119.2 18.4 %all-to-all-done.2.mine_ref = bf16[8,256,128]{2,1,0:T(8,128)(2,1)S(1)} async-done(((bf16[8,256,128]{2,1,0:T(8,128)(2,1)}), bf16[8,256,128]{2,1,0:T(8,128)(2,1)S(1)}, u32[]{:S(2)}, u32[]{:S(2)}) %all-to-all-start.2) | async-done | bytes 524320 | tf_op jit(solution)/shard_map/all_to_all | solution.py:357
  138.9 19.3 %middle.1 = (bf16[256,1024]{1,0:T(8,128)(2,1)}, f32[256,1024]{1,0:T(8,128)}, bf16[8,256,128]{2,1,0:T(8,128)(2,1)}, f32[16,4096]{1,0:T(8,128)}, bf16[4096,256]{1,0:T(8,128)(2,1)}, /*index=5*/bf16[256,4096]{1,0:T(8,128)(2,1)}) custom-call(bf16[8,256,128]{2,1,0:T(8,128)(2,1)} %copy-done.39, bf16[256,1024]{1,0:T(8,128)(2,1)} %bitcast.107, ...), custom_call_target="tpu_custom_call" | custom-call | flops 20000000000 | bytes 60000000 | tf_op jit(solution)/shard_map/middle/pallas_call | solution.py:786
  158.3 4.0 %collective-permute-start.14 = (bf16[4096,256]{1,0:T(8,128)(2,1)}, bf16[4096,256]{1,0:T(8,128)(2,1)}, u32[]{:S(2)}, u32[]{:S(2)}) collective-permute-start(bf16[4096,256]{1,0:T(8,128)(2,1)} %get-tuple-element.137.down_l.up_l.out_l), channel_id=1, source_target_pairs={{0,1},{1,0},{2,3},{3,2},{4,5},{5,4},{6,7},{7,6},{8,9},{9,8},{10,11... | collective-permute-start | bytes 6291464 | tf_op jit(solution)/shard_map/ppermute | solution.py:353
  163.1 5.8 %all-to-all-start.3 = ((bf16[8,256,128]{2,1,0:T(8,128)(2,1)}), bf16[8,256,128]{2,1,0:T(8,128)(2,1)}, u32[]{:S(2)}, u32[]{:S(2)}) async-start(bf16[8,256,128]{2,1,0:T(8,128)(2,1)} %get-tuple-element.134), calls=%async_computation.3 | async-start | bytes 1048576 | tf_op jit(solution)/shard_map/all_to_all | solution.py:357
  170.6 10.1 %weight_grads.1 = (bf16[8,768,128]{2,1,0:T(8,128)(2,1)}, bf16[8,768,128]{2,1,0:T(8,128)(2,1)}, bf16[2,4,512,128]{3,2,1,0:T(8,128)(2,1)}, bf16[2,4,512,128]{3,2,1,0:T(8,128)(2,1)}) custom-call(s32[3]{0:T(128)} %pad_add_fusion.1.place_ref, bf16[4096,256]{1,0:T(8,128)(2,1)} %get-tuple-element.137.down_l.up_l.out_l, ...), custom_call_target="tpu_custom_call" | custom-call | flops 8999999488 | bytes 27000000 | tf_op jit(solution)/shard_map/weight_grads/pallas_call | solution.py:861
  181.6 28.5 %attend_back.1.g_ref = bf16[2048,384]{1,0:T(8,128)(2,1)} custom-call(bf16[2048,128]{1,0:T(8,128)(2,1)} %copy-done.11, bf16[2048,128]{1,0:T(8,128)(2,1)} %copy-done.5, bf16[2048,128]{1,0:T(8,128)(2,1)} %bitcast.25.grad_ref, f32[2048,128]{1,0:T(8,128)} %copy-done.24, f32[8,2048]{1,0:T(8,128)} %copy-done.25, f32[2048,128]{1,0:T(8,128)} %copy-done.3, ...), custom_call_target="tpu_custom_call" | custom-call | flops 27000000512 | bytes 81000000 | tf_op jit(solution)/shard_map/attend_back/pallas_call | solution.py:579
  210.1 5.7 %all-to-all-start.4 = ((bf16[8,256,384]{2,1,0:T(8,128)(2,1)}), bf16[8,256,384]{2,1,0:T(8,128)(2,1)}, u32[]{:S(2)}, u32[]{:S(2)}) async-start(bf16[8,256,384]{2,1,0:T(8,128)(2,1)} %bitcast.110), calls=%async_computation.4 | async-start | bytes 3145728 | tf_op jit(solution)/shard_map/all_to_all | solution.py:357
  223.0 4.7 %convolution_convert_fusion = bf16[1024,384]{1,0:T(8,128)(2,1)S(1)} fusion(bf16[2048,1024]{1,0:T(8,128)(2,1)} %copy-done.7, bf16[2048,384]{1,0:T(8,128)(2,1)S(1)} %copy-done.28), kind=kOutput, calls=%fused_computation.6 | convolution fusion | flops 1611005952 | bytes 6553600 | tf_op jit(solution)/shard_map/dot_general | solution.py:29
  227.7 5.6 %collective-permute-done.18 = bf16[4,512,128]{2,1,0:T(8,128)(2,1)S(1)} collective-permute-done((bf16[4,512,128]{2,1,0:T(8,128)(2,1)S(1)}, bf16[4,512,128]{2,1,0:T(8,128)(2,1)S(1)}, u32[]{:S(2)}, u32[]{:S(2)}) %collective-permute-start.18) | collective-permute-done | bytes 524320 | tf_op jit(solution)/shard_map/ppermute | solution.py:353
  239.4 11.0 %clip_grads.1 = f32[16,2048]{1,0:T(8,128)} custom-call(s32[2]{0:T(128)} %copy-done.21, bf16[2048,1024]{1,0:T(8,128)(2,1)} %copy-done.6, s32[1,2048]{1,0:T(1,128)} %and_select_fusion.clip_ref, bf16[2048,384]{1,0:T(8,128)(2,1)} %attend_back.1.g_ref, bf16[4,256,384]{2,1,0:T(8,128)(2,1)} %copy-done.4), custom_call_target="tpu_custom_call" | custom-call | flops 8999999488 | bytes 27000000 | tf_op jit(solution)/shard_map/clip_grads/pallas_call | solution.py:892
  254.9 8.2 %all-to-all-start.5 = ((f32[8,16,768]{2,1,0:T(8,128)}), f32[8,16,768]{2,1,0:T(8,128)S(1)}, u32[]{:S(2)}, u32[]{:S(2)}) async-start(f32[8,16,768]{2,1,0:T(8,128)} %bitcast.103), calls=%async_computation.5 | async-start | bytes 786432 | tf_op jit(solution)/shard_map/all_to_all | solution.py:357
  267.2 2.7 collective-permute-start.22
  277.2 5.5 %last.1 = bf16[256,1024]{1,0:T(8,128)(2,1)} custom-call(s32[3]{0:T(128)S(1)} %copy-done.22, bf16[8,256,384]{2,1,0:T(8,128)(2,1)} %all-to-all-done.4.own_ref, bf16[256,1024]{1,0:T(8,128)(2,1)S(1)} %bitcast.109, f32[256,1024]{1,0:T(8,128)S(1)} %copy-done.23, bf16[256,128]{1,0:T(8,128)(2,1)S(1)} %copy-done.20, bf16[128,6144]{1,0:T(8,128)(2,1)S(1)} %copy-done.1, ...), custom_call_target="tpu_custom_call" | custom-call | flops 4000000000 | bytes 12000000 | tf_op jit(solution)/shard_map/last/pallas_call | solution.py:941
  282.7 7.1 %all_gather.15 = f32[64,768]{1,0:T(8,128)S(1)} all-gather(f32[16,768]{1,0:T(8,128)S(1)} %reduce_sum.39), channel_id=1, replica_groups=mesh['seq'=8,'batch'=4] {'batch'}, dimensions={0}, use_global_device_ids=true | all-gather | bytes 245760 | tf_op jit(solution)/shard_map/all_gather | solution.py:1107
  (241 shorter events, 78.1 us)
Async XLA Ops:
  7.2 23.2 %collective-permute-start = (bf16[256,1024]{1,0:T(8,128)(2,1)}, bf16[256,1024]{1,0:T(8,128)(2,1)S(1)}, u32[]{:S(2)}, u32[]{:S(2)}) collective-permute-start(bf16[256,1024]{1,0:T(8,128)(2,1)} %bitcast.104), channel_id=1, source_target_pairs={{0,8},{4,12},{8,0},{12,4},{16,24},{20,28},{24,16},{28,20},{1,9},{5... | collective-permute-start | bytes 1572872 | tf_op jit(solution)/shard_map/ppermute | solution.py:353
  7.4 25.1 %collective-permute-start.1 = (bf16[256,1024]{1,0:T(8,128)(2,1)}, bf16[256,1024]{1,0:T(8,128)(2,1)S(1)}, u32[]{:S(2)}, u32[]{:S(2)}) collective-permute-start(bf16[256,1024]{1,0:T(8,128)(2,1)} %bitcast.105), channel_id=1, source_target_pairs={{0,16},{4,20},{8,24},{12,28},{16,0},{20,4},{24,8},{28,12},{1,17},{... | collective-permute-start | bytes 1572872 | tf_op jit(solution)/shard_map/ppermute | solution.py:353
  9.8 22.8 %collective-permute-start.2 = (bf16[256,1024]{1,0:T(8,128)(2,1)}, bf16[256,1024]{1,0:T(8,128)(2,1)S(1)}, u32[]{:S(2)}, u32[]{:S(2)}) collective-permute-start(bf16[256,1024]{1,0:T(8,128)(2,1)} %bitcast.106), channel_id=1, source_target_pairs={{0,4},{4,0},{8,12},{12,8},{16,20},{20,16},{24,28},{28,24},{1,5},{5... | collective-permute-start | bytes 1572872 | tf_op jit(solution)/shard_map/ppermute | solution.py:353
  25.1 113.9 %all-gather.4.cloned.1.call-start = ((), (), s32[]{:S(2)}) async-start(), calls=%async_computation.6 | async-start | bytes 10813440 | tf_op jit(solution)/shard_map/all_gather | solution.py:1007
  33.5 35.5 %all-to-all-start.1 = ((f32[8,24,768]{2,1,0:T(8,128)}), f32[8,24,768]{2,1,0:T(8,128)}, u32[]{:S(2)}, u32[]{:S(2)}) async-start(f32[8,24,768]{2,1,0:T(8,128)} %broadcast_in_dim.16), calls=%async_computation.1 | async-start | bytes 1179648 | tf_op jit(solution)/shard_map/all_to_all | solution.py:357
  37.8 25.7 %collective-permute-start.4 = (bf16[256,1024]{1,0:T(8,128)(2,1)S(1)}, bf16[256,1024]{1,0:T(8,128)(2,1)}, u32[]{:S(2)}, u32[]{:S(2)}) collective-permute-start(bf16[256,1024]{1,0:T(8,128)(2,1)S(1)} %collective-permute-done.1.c_ref), channel_id=1, source_target_pairs={{0,8},{4,12},{8,0},{12,4},{16,24},{20,28},{24,16},{28,20},{1,9},{5... | collective-permute-start | bytes 1572872 | tf_op jit(solution)/shard_map/ppermute | solution.py:353
  40.0 35.8 %collective-permute-start.7 = (bf16[256,1024]{1,0:T(8,128)(2,1)S(1)}, bf16[256,1024]{1,0:T(8,128)(2,1)S(1)}, u32[]{:S(2)}, u32[]{:S(2)}) collective-permute-start(bf16[256,1024]{1,0:T(8,128)(2,1)S(1)} %collective-permute-done.1.c_ref), channel_id=1, source_target_pairs={{0,4},{4,0},{8,12},{12,8},{16,20},{20,16},{24,28},{28,24},{1,5},{5... | collective-permute-start | bytes 1572872 | tf_op jit(solution)/shard_map/ppermute | solution.py:353
  40.2 35.6 %collective-permute-start.6 = (bf16[256,1024]{1,0:T(8,128)(2,1)S(1)}, bf16[256,1024]{1,0:T(8,128)(2,1)S(1)}, u32[]{:S(2)}, u32[]{:S(2)}) collective-permute-start(bf16[256,1024]{1,0:T(8,128)(2,1)S(1)} %collective-permute-done.b_ref), channel_id=1, source_target_pairs={{0,4},{4,0},{8,12},{12,8},{16,20},{20,16},{24,28},{28,24},{1,5},{5... | collective-permute-start | bytes 1572872 | tf_op jit(solution)/shard_map/ppermute | solution.py:353
  63.5 22.7 %collective-permute-start.8 = (bf16[256,1024]{1,0:T(8,128)(2,1)}, bf16[256,1024]{1,0:T(8,128)(2,1)}, u32[]{:S(2)}, u32[]{:S(2)}) collective-permute-start(bf16[256,1024]{1,0:T(8,128)(2,1)} %collective-permute-done.4.d_ref), channel_id=1, source_target_pairs={{0,4},{4,0},{8,12},{12,8},{16,20},{20,16},{24,28},{28,24},{1,5},{5... | collective-permute-start | bytes 1572872 | tf_op jit(solution)/shard_map/ppermute | solution.py:353
  63.8 21.0 %collective-permute-start.9 = (bf16[768,128]{1,0:T(8,128)(2,1)}, bf16[768,128]{1,0:T(8,128)(2,1)}, u32[]{:S(2)}, u32[]{:S(2)}) collective-permute-start(bf16[768,128]{1,0:T(8,128)(2,1)} %pad_maximum_fusion.7), channel_id=1, source_target_pairs={{0,8},{4,12},{8,0},{12,4},{16,24},{20,28},{24,16},{28,20},{1,9},{5... | collective-permute-start | bytes 589832 | tf_op jit(solution)/shard_map/ppermute | solution.py:353
  86.2 25.4 %collective-permute-start.11 = (bf16[768,128]{1,0:T(8,128)(2,1)}, bf16[768,128]{1,0:T(8,128)(2,1)S(1)}, u32[]{:S(2)}, u32[]{:S(2)}) collective-permute-start(bf16[768,128]{1,0:T(8,128)(2,1)} %collective-permute-done.10), channel_id=1, source_target_pairs={{0,8},{4,12},{8,0},{12,4},{16,24},{20,28},{24,16},{28,20},{1,9},{5... | collective-permute-start | bytes 589832 | tf_op jit(solution)/shard_map/ppermute | solution.py:353
  112.2 25.4 %all-to-all-start.2 = ((bf16[8,256,128]{2,1,0:T(8,128)(2,1)}), bf16[8,256,128]{2,1,0:T(8,128)(2,1)S(1)}, u32[]{:S(2)}, u32[]{:S(2)}) async-start(bf16[8,256,128]{2,1,0:T(8,128)(2,1)} %bitcast.15), calls=%async_computation.2 | async-start | bytes 1048576 | tf_op jit(solution)/shard_map/all_to_all | solution.py:357
  137.6 20.6 %collective-permute-start.12 = (bf16[4,768,128]{2,1,0:T(8,128)(2,1)S(1)}, bf16[4,768,128]{2,1,0:T(8,128)(2,1)}, u32[]{:S(2)}, u32[]{:S(2)}) collective-permute-start(bf16[4,768,128]{2,1,0:T(8,128)(2,1)S(1)} %pad_maximum_fusion.1), channel_id=1, source_target_pairs={{0,4},{4,0},{8,12},{12,8},{16,20},{20,16},{24,28},{28,24},{1,5},{5... | collective-permute-start | bytes 2359304 | tf_op jit(solution)/shard_map/ppermute | solution.py:353
  137.6 20.6 %collective-permute-start.13 = (bf16[4,768,128]{2,1,0:T(8,128)(2,1)S(1)}, bf16[4,768,128]{2,1,0:T(8,128)(2,1)S(1)}, u32[]{:S(2)}, u32[]{:S(2)}) collective-permute-start(bf16[4,768,128]{2,1,0:T(8,128)(2,1)S(1)} %pad_maximum_fusion.1), channel_id=1, source_target_pairs={{0,2},{1,3},{2,0},{3,1},{4,6},{5,7},{6,4},{7,5},{8,10},{9,11},{10,... | collective-permute-start | bytes 2359304 | tf_op jit(solution)/shard_map/ppermute | solution.py:353
  180.6 39.8 %collective-permute-start.16 = (bf16[8,768,128]{2,1,0:T(8,128)(2,1)}, bf16[8,768,128]{2,1,0:T(8,128)(2,1)}, u32[]{:S(2)}, u32[]{:S(2)}) collective-permute-start(bf16[8,768,128]{2,1,0:T(8,128)(2,1)} %get-tuple-element.143), channel_id=1, source_target_pairs={{0,2},{1,3},{2,0},{3,1},{4,6},{5,7},{6,4},{7,5},{8,10},{9,11},{10,... | collective-permute-start | bytes 4718600 | tf_op jit(solution)/shard_map/ppermute | solution.py:353
  181.3 34.5 %collective-permute-start.17 = (bf16[2,4,512,128]{3,2,1,0:T(8,128)(2,1)}, bf16[2,4,512,128]{3,2,1,0:T(8,128)(2,1)}, u32[]{:S(2)}, u32[]{:S(2)}) collective-permute-start(bf16[2,4,512,128]{3,2,1,0:T(8,128)(2,1)} %get-tuple-element.144), channel_id=1, source_target_pairs={{0,4},{4,0},{8,12},{12,8},{16,20},{20,16},{24,28},{28,24},{1,5},{5... | collective-permute-start | bytes 3145736 | tf_op jit(solution)/shard_map/ppermute | solution.py:353
  210.1 43.1 %all-to-all-start.4 = ((bf16[8,256,384]{2,1,0:T(8,128)(2,1)}), bf16[8,256,384]{2,1,0:T(8,128)(2,1)}, u32[]{:S(2)}, u32[]{:S(2)}) async-start(bf16[8,256,384]{2,1,0:T(8,128)(2,1)} %bitcast.110), calls=%async_computation.4 | async-start | bytes 3145728 | tf_op jit(solution)/shard_map/all_to_all | solution.py:357
  217.3 34.3 %collective-permute-start.20 = (bf16[12,768,128]{2,1,0:T(8,128)(2,1)S(1)}, bf16[12,768,128]{2,1,0:T(8,128)(2,1)}, u32[]{:S(2)}, u32[]{:S(2)}) collective-permute-start(bf16[12,768,128]{2,1,0:T(8,128)(2,1)S(1)} %pad_maximum_fusion.refs_0_), channel_id=1, source_target_pairs={{0,1},{1,0},{2,3},{3,2},{4,5},{5,4},{6,7},{7,6},{8,9},{9,8},{10,11... | collective-permute-start | bytes 7077896 | tf_op jit(solution)/shard_map/ppermute | solution.py:353
  222.7 27.7 %collective-permute-start.19 = (bf16[4,768,128]{2,1,0:T(8,128)(2,1)}, bf16[4,768,128]{2,1,0:T(8,128)(2,1)}, u32[]{:S(2)}, u32[]{:S(2)}) collective-permute-start(bf16[4,768,128]{2,1,0:T(8,128)(2,1)} %add_convert_fusion.1), channel_id=1, source_target_pairs={{0,4},{4,0},{8,12},{12,8},{16,20},{20,16},{24,28},{28,24},{1,5},{5... | collective-permute-start | bytes 2359304 | tf_op jit(solution)/shard_map/ppermute | solution.py:353
  234.5 32.7 %collective-permute-start.21 = (bf16[4,768,128]{2,1,0:T(8,128)(2,1)}, bf16[4,768,128]{2,1,0:T(8,128)(2,1)S(1)}, u32[]{:S(2)}, u32[]{:S(2)}) collective-permute-start(bf16[4,768,128]{2,1,0:T(8,128)(2,1)} %collective-permute-done.12), channel_id=1, source_target_pairs={{0,2},{1,3},{2,0},{3,1},{4,6},{5,7},{6,4},{7,5},{8,10},{9,11},{10,... | collective-permute-start | bytes 2359304 | tf_op jit(solution)/shard_map/ppermute | solution.py:353
  236.2 34.7 %collective-permute-start.23 = (bf16[512,128]{1,0:T(8,128)(2,1)}, bf16[512,128]{1,0:T(8,128)(2,1)}, u32[]{:S(2)}, u32[]{:S(2)}) collective-permute-start(bf16[512,128]{1,0:T(8,128)(2,1)} %get-tuple-element.186), channel_id=1, source_target_pairs={{0,8},{4,12},{8,0},{12,4},{16,24},{20,28},{24,16},{28,20},{1,9},{5... | collective-permute-start | bytes 393224 | tf_op jit(solution)/shard_map/ppermute | solution.py:353
  236.5 34.8 %collective-permute-start.24 = (bf16[512,128]{1,0:T(8,128)(2,1)}, bf16[512,128]{1,0:T(8,128)(2,1)}, u32[]{:S(2)}, u32[]{:S(2)}) collective-permute-start(bf16[512,128]{1,0:T(8,128)(2,1)} %get-tuple-element.185), channel_id=1, source_target_pairs={{0,16},{4,20},{8,24},{12,28},{16,0},{20,4},{24,8},{28,12},{1,17},{... | collective-permute-start | bytes 393224 | tf_op jit(solution)/shard_map/ppermute | solution.py:353
  250.4 22.8 %collective-permute-start.25 = (bf16[512,128]{1,0:T(8,128)(2,1)}, bf16[512,128]{1,0:T(8,128)(2,1)}, u32[]{:S(2)}, u32[]{:S(2)}) collective-permute-start(bf16[512,128]{1,0:T(8,128)(2,1)} %get-tuple-element.184), channel_id=1, source_target_pairs={{0,24},{4,28},{8,16},{12,20},{16,8},{20,12},{24,0},{28,4},{1,25},{... | collective-permute-start | bytes 393224 | tf_op jit(solution)/shard_map/ppermute | solution.py:353
  265.1 26.2 %collective-permute-start.27 = (bf16[256,384]{1,0:T(8,128)(2,1)}, bf16[256,384]{1,0:T(8,128)(2,1)}, u32[]{:S(2)}, u32[]{:S(2)}) collective-permute-start(bf16[256,384]{1,0:T(8,128)(2,1)} %dynamic-slice_bitcast_fusion.1), channel_id=1, source_target_pairs={{0,2},{1,3},{2,0},{3,1},{4,6},{5,7},{6,4},{7,5},{8,10},{9,11},{10,... | collective-permute-start | bytes 589832 | tf_op jit(solution)/shard_map/ppermute | solution.py:353
  (60 other events, 674.8 us)
Sparse Core Ops, SparseCore 0:
  33.6 105.2 all-gather.3

commit v5 on v4

--- a/solution.py
+++ b/solution.py
@@ -825,7 +825,7 @@
         return matmul(left, right).astype(low)
 
     def fill(ref):
-        @pl.loop(0, 4)
+        @pl.loop(0, 4, unroll=2)
         def _(k):
             block = z ^ k
             for left, first, rows in ((lefts[0], 0, slice(0, 512)), (lefts[2], 3 * D, slice(512, 768))):

time: 306 us -> 305 us (level)
  no operation moved by 1% of the time
where the time goes in v5:
time: 305 us; the launch traced here: 302 us
  Pallas kernels  102 us (33%)
  starting transfers between devices  65.7 us (22%)
  waiting for transfers between devices  51.2 us (17%)
  other arithmetic  26.8 us (9%)
  local copies, waits for them, and re-layouts  19.8 us (6%)
  between operations  15.6 us (5%)
  blocking collectives  12.5 us (4%)
  matrix products  8.34 us (3%)
    ppermute x31, starting transfers between devices, swap(): return lax.ppermute(part, axis, [(i, i ^ distance) for i in range(size)])  31.9 us
    ppermute x31, waiting for transfers between devices, swap(): return lax.ppermute(part, axis, [(i, i ^ distance) for i in range(size)])  30.4 us
    all_to_all x5, starting transfers between devices, exchange(): return lax.all_to_all(blocks, 'seq', 0, 0, tiled=True)  29.4 us
    pallas_call x1, Pallas kernels, attend_back(): pl.pallas_call(attend_back_kernel, grid=(frames // ROWS,), in_specs=[rows...  28.5 us
    pallas_call x1, Pallas kernels, middle_part(): pl.pallas_call(middle_kernel, in_specs=[vmem] * 4 + [anywhere] * 3, out_s...  19.3 us
    all_to_all x5, waiting for transfers between devices, exchange(): return lax.all_to_all(blocks, 'seq', 0, 0, tiled=True)  18.4 us
    pallas_call x1, Pallas kernels, attend(): pl.pallas_call(attend_kernel, grid=(frames // BLOCK,), in_specs=[block_sp...  16.1 us
    pallas_call x2, Pallas kernels, project(): pl.pallas_call(project_kernel, grid_spec=pltpu.PrefetchScalarGridSpec(num...  12.7 us
  transfers between devices with their start and end apart: 38, of which 8 were waited for; matrix products, arithmetic and copies ran while one was open for 14% of the time, Pallas kernels for 34%

profile of v5, /device:TPU:13, one launch (start us, length us, event | category | flops | bytes accessed | tf_op | source)
XLA Modules:
  0.0 302.5 jit_solution(9432012742350400094)
XLA Ops:
  12.6 5.4 %all-reduce.1 = s32[64]{0:T(128)S(1)} all-reduce(s32[64]{0:T(128)S(1)} %bitcast_dynamic-update-slice_fusion), channel_id=2, replica_groups=mesh['seq'=8,'batch'=4] {'batch'}, use_global_device_ids=true, to_apply=%add.1 | all-reduce | flops 64 | bytes 512
  20.7 4.4 %all-to-all-start = ((f32[4,16,768]{2,1,0:T(8,128)}), f32[4,16,768]{2,1,0:T(8,128)S(1)}, u32[]{:S(2)}, u32[]{:S(2)}) async-start(f32[4,16,768]{2,1,0:T(8,128)} %bitcast.5), calls=%async_computation | async-start | bytes 393216 | tf_op jit(solution)/shard_map/all_to_all | solution.py:997
  33.5 4.2 %all-to-all-start.1 = ((f32[8,24,768]{2,1,0:T(8,128)}), f32[8,24,768]{2,1,0:T(8,128)}, u32[]{:S(2)}, u32[]{:S(2)}) async-start(f32[8,24,768]{2,1,0:T(8,128)} %broadcast_in_dim.16), calls=%async_computation.1 | async-start | bytes 1179648 | tf_op jit(solution)/shard_map/all_to_all | solution.py:357
  42.5 2.8 collective-permute-done.5
  45.3 18.1 %collective-permute-done.4.d_ref = bf16[256,1024]{1,0:T(8,128)(2,1)} collective-permute-done((bf16[256,1024]{1,0:T(8,128)(2,1)S(1)}, bf16[256,1024]{1,0:T(8,128)(2,1)}, u32[]{:S(2)}, u32[]{:S(2)}) %collective-permute-start.4) | collective-permute-done | bytes 524320 | tf_op jit(solution)/shard_map/ppermute | solution.py:353
  72.1 3.7 %multiply_sine_fusion = (f32[2048,128]{1,0:T(8,128)S(1)}, f32[2048,128]{1,0:T(8,128)S(1)}) fusion(f32[128]{0:T(128)S(1)} %mul.62, f32[2048]{0:T(1024)S(1)} %bitcast.120), kind=kLoop, calls=%fused_computation.4 | loop fusion | flops 262144 | bytes 2105856 | tf_op jit(solution)/shard_map/sin | solution.py:1032
  78.5 6.3 %project.2 = (bf16[2048,1024]{1,0:T(8,128)(2,1)S(1)}, bf16[2048,1024]{1,0:T(8,128)(2,1)S(1)}, bf16[2048,128]{1,0:T(8,128)(2,1)S(1)}, bf16[2048,256]{1,0:T(8,128)...) custom-call(s32[2]{0:T(128)S(1)} %pad_add_fusion.place_ref, ...), custom_call_target="tpu_custom_call" | custom-call | flops 2000000000 | bytes 6000000 | tf_op jit(solution)/shard_map/project/pallas_call | solution.py:449
  87.3 6.4 %project.3 = (bf16[2048,1024]{1,0:T(8,128)(2,1)S(1)}, bf16[2048,1024]{1,0:T(8,128)(2,1)S(1)}, bf16[2048,128]{1,0:T(8,128)(2,1)S(1)}, bf16[2048,256]{1,0:T(8,128)...) custom-call(s32[2]{0:T(128)S(1)} %pad_add_fusion.place_ref, ...), custom_call_target="tpu_custom_call", output_to_operand_aliasing={{0}: (11, {}), {1}: (12, {}), {2}: (13, {}), {3}: (14, {}),... | custom-call | flops 2000000000 | bytes 6000000 | tf_op jit(solution)/shard_map/project/pallas_call | solution.py:449
  93.7 16.1 %attend.1 = (f32[2048,128]{1,0:T(8,128)S(1)}, bf16[2048,128]{1,0:T(8,128)(2,1)}, f32[8,2048]{1,0:T(8,128)S(1)}) custom-call(bf16[2048,128]{1,0:T(8,128)(2,1)S(1)} %get-tuple-element.122.q_ref, bf16[2048,128]{1,0:T(8,128)(2,1)S(1)} %and_convert_fusion.member_ref, bf16[2048,256]{1,0:T(8,128)(2,1)S(1)} %get-tuple-element.123.k_ref, ...), custom_call_target="tpu_custom_call" | custom-call | flops 17999998976 | bytes 54000000 | tf_op jit(solution)/shard_map/attend/pallas_call | solution.py:512
  112.2 5.0 %all-to-all-start.2 = ((bf16[8,256,128]{2,1,0:T(8,128)(2,1)}), bf16[8,256,128]{2,1,0:T(8,128)(2,1)S(1)}, u32[]{:S(2)}, u32[]{:S(2)}) async-start(bf16[8,256,128]{2,1,0:T(8,128)(2,1)} %bitcast.15), calls=%async_computation.2 | async-start | bytes 1048576 | tf_op jit(solution)/shard_map/all_to_all | solution.py:357
  119.2 18.4 %all-to-all-done.2.mine_ref = bf16[8,256,128]{2,1,0:T(8,128)(2,1)S(1)} async-done(((bf16[8,256,128]{2,1,0:T(8,128)(2,1)}), bf16[8,256,128]{2,1,0:T(8,128)(2,1)S(1)}, u32[]{:S(2)}, u32[]{:S(2)}) %all-to-all-start.2) | async-done | bytes 524320 | tf_op jit(solution)/shard_map/all_to_all | solution.py:357
  138.9 19.3 %middle.1 = (bf16[256,1024]{1,0:T(8,128)(2,1)}, f32[256,1024]{1,0:T(8,128)}, bf16[8,256,128]{2,1,0:T(8,128)(2,1)}, f32[16,4096]{1,0:T(8,128)}, bf16[4096,256]{1,0:T(8,128)(2,1)}, /*index=5*/bf16[256,4096]{1,0:T(8,128)(2,1)}) custom-call(bf16[8,256,128]{2,1,0:T(8,128)(2,1)} %copy-done.39, bf16[256,1024]{1,0:T(8,128)(2,1)} %bitcast.107, ...), custom_call_target="tpu_custom_call" | custom-call | flops 20000000000 | bytes 60000000 | tf_op jit(solution)/shard_map/middle/pallas_call | solution.py:786
  158.3 4.0 %collective-permute-start.14 = (bf16[4096,256]{1,0:T(8,128)(2,1)}, bf16[4096,256]{1,0:T(8,128)(2,1)}, u32[]{:S(2)}, u32[]{:S(2)}) collective-permute-start(bf16[4096,256]{1,0:T(8,128)(2,1)} %get-tuple-element.137.down_l.up_l.out_l), channel_id=1, source_target_pairs={{0,1},{1,0},{2,3},{3,2},{4,5},{5,4},{6,7},{7,6},{8,9},{9,8},{10,11... | collective-permute-start | bytes 6291464 | tf_op jit(solution)/shard_map/ppermute | solution.py:353
  163.1 5.8 %all-to-all-start.3 = ((bf16[8,256,128]{2,1,0:T(8,128)(2,1)}), bf16[8,256,128]{2,1,0:T(8,128)(2,1)}, u32[]{:S(2)}, u32[]{:S(2)}) async-start(bf16[8,256,128]{2,1,0:T(8,128)(2,1)} %get-tuple-element.134), calls=%async_computation.3 | async-start | bytes 1048576 | tf_op jit(solution)/shard_map/all_to_all | solution.py:357
  170.6 9.4 %weight_grads.1 = (bf16[8,768,128]{2,1,0:T(8,128)(2,1)}, bf16[8,768,128]{2,1,0:T(8,128)(2,1)}, bf16[2,4,512,128]{3,2,1,0:T(8,128)(2,1)}, bf16[2,4,512,128]{3,2,1,0:T(8,128)(2,1)}) custom-call(s32[3]{0:T(128)} %pad_add_fusion.1.place_ref, bf16[4096,256]{1,0:T(8,128)(2,1)} %get-tuple-element.137.down_l.up_l.out_l, ...), custom_call_target="tpu_custom_call" | custom-call | flops 8999999488 | bytes 27000000 | tf_op jit(solution)/shard_map/weight_grads/pallas_call | solution.py:861
  180.9 28.5 %attend_back.1.g_ref = bf16[2048,384]{1,0:T(8,128)(2,1)} custom-call(bf16[2048,128]{1,0:T(8,128)(2,1)} %copy-done.11, bf16[2048,128]{1,0:T(8,128)(2,1)} %copy-done.5, bf16[2048,128]{1,0:T(8,128)(2,1)} %bitcast.25.grad_ref, f32[2048,128]{1,0:T(8,128)} %copy-done.24, f32[8,2048]{1,0:T(8,128)} %copy-done.25, f32[2048,128]{1,0:T(8,128)} %copy-done.3, ...), custom_call_target="tpu_custom_call" | custom-call | flops 27000000512 | bytes 81000000 | tf_op jit(solution)/shard_map/attend_back/pallas_call | solution.py:579
  209.4 6.4 %all-to-all-start.4 = ((bf16[8,256,384]{2,1,0:T(8,128)(2,1)}), bf16[8,256,384]{2,1,0:T(8,128)(2,1)}, u32[]{:S(2)}, u32[]{:S(2)}) async-start(bf16[8,256,384]{2,1,0:T(8,128)(2,1)} %bitcast.110), calls=%async_computation.4 | async-start | bytes 3145728 | tf_op jit(solution)/shard_map/all_to_all | solution.py:357
  222.7 4.7 %convolution_convert_fusion = bf16[1024,384]{1,0:T(8,128)(2,1)S(1)} fusion(bf16[2048,1024]{1,0:T(8,128)(2,1)} %copy-done.7, bf16[2048,384]{1,0:T(8,128)(2,1)S(1)} %copy-done.28), kind=kOutput, calls=%fused_computation.6 | convolution fusion | flops 1611005952 | bytes 6553600 | tf_op jit(solution)/shard_map/dot_general | solution.py:29
  227.4 5.9 %collective-permute-done.18 = bf16[4,512,128]{2,1,0:T(8,128)(2,1)S(1)} collective-permute-done((bf16[4,512,128]{2,1,0:T(8,128)(2,1)S(1)}, bf16[4,512,128]{2,1,0:T(8,128)(2,1)S(1)}, u32[]{:S(2)}, u32[]{:S(2)}) %collective-permute-start.18) | collective-permute-done | bytes 524320 | tf_op jit(solution)/shard_map/ppermute | solution.py:353
  239.2 11.0 %clip_grads.1 = f32[16,2048]{1,0:T(8,128)} custom-call(s32[2]{0:T(128)} %copy-done.21, bf16[2048,1024]{1,0:T(8,128)(2,1)} %copy-done.6, s32[1,2048]{1,0:T(1,128)} %and_select_fusion.clip_ref, bf16[2048,384]{1,0:T(8,128)(2,1)} %attend_back.1.g_ref, bf16[4,256,384]{2,1,0:T(8,128)(2,1)} %copy-done.4), custom_call_target="tpu_custom_call" | custom-call | flops 8999999488 | bytes 27000000 | tf_op jit(solution)/shard_map/clip_grads/pallas_call | solution.py:892
  254.9 8.0 %all-to-all-start.5 = ((f32[8,16,768]{2,1,0:T(8,128)}), f32[8,16,768]{2,1,0:T(8,128)S(1)}, u32[]{:S(2)}, u32[]{:S(2)}) async-start(f32[8,16,768]{2,1,0:T(8,128)} %bitcast.103), calls=%async_computation.5 | async-start | bytes 786432 | tf_op jit(solution)/shard_map/all_to_all | solution.py:357
  267.4 2.5 collective-permute-start.22
  277.2 5.5 %last.1 = bf16[256,1024]{1,0:T(8,128)(2,1)} custom-call(s32[3]{0:T(128)S(1)} %copy-done.22, bf16[8,256,384]{2,1,0:T(8,128)(2,1)} %all-to-all-done.4.own_ref, bf16[256,1024]{1,0:T(8,128)(2,1)S(1)} %bitcast.109, f32[256,1024]{1,0:T(8,128)S(1)} %copy-done.23, bf16[256,128]{1,0:T(8,128)(2,1)S(1)} %copy-done.20, bf16[128,6144]{1,0:T(8,128)(2,1)S(1)} %copy-done.1, ...), custom_call_target="tpu_custom_call" | custom-call | flops 4000000000 | bytes 12000000 | tf_op jit(solution)/shard_map/last/pallas_call | solution.py:941
  282.6 7.1 %all_gather.15 = f32[64,768]{1,0:T(8,128)S(1)} all-gather(f32[16,768]{1,0:T(8,128)S(1)} %reduce_sum.39), channel_id=1, replica_groups=mesh['seq'=8,'batch'=4] {'batch'}, dimensions={0}, use_global_device_ids=true | all-gather | bytes 245760 | tf_op jit(solution)/shard_map/all_gather | solution.py:1107
  (241 shorter events, 78.1 us)
Async XLA Ops:
  7.2 23.2 %collective-permute-start = (bf16[256,1024]{1,0:T(8,128)(2,1)}, bf16[256,1024]{1,0:T(8,128)(2,1)S(1)}, u32[]{:S(2)}, u32[]{:S(2)}) collective-permute-start(bf16[256,1024]{1,0:T(8,128)(2,1)} %bitcast.104), channel_id=1, source_target_pairs={{0,8},{4,12},{8,0},{12,4},{16,24},{20,28},{24,16},{28,20},{1,9},{5... | collective-permute-start | bytes 1572872 | tf_op jit(solution)/shard_map/ppermute | solution.py:353
  7.4 25.1 %collective-permute-start.1 = (bf16[256,1024]{1,0:T(8,128)(2,1)}, bf16[256,1024]{1,0:T(8,128)(2,1)S(1)}, u32[]{:S(2)}, u32[]{:S(2)}) collective-permute-start(bf16[256,1024]{1,0:T(8,128)(2,1)} %bitcast.105), channel_id=1, source_target_pairs={{0,16},{4,20},{8,24},{12,28},{16,0},{20,4},{24,8},{28,12},{1,17},{... | collective-permute-start | bytes 1572872 | tf_op jit(solution)/shard_map/ppermute | solution.py:353
  9.8 22.8 %collective-permute-start.2 = (bf16[256,1024]{1,0:T(8,128)(2,1)}, bf16[256,1024]{1,0:T(8,128)(2,1)S(1)}, u32[]{:S(2)}, u32[]{:S(2)}) collective-permute-start(bf16[256,1024]{1,0:T(8,128)(2,1)} %bitcast.106), channel_id=1, source_target_pairs={{0,4},{4,0},{8,12},{12,8},{16,20},{20,16},{24,28},{28,24},{1,5},{5... | collective-permute-start | bytes 1572872 | tf_op jit(solution)/shard_map/ppermute | solution.py:353
  25.1 113.9 %all-gather.4.cloned.1.call-start = ((), (), s32[]{:S(2)}) async-start(), calls=%async_computation.6 | async-start | bytes 10813440 | tf_op jit(solution)/shard_map/all_gather | solution.py:1007
  33.5 35.5 %all-to-all-start.1 = ((f32[8,24,768]{2,1,0:T(8,128)}), f32[8,24,768]{2,1,0:T(8,128)}, u32[]{:S(2)}, u32[]{:S(2)}) async-start(f32[8,24,768]{2,1,0:T(8,128)} %broadcast_in_dim.16), calls=%async_computation.1 | async-start | bytes 1179648 | tf_op jit(solution)/shard_map/all_to_all | solution.py:357
  37.8 25.7 %collective-permute-start.4 = (bf16[256,1024]{1,0:T(8,128)(2,1)S(1)}, bf16[256,1024]{1,0:T(8,128)(2,1)}, u32[]{:S(2)}, u32[]{:S(2)}) collective-permute-start(bf16[256,1024]{1,0:T(8,128)(2,1)S(1)} %collective-permute-done.1.c_ref), channel_id=1, source_target_pairs={{0,8},{4,12},{8,0},{12,4},{16,24},{20,28},{24,16},{28,20},{1,9},{5... | collective-permute-start | bytes 1572872 | tf_op jit(solution)/shard_map/ppermute | solution.py:353
  40.0 35.8 %collective-permute-start.7 = (bf16[256,1024]{1,0:T(8,128)(2,1)S(1)}, bf16[256,1024]{1,0:T(8,128)(2,1)S(1)}, u32[]{:S(2)}, u32[]{:S(2)}) collective-permute-start(bf16[256,1024]{1,0:T(8,128)(2,1)S(1)} %collective-permute-done.1.c_ref), channel_id=1, source_target_pairs={{0,4},{4,0},{8,12},{12,8},{16,20},{20,16},{24,28},{28,24},{1,5},{5... | collective-permute-start | bytes 1572872 | tf_op jit(solution)/shard_map/ppermute | solution.py:353
  40.2 35.6 %collective-permute-start.6 = (bf16[256,1024]{1,0:T(8,128)(2,1)S(1)}, bf16[256,1024]{1,0:T(8,128)(2,1)S(1)}, u32[]{:S(2)}, u32[]{:S(2)}) collective-permute-start(bf16[256,1024]{1,0:T(8,128)(2,1)S(1)} %collective-permute-done.b_ref), channel_id=1, source_target_pairs={{0,4},{4,0},{8,12},{12,8},{16,20},{20,16},{24,28},{28,24},{1,5},{5... | collective-permute-start | bytes 1572872 | tf_op jit(solution)/shard_map/ppermute | solution.py:353
  63.5 22.7 %collective-permute-start.8 = (bf16[256,1024]{1,0:T(8,128)(2,1)}, bf16[256,1024]{1,0:T(8,128)(2,1)}, u32[]{:S(2)}, u32[]{:S(2)}) collective-permute-start(bf16[256,1024]{1,0:T(8,128)(2,1)} %collective-permute-done.4.d_ref), channel_id=1, source_target_pairs={{0,4},{4,0},{8,12},{12,8},{16,20},{20,16},{24,28},{28,24},{1,5},{5... | collective-permute-start | bytes 1572872 | tf_op jit(solution)/shard_map/ppermute | solution.py:353
  63.8 21.0 %collective-permute-start.9 = (bf16[768,128]{1,0:T(8,128)(2,1)}, bf16[768,128]{1,0:T(8,128)(2,1)}, u32[]{:S(2)}, u32[]{:S(2)}) collective-permute-start(bf16[768,128]{1,0:T(8,128)(2,1)} %pad_maximum_fusion.7), channel_id=1, source_target_pairs={{0,8},{4,12},{8,0},{12,4},{16,24},{20,28},{24,16},{28,20},{1,9},{5... | collective-permute-start | bytes 589832 | tf_op jit(solution)/shard_map/ppermute | solution.py:353
  86.2 25.4 %collective-permute-start.11 = (bf16[768,128]{1,0:T(8,128)(2,1)}, bf16[768,128]{1,0:T(8,128)(2,1)S(1)}, u32[]{:S(2)}, u32[]{:S(2)}) collective-permute-start(bf16[768,128]{1,0:T(8,128)(2,1)} %collective-permute-done.10), channel_id=1, source_target_pairs={{0,8},{4,12},{8,0},{12,4},{16,24},{20,28},{24,16},{28,20},{1,9},{5... | collective-permute-start | bytes 589832 | tf_op jit(solution)/shard_map/ppermute | solution.py:353
  112.2 25.4 %all-to-all-start.2 = ((bf16[8,256,128]{2,1,0:T(8,128)(2,1)}), bf16[8,256,128]{2,1,0:T(8,128)(2,1)S(1)}, u32[]{:S(2)}, u32[]{:S(2)}) async-start(bf16[8,256,128]{2,1,0:T(8,128)(2,1)} %bitcast.15), calls=%async_computation.2 | async-start | bytes 1048576 | tf_op jit(solution)/shard_map/all_to_all | solution.py:357
  137.6 20.6 %collective-permute-start.12 = (bf16[4,768,128]{2,1,0:T(8,128)(2,1)S(1)}, bf16[4,768,128]{2,1,0:T(8,128)(2,1)}, u32[]{:S(2)}, u32[]{:S(2)}) collective-permute-start(bf16[4,768,128]{2,1,0:T(8,128)(2,1)S(1)} %pad_maximum_fusion.1), channel_id=1, source_target_pairs={{0,4},{4,0},{8,12},{12,8},{16,20},{20,16},{24,28},{28,24},{1,5},{5... | collective-permute-start | bytes 2359304 | tf_op jit(solution)/shard_map/ppermute | solution.py:353
  137.6 20.6 %collective-permute-start.13 = (bf16[4,768,128]{2,1,0:T(8,128)(2,1)S(1)}, bf16[4,768,128]{2,1,0:T(8,128)(2,1)S(1)}, u32[]{:S(2)}, u32[]{:S(2)}) collective-permute-start(bf16[4,768,128]{2,1,0:T(8,128)(2,1)S(1)} %pad_maximum_fusion.1), channel_id=1, source_target_pairs={{0,2},{1,3},{2,0},{3,1},{4,6},{5,7},{6,4},{7,5},{8,10},{9,11},{10,... | collective-permute-start | bytes 2359304 | tf_op jit(solution)/shard_map/ppermute | solution.py:353
  180.0 40.2 %collective-permute-start.16 = (bf16[8,768,128]{2,1,0:T(8,128)(2,1)}, bf16[8,768,128]{2,1,0:T(8,128)(2,1)}, u32[]{:S(2)}, u32[]{:S(2)}) collective-permute-start(bf16[8,768,128]{2,1,0:T(8,128)(2,1)} %get-tuple-element.143), channel_id=1, source_target_pairs={{0,2},{1,3},{2,0},{3,1},{4,6},{5,7},{6,4},{7,5},{8,10},{9,11},{10,... | collective-permute-start | bytes 4718600 | tf_op jit(solution)/shard_map/ppermute | solution.py:353
  180.6 35.1 %collective-permute-start.17 = (bf16[2,4,512,128]{3,2,1,0:T(8,128)(2,1)}, bf16[2,4,512,128]{3,2,1,0:T(8,128)(2,1)}, u32[]{:S(2)}, u32[]{:S(2)}) collective-permute-start(bf16[2,4,512,128]{3,2,1,0:T(8,128)(2,1)} %get-tuple-element.144), channel_id=1, source_target_pairs={{0,4},{4,0},{8,12},{12,8},{16,20},{20,16},{24,28},{28,24},{1,5},{5... | collective-permute-start | bytes 3145736 | tf_op jit(solution)/shard_map/ppermute | solution.py:353
  209.4 43.8 %all-to-all-start.4 = ((bf16[8,256,384]{2,1,0:T(8,128)(2,1)}), bf16[8,256,384]{2,1,0:T(8,128)(2,1)}, u32[]{:S(2)}, u32[]{:S(2)}) async-start(bf16[8,256,384]{2,1,0:T(8,128)(2,1)} %bitcast.110), calls=%async_computation.4 | async-start | bytes 3145728 | tf_op jit(solution)/shard_map/all_to_all | solution.py:357
  217.3 34.3 %collective-permute-start.20 = (bf16[12,768,128]{2,1,0:T(8,128)(2,1)S(1)}, bf16[12,768,128]{2,1,0:T(8,128)(2,1)}, u32[]{:S(2)}, u32[]{:S(2)}) collective-permute-start(bf16[12,768,128]{2,1,0:T(8,128)(2,1)S(1)} %pad_maximum_fusion.refs_0_), channel_id=1, source_target_pairs={{0,1},{1,0},{2,3},{3,2},{4,5},{5,4},{6,7},{7,6},{8,9},{9,8},{10,11... | collective-permute-start | bytes 7077896 | tf_op jit(solution)/shard_map/ppermute | solution.py:353
  222.4 27.9 %collective-permute-start.19 = (bf16[4,768,128]{2,1,0:T(8,128)(2,1)}, bf16[4,768,128]{2,1,0:T(8,128)(2,1)}, u32[]{:S(2)}, u32[]{:S(2)}) collective-permute-start(bf16[4,768,128]{2,1,0:T(8,128)(2,1)} %add_convert_fusion.1), channel_id=1, source_target_pairs={{0,4},{4,0},{8,12},{12,8},{16,20},{20,16},{24,28},{28,24},{1,5},{5... | collective-permute-start | bytes 2359304 | tf_op jit(solution)/shard_map/ppermute | solution.py:353
  234.5 32.9 %collective-permute-start.21 = (bf16[4,768,128]{2,1,0:T(8,128)(2,1)}, bf16[4,768,128]{2,1,0:T(8,128)(2,1)S(1)}, u32[]{:S(2)}, u32[]{:S(2)}) collective-permute-start(bf16[4,768,128]{2,1,0:T(8,128)(2,1)} %collective-permute-done.12), channel_id=1, source_target_pairs={{0,2},{1,3},{2,0},{3,1},{4,6},{5,7},{6,4},{7,5},{8,10},{9,11},{10,... | collective-permute-start | bytes 2359304 | tf_op jit(solution)/shard_map/ppermute | solution.py:353
  236.0 34.7 %collective-permute-start.23 = (bf16[512,128]{1,0:T(8,128)(2,1)}, bf16[512,128]{1,0:T(8,128)(2,1)}, u32[]{:S(2)}, u32[]{:S(2)}) collective-permute-start(bf16[512,128]{1,0:T(8,128)(2,1)} %get-tuple-element.186), channel_id=1, source_target_pairs={{0,8},{4,12},{8,0},{12,4},{16,24},{20,28},{24,16},{28,20},{1,9},{5... | collective-permute-start | bytes 393224 | tf_op jit(solution)/shard_map/ppermute | solution.py:353
  236.3 34.9 %collective-permute-start.24 = (bf16[512,128]{1,0:T(8,128)(2,1)}, bf16[512,128]{1,0:T(8,128)(2,1)}, u32[]{:S(2)}, u32[]{:S(2)}) collective-permute-start(bf16[512,128]{1,0:T(8,128)(2,1)} %get-tuple-element.185), channel_id=1, source_target_pairs={{0,16},{4,20},{8,24},{12,28},{16,0},{20,4},{24,8},{28,12},{1,17},{... | collective-permute-start | bytes 393224 | tf_op jit(solution)/shard_map/ppermute | solution.py:353
  250.3 22.9 %collective-permute-start.25 = (bf16[512,128]{1,0:T(8,128)(2,1)}, bf16[512,128]{1,0:T(8,128)(2,1)}, u32[]{:S(2)}, u32[]{:S(2)}) collective-permute-start(bf16[512,128]{1,0:T(8,128)(2,1)} %get-tuple-element.184), channel_id=1, source_target_pairs={{0,24},{4,28},{8,16},{12,20},{16,8},{20,12},{24,0},{28,4},{1,25},{... | collective-permute-start | bytes 393224 | tf_op jit(solution)/shard_map/ppermute | solution.py:353
  264.9 26.3 %collective-permute-start.27 = (bf16[256,384]{1,0:T(8,128)(2,1)}, bf16[256,384]{1,0:T(8,128)(2,1)}, u32[]{:S(2)}, u32[]{:S(2)}) collective-permute-start(bf16[256,384]{1,0:T(8,128)(2,1)} %dynamic-slice_bitcast_fusion.1), channel_id=1, source_target_pairs={{0,2},{1,3},{2,0},{3,1},{4,6},{5,7},{6,4},{7,5},{8,10},{9,11},{10,... | collective-permute-start | bytes 589832 | tf_op jit(solution)/shard_map/ppermute | solution.py:353
  (60 other events, 672.7 us)
Sparse Core Ops, SparseCore 0:
  33.6 105.2 all-gather.3
